TPU v7x, 32 devices: a whole 2x2x4 slice. The times are simulated.
32 devices in a mesh: wide: 8 (over y, x, core), narrow: 4 (over z).
Axes of the slice: x: 2, y: 2, z: 4, core: 2. Of those that a mesh axis runs over, the one named last changes fastest.
Arguments:
- hidden_in: bfloat16 [8192, 2048], P(('wide', 'narrow')), may hold values from -6 to 6
- attn_gain: float32 [2048], replicated, may hold values from 0.5 to 1.5
- mlp_gain: float32 [2048], replicated, may hold values from 0.5 to 1.5
- w_query: bfloat16 [2048, 2048], P(None, 'narrow'), may hold values from -0.125 to 0.125
- w_key: bfloat16 [2048, 512], P(None, 'narrow'), may hold values from -0.125 to 0.125
- w_value: bfloat16 [2048, 512], P(None, 'narrow'), may hold values from -0.125 to 0.125
- w_out: bfloat16 [2048, 2048], P('narrow'), may hold values from -0.5 to 0.5
- w_gate: bfloat16 [2048, 8192], P(None, 'narrow'), may hold values from -0.125 to 0.125
- w_up: bfloat16 [2048, 8192], P(None, 'narrow'), may hold values from -0.125 to 0.125
- w_down: bfloat16 [8192, 2048], P('narrow'), may hold values from -0.0625 to 0.0625
- upstream: bfloat16 [8192, 2048], P(('wide', 'narrow')), may hold values from -6 to 6
- doc_lengths: int32 [8, 4], P('wide'), may hold values from 1 to 896, as said below
Outputs:
- layer_out: bfloat16 [8192, 2048], P(('wide', 'narrow'))
- input_grad: float32 [8192, 2048], P(('wide', 'narrow'))
- attn_gain_grad: float32 [2048], replicated
- mlp_gain_grad: float32 [2048], replicated
- query_grad: float32 [2048, 2048], P('wide', 'narrow')
- key_grad: float32 [2048, 512], P('wide', 'narrow')
- value_grad: float32 [2048, 512], P('wide', 'narrow')
- out_proj_grad: float32 [2048, 2048], P('narrow', 'wide')
- gate_grad: float32 [2048, 8192], P('wide', 'narrow')
- up_grad: float32 [2048, 8192], P('wide', 'narrow')
- down_grad: float32 [8192, 2048], P('narrow', 'wide')
Inputs may be any that keep to these rules, and one draw needn't show every extreme that they name: `doc_lengths`: in every group one document has 896 tokens and the other 3 have 256 // 2 tokens together; the lengths of a group sum to 1024.
All inputs are finite; a program needn't handle non-finite values.
Results may differ from a plain program's by a relative error of at most 0.018.
Values may be sent and summed in bfloat16 or wider, within the bound.
No kernel may reach another device: no remote copies, remote signals or barrier semaphores. Data moves between devices by JAX's collectives and lax.ppermute only.
A program may use at most 256 MiB of HBM per device.

v0:
```python
import math

import jax
import jax.numpy as jnp
from jax import lax
from jax.sharding import PartitionSpec as P

HD = 64


EPSILON = 1e-05
THETA_BASE = 500000.0


def doc_layout(lengths, total_rows):
    ends = jnp.cumsum(lengths)
    starts = ends - lengths
    places = jnp.arange(total_rows, dtype=jnp.int32)
    owner = jnp.sum((places[:, None] >= ends[None, :]).astype(jnp.int32), axis=1)
    picked = owner[:, None] == jnp.arange(lengths.shape[0], dtype=jnp.int32)[None, :]
    first = jnp.sum(jnp.where(picked, starts[None, :], 0), axis=1)
    return (owner, (places - first).astype(jnp.float32))


def angle_tables(positions, head_size):
    indices = jnp.arange(head_size // 2, dtype=jnp.float32)
    inverse = jnp.exp(indices * (-2.0 * math.log(THETA_BASE) / head_size))
    turned = positions[:, None] * inverse[None, :]
    return (jnp.cos(turned), jnp.sin(turned))


def rotate(values, cosine, sine):
    half = values.shape[-1] // 2
    first, second = (values[..., :half], values[..., half:])
    cosine = cosine[:, None, :]
    sine = sine[:, None, :]
    return jnp.concatenate(
        [first * cosine - second * sine, second * cosine + first * sine], axis=-1
    )


def rotate_back(values, cosine, sine):
    half = values.shape[-1] // 2
    first, second = (values[..., :half], values[..., half:])
    cosine = cosine[:, None, :]
    sine = sine[:, None, :]
    return jnp.concatenate(
        [first * cosine + second * sine, second * cosine - first * sine], axis=-1
    )


def contract_rows(left, right):
    return lax.dot_general(
        left, right, (((0,), (0,)), ((), ())), preferred_element_type=jnp.float32
    )


def contract_cols(left, right):
    return lax.dot_general(
        left, right, (((1,), (1,)), ((), ())), preferred_element_type=jnp.float32
    )


def on_device(
    hidden_in,
    attn_gain,
    mlp_gain,
    w_query,
    w_key,
    w_value,
    w_out,
    w_gate,
    w_up,
    w_down,
    upstream,
    doc_lengths,
):
    local_rows = hidden_in.shape[0]
    total_rows = local_rows * lax.axis_size("narrow")
    owner, positions = doc_layout(doc_lengths[0], total_rows)
    cosine, sine = angle_tables(positions, HD)
    query_width = w_query.shape[1]
    key_width = w_key.shape[1]
    kv_heads = key_width // HD
    group = query_width // key_width
    scale = HD ** (-0.5)
    block = min(512, total_rows)
    count = total_rows // block
    columns = jnp.arange(total_rows, dtype=jnp.int32)
    firsts = jnp.arange(count, dtype=jnp.int32) * block

    def allowed_at(first_row):
        row_ids = first_row + jnp.arange(block, dtype=jnp.int32)
        row_owner = lax.dynamic_slice_in_dim(owner, first_row, block)
        return (row_owner[:, None] == owner[None, :]) & (columns[None, :] <= row_ids[:, None])

    source = hidden_in.astype(jnp.float32)
    inverse_one = lax.rsqrt(jnp.mean(source * source, axis=-1, keepdims=True) + EPSILON)
    unit_one = source * inverse_one
    normed_one = (unit_one * attn_gain).astype(jnp.bfloat16)
    gathered_one = lax.all_gather(normed_one, "narrow", axis=0, tiled=True)
    w_joined = jnp.concatenate([w_query, w_key, w_value], axis=1)
    projected = jnp.dot(gathered_one, w_joined, preferred_element_type=jnp.float32)
    queries = rotate(
        projected[:, :query_width].reshape(total_rows, kv_heads * group, HD), cosine, sine
    )
    queries = queries.astype(jnp.bfloat16).reshape(total_rows, kv_heads, group, HD)
    keys = rotate(
        projected[:, query_width : query_width + key_width].reshape(total_rows, kv_heads, HD),
        cosine,
        sine,
    ).astype(jnp.bfloat16)
    values = (
        projected[:, query_width + key_width :]
        .astype(jnp.bfloat16)
        .reshape(total_rows, kv_heads, HD)
    )

    def attend_block(first_row):
        query_block = lax.dynamic_slice_in_dim(queries, first_row, block, 0)
        scores = (
            jnp.einsum("qcgd,kcd->cgqk", query_block, keys, preferred_element_type=jnp.float32)
            * scale
        )
        scores = jnp.where(allowed_at(first_row), scores, -1e30)
        largest = jnp.max(scores, axis=-1, keepdims=True)
        raised = jnp.exp(scores - largest)
        summed = jnp.sum(raised, axis=-1, keepdims=True)
        weights_soft = (raised / summed).astype(jnp.bfloat16)
        mixed = jnp.einsum(
            "cgqk,kcd->qcgd", weights_soft, values, preferred_element_type=jnp.float32
        )
        return (mixed, largest + jnp.log(summed))

    attended, log_totals = lax.map(attend_block, firsts)
    heads_out = attended.reshape(total_rows, query_width).astype(jnp.bfloat16)
    resid = source + lax.psum_scatter(
        jnp.dot(heads_out, w_out, preferred_element_type=jnp.float32),
        "narrow",
        scatter_dimension=0,
        tiled=True,
    )
    inverse_two = lax.rsqrt(jnp.mean(resid * resid, axis=-1, keepdims=True) + EPSILON)
    unit_two = resid * inverse_two
    normed_two = (unit_two * mlp_gain).astype(jnp.bfloat16)
    gathered_two = lax.all_gather(normed_two, "narrow", axis=0, tiled=True)
    gate = jnp.dot(gathered_two, w_gate, preferred_element_type=jnp.float32)
    up_value = jnp.dot(gathered_two, w_up, preferred_element_type=jnp.float32)
    sigma = jax.nn.sigmoid(gate)
    activated = gate * sigma
    product = (activated * up_value).astype(jnp.bfloat16)
    layer_out = (
        resid
        + lax.psum_scatter(
            jnp.dot(product, w_down, preferred_element_type=jnp.float32).astype(jnp.bfloat16),
            "narrow",
            scatter_dimension=0,
            tiled=True,
        ).astype(jnp.float32)
    ).astype(jnp.bfloat16)
    upstream_full = lax.all_gather(upstream, "narrow", axis=0, tiled=True)
    down_grad = contract_rows(product, upstream_full)
    product_grad = contract_cols(upstream_full, w_down)
    up_grad_low = (product_grad * activated).astype(jnp.bfloat16)
    gate_grad_low = (product_grad * up_value * (sigma * (1.0 + gate * (1.0 - sigma)))).astype(
        jnp.bfloat16
    )
    gate_grad = contract_rows(gathered_two, gate_grad_low)
    up_grad = contract_rows(gathered_two, up_grad_low)
    normed_two_grad = lax.psum_scatter(
        contract_cols(gate_grad_low, w_gate) + contract_cols(up_grad_low, w_up),
        "narrow",
        scatter_dimension=0,
        tiled=True,
    )
    scaled_two = normed_two_grad * mlp_gain
    mlp_gain_part = jnp.sum(normed_two_grad * unit_two, axis=0)
    resid_grad = upstream.astype(jnp.float32) + inverse_two * (
        scaled_two - unit_two * jnp.mean(scaled_two * unit_two, axis=-1, keepdims=True)
    )
    resid_full = lax.all_gather(resid_grad.astype(jnp.bfloat16), "narrow", axis=0, tiled=True)
    out_proj_grad = contract_rows(heads_out, resid_full)
    heads_grad = (
        contract_cols(resid_full, w_out)
        .astype(jnp.bfloat16)
        .reshape(total_rows, kv_heads, group, HD)
    )

    def back_block(carry, element):
        key_total, value_total = carry
        first_row, log_total = element
        query_block = lax.dynamic_slice_in_dim(queries, first_row, block, 0)
        grad_block = lax.dynamic_slice_in_dim(heads_grad, first_row, block, 0)
        scores = (
            jnp.einsum("qcgd,kcd->cgqk", query_block, keys, preferred_element_type=jnp.float32)
            * scale
        )
        weights_soft = jnp.where(allowed_at(first_row), jnp.exp(scores - log_total), 0.0)
        soft_grad = jnp.einsum(
            "qcgd,kcd->cgqk", grad_block, values, preferred_element_type=jnp.float32
        )
        score_grad = (
            weights_soft * (soft_grad - jnp.sum(soft_grad * weights_soft, axis=-1, keepdims=True))
        ).astype(jnp.bfloat16)
        query_part = (
            jnp.einsum("cgqk,kcd->qcgd", score_grad, keys, preferred_element_type=jnp.float32)
            * scale
        )
        key_total = (
            key_total
            + jnp.einsum(
                "cgqk,qcgd->kcd", score_grad, query_block, preferred_element_type=jnp.float32
            )
            * scale
        )
        value_total = value_total + jnp.einsum(
            "cgqk,qcgd->kcd",
            weights_soft.astype(jnp.bfloat16),
            grad_block,
            preferred_element_type=jnp.float32,
        )
        return ((key_total, value_total), query_part)

    empty = jnp.zeros((total_rows, kv_heads, HD), jnp.float32)
    (key_total, value_total), query_parts = lax.scan(
        back_block, (empty, empty), (firsts, log_totals)
    )
    query_grad_low = (
        rotate_back(query_parts.reshape(total_rows, kv_heads * group, HD), cosine, sine)
        .astype(jnp.bfloat16)
        .reshape(total_rows, query_width)
    )
    key_grad_low = (
        rotate_back(key_total, cosine, sine).astype(jnp.bfloat16).reshape(total_rows, key_width)
    )
    value_grad_low = value_total.astype(jnp.bfloat16).reshape(total_rows, key_width)
    joined_grad = jnp.concatenate([query_grad_low, key_grad_low, value_grad_low], axis=1)
    joined_weight_grad = contract_rows(gathered_one, joined_grad)
    query_grad = joined_weight_grad[:, :query_width]
    key_grad = joined_weight_grad[:, query_width : query_width + key_width]
    value_grad = joined_weight_grad[:, query_width + key_width :]
    normed_one_grad = lax.psum_scatter(
        contract_cols(joined_grad, w_joined).astype(jnp.bfloat16),
        "narrow",
        scatter_dimension=0,
        tiled=True,
    ).astype(jnp.float32)
    scaled_one = normed_one_grad * attn_gain
    attn_gain_part = jnp.sum(normed_one_grad * unit_one, axis=0)
    input_grad = resid_grad + inverse_one * (
        scaled_one - unit_one * jnp.mean(scaled_one * unit_one, axis=-1, keepdims=True)
    )
    attn_gain_grad, mlp_gain_grad = lax.psum((attn_gain_part, mlp_gain_part), ("wide", "narrow"))
    query_sum, key_sum, value_sum, out_sum, gate_sum, up_sum, down_sum = (
        lax.psum_scatter(
            query_grad.astype(jnp.bfloat16), "wide", scatter_dimension=0, tiled=True
        ).astype(jnp.float32),
        lax.psum_scatter(
            key_grad.astype(jnp.bfloat16), "wide", scatter_dimension=0, tiled=True
        ).astype(jnp.float32),
        lax.psum_scatter(
            value_grad.astype(jnp.bfloat16), "wide", scatter_dimension=0, tiled=True
        ).astype(jnp.float32),
        lax.psum_scatter(
            out_proj_grad.astype(jnp.bfloat16), "wide", scatter_dimension=1, tiled=True
        ).astype(jnp.float32),
        lax.psum_scatter(
            gate_grad.astype(jnp.bfloat16), "wide", scatter_dimension=0, tiled=True
        ).astype(jnp.float32),
        lax.psum_scatter(
            up_grad.astype(jnp.bfloat16), "wide", scatter_dimension=0, tiled=True
        ).astype(jnp.float32),
        lax.psum_scatter(
            down_grad.astype(jnp.bfloat16), "wide", scatter_dimension=1, tiled=True
        ).astype(jnp.float32),
    )
    return (
        layer_out,
        input_grad,
        attn_gain_grad,
        mlp_gain_grad,
        query_sum,
        key_sum,
        value_sum,
        out_sum,
        gate_sum,
        up_sum,
        down_sum,
    )


def solution(mesh):
    in_specs = (
        P(("wide", "narrow"), None),
        P(),
        P(),
        P(None, "narrow"),
        P(None, "narrow"),
        P(None, "narrow"),
        P("narrow", None),
        P(None, "narrow"),
        P(None, "narrow"),
        P("narrow", None),
        P(("wide", "narrow"), None),
        P("wide", None),
    )
    out_specs = (
        P(("wide", "narrow"), None),
        P(("wide", "narrow"), None),
        P(),
        P(),
        P("wide", "narrow"),
        P("wide", "narrow"),
        P("wide", "narrow"),
        P("narrow", "wide"),
        P("wide", "narrow"),
        P("wide", "narrow"),
        P("narrow", "wide"),
    )
    return jax.shard_map(
        on_device, mesh=mesh, in_specs=in_specs, out_specs=out_specs, check_vma=False
    )
```

profile of v0, /device:TPU:0, one launch (start us, length us, event | category | flops | bytes accessed | tf_op | source)
XLA Modules:
  0.0 1301.4 jit_solution(4283034291725066131)
XLA Ops:
  17.6 77.6 %all-gather.5.cloned.1.call-done = bf16[1024,2048]{1,0:T(8,128)(2,1)} async-done(((bf16[256,2048]{1,0:T(8,128)(2,1)}), bf16[1024,2048]{1,0:T(8,128)(2,1)}) %all-gather.5.cloned.1.call-update) | async-done | bytes 4194320 | tf_op jit(solution)/shard_map/all_gather | solution.py:101
  95.2 6.2 fusion.69
  102.8 35.8 %while.28 = (s32[]{:T(128)}, bf16[2,512,2,4,64]{1,4,3,2,0:T(8,128)(2,1)}, f32[2,2,4,512,1]{3,2,1,4,0:T(4,128)S(1)}, s32[2]{0:T(128)S(1)}, s32[1024]{0:T(1024)S(1...) while((s32[]{:T(128)}, ...), condition=%wide.region_7.8_spmd.clone, body=%wide.region_4.7_spmd.clone.sunk | while | flops 1125642752 | bytes 64108808 | solution.py:135
  110.2 4.4 fusion.125
  114.6 5.1 fusion.126
  128.0 4.4 fusion.125
  132.4 5.1 fusion.126
  142.7 5.7 fusion.70
  148.4 143.1 %reduce-scatter.12.cloned.1.call-done = f32[256,2048]{1,0:T(8,128)} async-done(((f32[1024,2048]{1,0:T(8,128)}), f32[256,2048]{1,0:T(8,128)}) %reduce-scatter.12.cloned.1.call-update) | async-done | bytes 2097168 | tf_op jit(solution)/shard_map/reduce_scatter | solution.py:137
  298.4 81.0 %all-gather.7.cloned.1.call-done = bf16[1024,2048]{1,0:T(8,128)(2,1)} async-done(((bf16[256,2048]{1,0:T(8,128)(2,1)}), bf16[1024,2048]{1,0:T(8,128)(2,1)}) %all-gather.7.cloned.1.call-update) | async-done | bytes 4194320 | tf_op jit(solution)/shard_map/all_gather | solution.py:146
  379.4 15.4 %fusion.72 = f32[1024,2048]{1,0:T(8,128)} fusion(bf16[1024,2048]{1,0:T(8,128)(2,1)} %all-gather.7.cloned.1.call-done, bf16[2048,2048]{1,0:T(8,128)(2,1)} %param.24), kind=kOutput, calls=%fused_computation.134 | convolution fusion | flops 8589934592 | bytes 20971520 | tf_op jit(solution)/shard_map/dot_general | solution.py:148
  394.9 13.3 %fusion.71 = f32[1024,2048]{1,0:T(8,128)} fusion(bf16[1024,2048]{1,0:T(8,128)(2,1)S(1)} %copy-done.38, bf16[2048,2048]{1,0:T(8,128)(2,1)} %param.23), kind=kOutput, calls=%fused_computation.133 | convolution fusion | flops 8589934592 | bytes 20971520 | tf_op jit(solution)/shard_map/dot_general | solution.py:147
  408.2 52.0 %all-gather.9.cloned.1.call-done = bf16[1024,2048]{1,0:T(8,128)(2,1)} async-done(((bf16[256,2048]{1,0:T(8,128)(2,1)}), bf16[1024,2048]{1,0:T(8,128)(2,1)}) %all-gather.9.cloned.1.call-update) | async-done | bytes 4194320 | tf_op jit(solution)/shard_map/all_gather | solution.py:161
  460.2 21.7 %multiply_convert_fusion = (bf16[1024,2048]{1,0:T(8,128)(2,1)}, bf16[1024,2048]{1,0:T(8,128)(2,1)}, bf16[1024,2048]{1,0:T(8,128)(2,1)}) fusion(f32[1024,2048]{1,0:T(8,128)} %fusion.71, f32[1024,2048]{1,0:T(8,128)} %fusion.72, bf16[1024,2048]{1,0:T(8,128)(2,1)} %all-gather.9.cloned.1.call-done, bf16[2048,2048]{1,0:T(8,128)(2,1)} %param.25), kind=kOutput, calls=%fused_computation.60 | convolution fusion | flops 8621391872 | bytes 41943040 | tf_op jit(solution)/shard_map/dot_general | solution.py:59
  481.9 13.1 %fusion.73 = f32[1024,2048]{1,0:T(8,128)S(1)} fusion(bf16[1024,2048]{1,0:T(8,128)(2,1)} %get-tuple-element.235, bf16[2048,2048]{1,0:T(8,128)(2,1)} %param.23), kind=kOutput, calls=%fused_computation.135 | convolution fusion | flops 8589934592 | bytes 20971520 | tf_op jit(solution)/shard_map/dot_general | solution.py:59
  495.1 13.6 %convolution_add_fusion = f32[1024,2048]{1,0:T(8,128)} fusion(f32[1024,2048]{1,0:T(8,128)S(1)} %fusion.73, bf16[1024,2048]{1,0:T(8,128)(2,1)S(1)} %copy-done.42, bf16[2048,2048]{1,0:T(8,128)(2,1)} %param.24), kind=kOutput, calls=%fused_computation.68 | convolution fusion | flops 8592031744 | bytes 29360128 | tf_op jit(solution)/shard_map/dot_general | solution.py:59
  508.7 143.1 %reduce-scatter.16.cloned.1.call-done = f32[256,2048]{1,0:T(8,128)} async-done(((f32[1024,2048]{1,0:T(8,128)}), f32[256,2048]{1,0:T(8,128)}) %reduce-scatter.16.cloned.1.call-update) | async-done | bytes 2097168 | tf_op jit(solution)/shard_map/reduce_scatter | solution.py:170
  659.3 14.3 %convolution_convert_fusion = bf16[2048,2048]{1,0:T(8,128)(2,1)} fusion(bf16[1024,2048]{1,0:T(8,128)(2,1)} %get-tuple-element.236, bf16[1024,2048]{1,0:T(8,128)(2,1)} %all-gather.9.cloned.1.call-done), kind=kOutput, calls=%fused_computation.65 | convolution fusion | flops 8594128896 | bytes 16777216 | tf_op jit(solution)/shard_map/dot_general | solution.py:53
  673.6 14.1 %convolution_convert_fusion.1 = bf16[2048,2048]{1,0:T(8,128)(2,1)} fusion(bf16[1024,2048]{1,0:T(8,128)(2,1)} %all-gather.7.cloned.1.call-done, bf16[1024,2048]{1,0:T(8,128)(2,1)} %get-tuple-element.234), kind=kOutput, calls=%fused_computation.66 | convolution fusion | flops 8594128896 | bytes 16777216 | tf_op jit(solution)/shard_map/dot_general | solution.py:53
  687.8 14.1 %convolution_convert_fusion.2 = bf16[2048,2048]{1,0:T(8,128)(2,1)} fusion(bf16[1024,2048]{1,0:T(8,128)(2,1)} %all-gather.7.cloned.1.call-done, bf16[1024,2048]{1,0:T(8,128)(2,1)} %get-tuple-element.235), kind=kOutput, calls=%fused_computation.67 | convolution fusion | flops 8594128896 | bytes 16777216 | tf_op jit(solution)/shard_map/dot_general | solution.py:53
  702.0 38.9 %all-gather.11.cloned.1.call-done = bf16[1024,2048]{1,0:T(8,128)(2,1)} async-done(((bf16[256,2048]{1,0:T(8,128)(2,1)}), bf16[1024,2048]{1,0:T(8,128)(2,1)}) %all-gather.11.cloned.1.call-update) | async-done | bytes 4194320 | tf_op jit(solution)/shard_map/all_gather | solution.py:181
  740.9 5.5 convolution_convert_fusion.7
  746.4 138.8 %while.29 = (s32[]{:T(128)}, f32[1024,2,64]{0,2,1:T(8,128)}, f32[1024,2,64]{0,2,1:T(8,128)}, f32[2,512,2,4,64]{1,0,4,3,2:T(2,128)}, s32[2]{0:T(128)S(1)}, /*inde...) while((s32[]{:T(128)}, f32[1024,2,64]{0,2,1:T(8,128)}, ...), condition=%wide.region_15.16_spmd.clone, body=%wide.region_13.15_spmd.clone.sunk | while | flops 2749755904 | bytes 146733376 | solution.py:225
  755.2 4.5 fusion.140
  759.7 11.5 fusion.137
  771.2 11.3 fusion.138
  782.5 6.0 fusion.139
  788.5 6.1 fusion.141
  795.7 19.7 %dynamic_update_slice.21 = f32[2,512,2,4,64]{1,0,4,3,2:T(2,128)} dynamic-update-slice(f32[2,512,2,4,64]{1,0,4,3,2:T(2,128)} %get-tuple-element.425, f32[1,512,2,4,64]{1,0,4,3,2:T(1,128)S(1)} %copy.43, s32[]{:T(128)S(6)} %copy.62, s32[]{:T(128)} %constant.35.clone.1..sunk.1, s32[]{:T(128)} %constant.35.clone.1..sunk.1, s32[]{:T(128)} %constant.35.clone.1..sunk.1, s32[]{:T(128)} %constant.35.clone.1..sunk.1) | dynamic-update-slice | bytes 2097156 | tf_op jit(solution)/shard_map/while/body/jit(dynamic_update_index_in_dim)/dynamic_update_slice | solution.py:135
  823.6 5.6 fusion.140
  829.1 11.6 fusion.137
  840.7 11.3 fusion.138
  852.0 6.1 fusion.139
  858.2 6.1 fusion.141
  865.4 19.7 %dynamic_update_slice.21 = f32[2,512,2,4,64]{1,0,4,3,2:T(2,128)} dynamic-update-slice(f32[2,512,2,4,64]{1,0,4,3,2:T(2,128)} %get-tuple-element.425, f32[1,512,2,4,64]{1,0,4,3,2:T(1,128)S(1)} %copy.43, s32[]{:T(128)S(6)} %copy.62, s32[]{:T(128)} %constant.35.clone.1..sunk.1, s32[]{:T(128)} %constant.35.clone.1..sunk.1, s32[]{:T(128)} %constant.35.clone.1..sunk.1, s32[]{:T(128)} %constant.35.clone.1..sunk.1) | dynamic-update-slice | bytes 2097156 | tf_op jit(solution)/shard_map/while/body/jit(dynamic_update_index_in_dim)/dynamic_update_slice | solution.py:135
  891.4 3.8 convolution_convert_fusion.5
  897.1 6.8 convolution_convert_fusion.6
  905.6 8.5 convolution_convert_fusion.4
  914.2 14.1 %convolution_convert_fusion.3 = bf16[1024,2048]{1,0:T(8,128)(2,1)} fusion(bf16[1024,2048]{1,0:T(8,128)(2,1)} %get-tuple-element.236, bf16[2048,2048]{1,0:T(8,128)(2,1)} %param.25), kind=kOutput, calls=%fused_computation.69 | convolution fusion | flops 8592031744 | bytes 16777216 | tf_op jit(solution)/shard_map/dot_general | solution.py:155
  933.9 30.2 %reduce-scatter.28.cloned.1.call-done = bf16[256,2048]{1,0:T(8,128)(2,1)} async-done(((bf16[2048,2048]{1,0:T(8,128)(2,1)}), bf16[256,2048]{1,0:T(8,128)(2,1)}) %reduce-scatter.28.cloned.1.call-update) | async-done | bytes 1048592 | tf_op jit(solution)/shard_map/reduce_scatter | solution.py:267
  966.9 35.2 %reduce-scatter.22.cloned.1.call-done = bf16[256,128]{1,0:T(8,128)(2,1)} async-done(((bf16[2048,128]{1,0:T(8,128)(2,1)}), bf16[256,128]{1,0:T(8,128)(2,1)}) %reduce-scatter.22.cloned.1.call-update) | async-done | bytes 65552 | tf_op jit(solution)/shard_map/reduce_scatter | solution.py:258
  1003.6 36.3 %reduce-scatter.24.cloned.1.call-done = bf16[256,128]{1,0:T(8,128)(2,1)} async-done(((bf16[2048,128]{1,0:T(8,128)(2,1)}), bf16[256,128]{1,0:T(8,128)(2,1)}) %reduce-scatter.24.cloned.1.call-update) | async-done | bytes 65552 | tf_op jit(solution)/shard_map/reduce_scatter | solution.py:261
  1041.4 43.3 %reduce-scatter.26.cloned.1.call-done = bf16[512,256]{1,0:T(8,128)(2,1)} async-done(((bf16[512,2048]{1,0:T(8,128)(2,1)}), bf16[512,256]{1,0:T(8,128)(2,1)}) %reduce-scatter.26.cloned.1.call-update) | async-done | bytes 262160 | tf_op jit(solution)/shard_map/reduce_scatter | solution.py:264
  1086.5 42.7 %reduce-scatter.20.cloned.1.call-done = bf16[256,512]{1,0:T(8,128)(2,1)} async-done(((bf16[2048,512]{1,0:T(8,128)(2,1)}), bf16[256,512]{1,0:T(8,128)(2,1)}) %reduce-scatter.20.cloned.1.call-update) | async-done | bytes 262160 | tf_op jit(solution)/shard_map/reduce_scatter | solution.py:255
  1131.0 77.3 %reduce-scatter.18.cloned.1.call-done = bf16[256,2048]{1,0:T(8,128)(2,1)} async-done(((bf16[1024,2048]{1,0:T(8,128)(2,1)}), bf16[256,2048]{1,0:T(8,128)(2,1)}) %reduce-scatter.18.cloned.1.call-update) | async-done | bytes 1048592 | tf_op jit(solution)/shard_map/reduce_scatter | solution.py:242
  1210.4 46.3 %all-reduce = (f32[2048]{0:T(1024)}, f32[2048]{0:T(1024)}) all-reduce(f32[2048]{0:T(1024)S(1)} %get-tuple-element.186, f32[2048]{0:T(1024)S(1)} %copy-done.30), channel_id=1, replica_groups=mesh['wide'=8,'narrow'=4] {'wide','narrow'}, use_global_device_ids=true, to_apply=%region_19.20 | all-reduce | flops 4096 | bytes 32768 | tf_op jit(solution)/shard_map/psum | solution.py:253
  1256.7 32.1 %reduce-scatter.14.cloned.1.call-done = bf16[256,2048]{1,0:T(8,128)(2,1)} async-done(((bf16[1024,2048]{1,0:T(8,128)(2,1)}), bf16[256,2048]{1,0:T(8,128)(2,1)}) %reduce-scatter.14.cloned.1.call-update) | async-done | bytes 1048592 | tf_op jit(solution)/shard_map/reduce_scatter | solution.py:154
  1288.8 5.9 fusion.59
  (207 shorter events, 84.4 us)
Async XLA Ops:
  7.2 135.5 %copy-start = (bf16[512,2048]{1,0:T(8,128)(2,1)S(1)}, bf16[512,2048]{1,0:T(8,128)(2,1)}, u32[]{:S(2)}) copy-start(bf16[512,2048]{1,0:T(8,128)(2,1)} %param.22) | copy-start | bytes 6291460
  7.2 4.4 copy-start.39
  7.2 8.6 copy-start.23
  7.2 87.9 %all-gather.5.cloned.1.call-start = ((), (), s32[]{:S(2)}) async-start(), calls=%async_computation.11 | async-start | bytes 5242880 | tf_op jit(solution)/shard_map/all_gather | solution.py:101
  8.9 7.7 copy-start.24
  11.5 280.0 %reduce-scatter.12.cloned.1.call-start = ((), (), s32[]{:S(2)}) async-start(), calls=%async_computation.12 | async-start | bytes 10485760 | tf_op jit(solution)/shard_map/reduce_scatter | solution.py:137
  12.6 90.1 %copy-start.13 = (f32[1024,32]{0,1:T(8,128)}, f32[1024,32]{0,1:T(8,128)S(1)}, u32[]{:S(2)}) copy-start(f32[1024,32]{0,1:T(8,128)S(1)} %get-tuple-element.249) | copy-start | bytes 393220
  12.6 90.1 %copy-start.15 = (f32[1024,32]{0,1:T(8,128)}, f32[1024,32]{0,1:T(8,128)S(1)}, u32[]{:S(2)}) copy-start(f32[1024,32]{0,1:T(8,128)S(1)} %get-tuple-element.250) | copy-start | bytes 393220
  110.2 4.4 copy-start.21
  138.6 9.7 copy-start.4
  138.6 9.7 copy-start.17
  138.6 9.7 copy-start.26
  138.6 9.7 copy-start.40
  138.7 9.7 copy-start.2
  148.4 146.6 %copy-start.27 = (f32[2048]{0:T(1024)S(1)}, f32[2048]{0:T(1024)}, u32[]{:S(2)}) copy-start(f32[2048]{0:T(1024)} %param.18) | copy-start | bytes 24580
  148.4 231.1 %all-gather.7.cloned.1.call-start = ((), (), s32[]{:S(2)}) async-start(), calls=%async_computation.13 | async-start | bytes 5242880 | tf_op jit(solution)/shard_map/all_gather | solution.py:146
  294.9 360.4 %copy-start.31 = (f32[256]{0:T(256)}, f32[256]{0:T(256)S(1)}, u32[]{:S(2)}) copy-start(f32[256]{0:T(256)S(1)} %add_rsqrt_fusion) | copy-start | bytes 3076
  297.8 162.4 %all-gather.9.cloned.1.call-start = ((), (), s32[]{:S(2)}) async-start(), calls=%async_computation.15 | async-start | bytes 5242880 | tf_op jit(solution)/shard_map/all_gather | solution.py:161
  298.4 353.5 %reduce-scatter.16.cloned.1.call-start = ((), (), s32[]{:S(2)}) async-start(), calls=%async_computation.16 | async-start | bytes 10485760 | tf_op jit(solution)/shard_map/reduce_scatter | solution.py:170
  379.4 15.4 %copy-start.38 = (bf16[1024,2048]{1,0:T(8,128)(2,1)S(1)}, bf16[1024,2048]{1,0:T(8,128)(2,1)}, u32[]{:S(2)}) copy-start(bf16[1024,2048]{1,0:T(8,128)(2,1)} %all-gather.7.cloned.1.call-done) | copy-start | bytes 12582916
  481.9 13.2 %copy-start.42 = (bf16[1024,2048]{1,0:T(8,128)(2,1)S(1)}, bf16[1024,2048]{1,0:T(8,128)(2,1)}, u32[]{:S(2)}) copy-start(bf16[1024,2048]{1,0:T(8,128)(2,1)} %get-tuple-element.234) | copy-start | bytes 12582916
  508.7 147.3 %copy-start.10 = (bf16[256,2048]{1,0:T(8,128)(2,1)S(1)}, bf16[256,2048]{1,0:T(8,128)(2,1)}, u32[]{:S(2)}) copy-start(bf16[256,2048]{1,0:T(8,128)(2,1)} %param.26) | copy-start | bytes 3145732
  508.7 232.2 %all-gather.11.cloned.1.call-start = ((), (), s32[]{:S(2)}) async-start(), calls=%async_computation.17 | async-start | bytes 5242880 | tf_op jit(solution)/shard_map/all_gather | solution.py:181
  659.2 269.1 %reduce-scatter.32.cloned.1.call-start = ((), (), s32[]{:S(2)}) async-start(), calls=%async_computation.25 | async-start | bytes 9437184 | tf_op jit(solution)/shard_map/reduce_scatter | solution.py:273
  673.5 257.5 %reduce-scatter.30.cloned.1.call-start = ((), (), s32[]{:S(2)}) async-start(), calls=%async_computation.24 | async-start | bytes 9437184 | tf_op jit(solution)/shard_map/reduce_scatter | solution.py:270
  687.7 276.4 %reduce-scatter.28.cloned.1.call-start = ((), (), s32[]{:S(2)}) async-start(), calls=%async_computation.23 | async-start | bytes 9437184 | tf_op jit(solution)/shard_map/reduce_scatter | solution.py:267
  701.9 44.5 %copy-start.5 = (bf16[1024,2,64]{0,2,1:T(8,128)(2,1)S(1)}, bf16[1024,2,64]{0,2,1:T(8,128)(2,1)}, u32[]{:S(2)}) copy-start(bf16[1024,2,64]{0,2,1:T(8,128)(2,1)} %copy-done.4) | copy-start | bytes 786436
  701.9 44.5 %copy-start.9 = (bf16[1024,2,64]{0,2,1:T(8,128)(2,1)S(1)}, bf16[1024,2,64]{0,2,1:T(8,128)(2,1)}, u32[]{:S(2)}) copy-start(bf16[1024,2,64]{0,2,1:T(8,128)(2,1)} %get-tuple-element.468) | copy-start | bytes 786436
  701.9 44.5 %copy-start.18 = (s32[1024]{0:T(1024)S(1)}, s32[1024]{0:T(1024)}, u32[]{:S(2)}) copy-start(s32[1024]{0:T(1024)} %copy-done.17) | copy-start | bytes 12292
  701.9 44.5 %copy-start.41 = (s32[2]{0:T(128)S(1)}, s32[2]{0:T(128)}, u32[]{:S(2)}) copy-start(s32[2]{0:T(128)} %copy-done.40) | copy-start | bytes 28
  701.9 300.2 %reduce-scatter.22.cloned.1.call-start = ((), (), s32[]{:S(2)}) async-start(), calls=%async_computation.20 | async-start | bytes 589824 | tf_op jit(solution)/shard_map/reduce_scatter | solution.py:258
  771.2 11.3 copy-start.3
  840.7 11.3 copy-start.3
  885.2 4.4 copy-start.14
  885.2 4.4 copy-start.16
  896.3 143.6 %reduce-scatter.24.cloned.1.call-start = ((), (), s32[]{:S(2)}) async-start(), calls=%async_computation.21 | async-start | bytes 589824 | tf_op jit(solution)/shard_map/reduce_scatter | solution.py:261
  897.0 187.6 %reduce-scatter.26.cloned.1.call-start = ((), (), s32[]{:S(2)}) async-start(), calls=%async_computation.22 | async-start | bytes 2359296 | tf_op jit(solution)/shard_map/reduce_scatter | solution.py:264
  904.0 225.2 %reduce-scatter.20.cloned.1.call-start = ((), (), s32[]{:S(2)}) async-start(), calls=%async_computation.19 | async-start | bytes 2359296 | tf_op jit(solution)/shard_map/reduce_scatter | solution.py:255
  905.6 302.7 %reduce-scatter.18.cloned.1.call-start = ((), (), s32[]{:S(2)}) async-start(), calls=%async_computation.18 | async-start | bytes 5242880 | tf_op jit(solution)/shard_map/reduce_scatter | solution.py:242
  914.1 374.6 %reduce-scatter.14.cloned.1.call-start = ((), (), s32[]{:S(2)}) async-start(), calls=%async_computation.14 | async-start | bytes 5242880 | tf_op jit(solution)/shard_map/reduce_scatter | solution.py:154
  931.0 277.3 %copy-start.6 = (bf16[256,2048]{1,0:T(8,128)(2,1)S(1)}, bf16[256,2048]{1,0:T(8,128)(2,1)}, u32[]{:S(2)}) copy-start(bf16[256,2048]{1,0:T(8,128)(2,1)} %param.16) | copy-start | bytes 3145732
  931.0 277.3 %copy-start.29 = (f32[2048]{0:T(1024)S(1)}, f32[2048]{0:T(1024)}, u32[]{:S(2)}) copy-start(f32[2048]{0:T(1024)} %param.17) | copy-start | bytes 24580
  931.0 277.3 %copy-start.34 = (f32[256]{0:T(256)S(1)}, f32[256]{0:T(256)}, u32[]{:S(2)}) copy-start(f32[256]{0:T(256)} %copy-done.33) | copy-start | bytes 3076
  933.9 276.4 %copy-start.30 = (f32[2048]{0:T(1024)S(1)}, f32[2048]{0:T(1024)}, u32[]{:S(2)}) copy-start(f32[2048]{0:T(1024)} %get-tuple-element.184) | copy-start | bytes 24580
  933.9 354.8 %copy-start.28 = (f32[2048]{0:T(1024)S(1)}, f32[2048]{0:T(1024)}, u32[]{:S(2)}) copy-start(f32[2048]{0:T(1024)} %param.18) | copy-start | bytes 24580
  933.9 354.8 %copy-start.32 = (f32[256]{0:T(256)S(1)}, f32[256]{0:T(256)}, u32[]{:S(2)}) copy-start(f32[256]{0:T(256)} %copy-done.31) | copy-start | bytes 3076
  933.9 354.8 %copy-start.36 = (f32[256]{0:T(256)S(1)}, f32[256]{0:T(256)}, u32[]{:S(2)}) copy-start(f32[256]{0:T(256)} %copy-done.35) | copy-start | bytes 3076
  1256.6 38.0 %copy-start.1 = (bf16[512,2048]{1,0:T(8,128)(2,1)S(1)}, bf16[512,2048]{1,0:T(8,128)(2,1)}, u32[]{:S(2)}) copy-start(bf16[512,2048]{1,0:T(8,128)(2,1)} %param.22) | copy-start | bytes 6291460
  (16 other events, 50.8 us)
Sparse Core Ops, SparseCore 0:
  11.7 83.4 all-gather.4
  148.5 142.9 reduce-scatter.11
  297.9 81.4 all-gather.6
  380.9 79.2 all-gather.8
  508.8 142.9 reduce-scatter.15
  659.3 81.4 all-gather.10
  744.3 69.8 reduce-scatter.31
  818.0 71.2 reduce-scatter.29
  892.8 71.2 reduce-scatter.27
  967.9 34.1 reduce-scatter.21
  1005.7 34.1 reduce-scatter.23
  1043.4 41.2 reduce-scatter.25
  1088.0 41.1 reduce-scatter.19
  1131.5 76.7 reduce-scatter.17
  1210.4 78.2 reduce-scatter.13
where the time goes:
time: 1310 us; the launch traced here: 1300 us
  waiting for transfers between devices  834 us (64%)
  matrix products  252 us (19%)
  other arithmetic  80.9 us (6%)
  local copies, waits for them, and re-layouts  63.8 us (5%)
  blocking collectives  46.3 us (4%)
  between operations  14.7 us (1%)
    reduce_scatter x1, waiting for transfers between devices, on_device(): lax.psum_scatter(contract_cols(gate_grad_low, w_gate) + contract_cols(up_...  143 us
    reduce_scatter x1, waiting for transfers between devices, on_device(): lax.psum_scatter(jnp.dot(heads_out, w_out, preferred_element_type=jnp.flo...  143 us
    all_gather x1, waiting for transfers between devices, on_device(): gathered_two = lax.all_gather(normed_two, 'narrow', axis=0, tiled=True)  81 us
    all_gather x1, waiting for transfers between devices, on_device(): gathered_one = lax.all_gather(normed_one, 'narrow', axis=0, tiled=True)  77.6 us
    reduce_scatter x1, waiting for transfers between devices, on_device(): lax.psum_scatter(contract_cols(joined_grad, w_joined).astype(jnp.bfloat16...  77.3 us
    dot_general x5, matrix products, contract_cols(): lax.dot_general(left, right, (((1,), (1,)), ((), ())), preferred_element_...  62.5 us
    dot_general x5, matrix products, contract_rows(): lax.dot_general(left, right, (((0,), (0,)), ((), ())), preferred_element_...  53 us
    all_gather x1, waiting for transfers between devices, on_device(): upstream_full = lax.all_gather(upstream, 'narrow', axis=0, tiled=True)  52 us
  transfers between devices with their start and end apart: 15, of which 13 were waited for; matrix products, arithmetic and copies ran while one was open for 21% of the time, Pallas kernels for 0%

commit v1 on v0

v1 whole, which is shorter than its diff:
```python
import functools, math
import jax, jax.numpy as jnp
from jax import lax
from jax.experimental import pallas as pl
from jax.experimental.pallas import tpu as pltpu

from jax.sharding import PartitionSpec as P

HD = 64
EPSILON = 1e-05
THETA_BASE = 500000.0
LANES = 128
VMEM_LIMIT = 56 * 1024 * 1024


def dot_nn(a, b):
    return lax.dot_general(a, b, (((1,), (0,)), ((), ())), preferred_element_type=jnp.float32)


def dot_nt(a, b):
    return lax.dot_general(a, b, (((1,), (1,)), ((), ())), preferred_element_type=jnp.float32)


def swap_halves(x):
    parts = []
    for t in range(x.shape[1] // LANES):
        tile = x[:, t * LANES : (t + 1) * LANES]
        lane = lax.broadcasted_iota(jnp.int32, tile.shape, 1)
        left = pltpu.roll(tile, LANES - HD // 2, 1)
        right = pltpu.roll(tile, HD // 2, 1)
        parts.append(jnp.where(lane % HD < HD // 2, left, right))
    return parts[0] if len(parts) == 1 else jnp.concatenate(parts, axis=1)


def turn(x, cosine, sine):
    n = x.shape[1] // LANES
    s = swap_halves(x)
    outs = [
        x[:, i * LANES : (i + 1) * LANES] * cosine + s[:, i * LANES : (i + 1) * LANES] * sine
        for i in range(n)
    ]
    return outs[0] if n == 1 else jnp.concatenate(outs, axis=1)


def qkv_body(qw, kw, x_ref, w_ref, cos_ref, sin_ref, q_ref, k_ref, v_ref):
    y = dot_nn(x_ref[...], w_ref[...])
    c, s = cos_ref[...], sin_ref[...]
    q_ref[...] = (turn(y[:, :qw], c, s) * (HD ** -0.5)).astype(jnp.bfloat16)
    k_ref[...] = turn(y[:, qw : qw + kw], c, s).astype(jnp.bfloat16)
    v_ref[...] = y[:, qw + kw :].astype(jnp.bfloat16)


def qkv_call(x, w, cosine, sine, qw, kw):
    rows, d = x.shape
    br = min(256, rows)
    spec = lambda n: pl.BlockSpec((br, n), lambda i: (i, 0))
    return pl.pallas_call(
        functools.partial(qkv_body, qw, kw),
        grid=(rows // br,),
        in_specs=[spec(d), pl.BlockSpec(w.shape, lambda i: (0, 0)), spec(LANES), spec(LANES)],
        out_specs=[spec(qw), spec(kw), spec(kw)],
        out_shape=[
            jax.ShapeDtypeStruct((rows, qw), jnp.bfloat16),
            jax.ShapeDtypeStruct((rows, kw), jnp.bfloat16),
            jax.ShapeDtypeStruct((rows, kw), jnp.bfloat16),
        ],
        compiler_params=pltpu.CompilerParams(vmem_limit_bytes=VMEM_LIMIT),
        cost_estimate=pl.CostEstimate(
            flops=2 * rows * d * w.shape[1], bytes_accessed=2 * (x.size + w.size) + 4 * rows * qw, transcendentals=0
        ),
        name="qkv",
    )(x, w, cosine, sine)


def half_mask(rows):
    lane = lax.broadcasted_iota(jnp.int32, (rows, LANES), 1)
    return lane < HD


def stack_heads(x, low):
    zero = jnp.zeros((x.shape[0], LANES), x.dtype)
    a, b = x[:, :LANES], x[:, LANES : 2 * LANES]
    return jnp.concatenate(
        [jnp.where(low, a, zero), jnp.where(low, zero, a), jnp.where(low, b, zero), jnp.where(low, zero, b)], axis=0
    )


def unstack_heads(x, low):
    r = x.shape[0] // 4
    return jnp.concatenate(
        [jnp.where(low, x[:r], x[r : 2 * r]), jnp.where(low, x[2 * r : 3 * r], x[3 * r :])], axis=1
    )


def allowed_mask(ext, b0, r, start):
    j = lax.broadcasted_iota(jnp.int32, (ext, 4 * r), 0)
    t = lax.broadcasted_iota(jnp.int32, (ext, 4 * r), 1) % r + b0
    return (j <= t) & (j >= start)


def block_extent(b0, r, total):
    return min(total, -(-(b0 + r) // LANES) * LANES)


def fwd_body(blocks, r, kv, group, q_ref, k_ref, v_ref, start_ref, o_ref, lse_ref):
    low = half_mask(r)
    total = k_ref.shape[0]
    width = group * HD
    for c in range(kv):
        vt = v_ref[:, c * LANES : (c + 1) * LANES].T
        for n, b0 in enumerate(blocks):
            ext = block_extent(b0, r, total)
            q4 = stack_heads(q_ref[b0 : b0 + r, c * width : (c + 1) * width], low)
            s = dot_nt(k_ref[:ext, c * LANES : (c + 1) * LANES], q4)
            s = jnp.where(allowed_mask(ext, b0, r, start_ref[n : n + 1, :]), s, -1e30)
            top = jnp.max(s, axis=0, keepdims=True)
            p = jnp.exp(s - top)
            total_p = jnp.sum(p, axis=0, keepdims=True)
            ot = dot_nn(vt[:, :ext], p.astype(jnp.bfloat16)) * (1.0 / total_p)
            o_ref[n * r : (n + 1) * r, c * width : (c + 1) * width] = unstack_heads(ot.T, low).astype(jnp.bfloat16)
            lse_ref[c, n : n + 1, :] = top + jnp.log(total_p)


def attend(q, k, v, start, blocks, r, kv, group):
    nb = len(blocks)
    area = sum(block_extent(b, r, q.shape[0]) for b in blocks) * r * kv * group
    return pl.pallas_call(
        functools.partial(fwd_body, blocks, r, kv, group),
        out_shape=[
            jax.ShapeDtypeStruct((nb * r, kv * group * HD), jnp.bfloat16),
            jax.ShapeDtypeStruct((kv, nb, 4 * r), jnp.float32),
        ],
        compiler_params=pltpu.CompilerParams(vmem_limit_bytes=VMEM_LIMIT),
        cost_estimate=pl.CostEstimate(flops=area * 512, bytes_accessed=4 << 20, transcendentals=area),
        name="attend",
    )(q, k, v, start)


def bwd_body(blocks, r, kv, group, first, last, *refs):
    refs = list(refs)
    q_ref, k_ref, v_ref, start_ref, do_ref, o_ref, lse_ref = refs[:7]
    refs = refs[7:]
    if not first:
        dq_in, dk_in, dv_in = refs[:3]
        refs = refs[3:]
    if last:
        cos_ref, sin_ref = refs[:2]
        out_ref, dq_s, dk_s, dv_s = refs[2:]
    else:
        dq_s, dk_s, dv_s = refs
    low = half_mask(r)
    total = k_ref.shape[0]
    width = group * HD
    for c in range(kv):
        cl = slice(c * LANES, (c + 1) * LANES)
        cw = slice(c * width, (c + 1) * width)
        kt = k_ref[:, cl].T
        if first:
            dk_s[:, cl] = jnp.zeros((total, LANES), jnp.float32)
            dv_s[:, cl] = jnp.zeros((total, LANES), jnp.float32)
        else:
            dk_s[:, cl] = dk_in[:, cl]
            dv_s[:, cl] = dv_in[:, cl]
        for n, b0 in enumerate(blocks):
            ext = block_extent(b0, r, total)
            q4 = stack_heads(q_ref[b0 : b0 + r, cw], low)
            do4 = stack_heads(do_ref[n * r : (n + 1) * r, cw], low)
            o4 = stack_heads(o_ref[n * r : (n + 1) * r, cw], low)
            delta = jnp.sum((do4.astype(jnp.float32) * o4.astype(jnp.float32)).T, axis=0, keepdims=True)
            s = dot_nt(k_ref[:ext, cl], q4)
            p = jnp.exp(
                jnp.where(allowed_mask(ext, b0, r, start_ref[n : n + 1, :]), s - lse_ref[c, n : n + 1, :], -1e30)
            )
            dp = dot_nt(v_ref[:ext, cl], do4)
            ds = (p * (dp - delta)).astype(jnp.bfloat16)
            dq4 = dot_nn(kt[:, :ext], ds).T
            dq_s[n * r : (n + 1) * r, cw] = unstack_heads(dq4, low) * (HD ** -0.5)
            dk_s[:ext, cl] += dot_nn(ds, q4)
            dv_s[:ext, cl] += dot_nn(p.astype(jnp.bfloat16), do4)
    if not last:
        return
    nc = 1 if first else 2
    cosine, sine = cos_ref[...], -sin_ref[...]
    qw = kv * width
    for n, b0 in enumerate(blocks):
        cs, sn = cos_ref[b0 : b0 + r, :], -sin_ref[b0 : b0 + r, :]
        out_ref[b0 : b0 + r, :qw] = turn(dq_s[n * r : (n + 1) * r, :], cs, sn).astype(jnp.bfloat16)
        if not first:
            a0 = b0 - r
            cs, sn = cos_ref[a0 : a0 + r, :], -sin_ref[a0 : a0 + r, :]
            out_ref[a0 : a0 + r, :qw] = turn(dq_in[n * r : (n + 1) * r, :], cs, sn).astype(jnp.bfloat16)
    lane = lax.broadcasted_iota(jnp.int32, (total, LANES), 1) < HD

    def fold(x):
        return x + pltpu.roll(x, HD, 1)

    for i, (ref, rot) in enumerate(((dk_s, True), (dv_s, False))):
        for c in range(0, kv, 2):
            x = fold(ref[:, c * LANES : (c + 1) * LANES])
            if c + 1 < kv:
                x = jnp.where(lane, x, fold(ref[:, (c + 1) * LANES : (c + 2) * LANES]))
            if rot:
                x = turn(x, cosine, sine)
            x = x.astype(jnp.bfloat16)
            at = qw + i * kv * HD + c * HD
            if c + 1 < kv:
                out_ref[:, at : at + LANES] = x
            else:
                out_ref[:, at : at + HD] = x[:, :HD]


def attend_back(q, k, v, start, do, o, lse, carried, tables, blocks, r, kv, group):
    first, last = carried is None, tables is not None
    rows = q.shape[0]
    nb = len(blocks)
    area = sum(block_extent(b, r, rows) for b in blocks) * r * kv * group
    sums = [
        jax.ShapeDtypeStruct((nb * r, kv * group * HD), jnp.float32),
        jax.ShapeDtypeStruct((rows, kv * LANES), jnp.float32),
        jax.ShapeDtypeStruct((rows, kv * LANES), jnp.float32),
    ]
    if last:
        out = jax.ShapeDtypeStruct((rows, kv * (group + 2) * HD), jnp.bfloat16)
        scratch = [pltpu.VMEM(s.shape, s.dtype) for s in sums]
    else:
        out, scratch = sums, []
    args = (q, k, v, start, do, o, lse) + (() if first else tuple(carried)) + (tuple(tables) if last else ())
    return pl.pallas_call(
        functools.partial(bwd_body, blocks, r, kv, group, first, last),
        out_shape=out,
        scratch_shapes=scratch,
        compiler_params=pltpu.CompilerParams(vmem_limit_bytes=VMEM_LIMIT),
        cost_estimate=pl.CostEstimate(flops=area * 1280, bytes_accessed=8 << 20, transcendentals=area),
        name="attend_back",
    )(*args)


def mlp_body(x_ref, dy_ref, wg_ref, wu_ref, wd_ref, m_ref, dg_ref, du_ref):
    x = x_ref[...]
    dy = dy_ref[...].reshape(x.shape)
    gate = dot_nn(x, wg_ref[...])
    up = dot_nn(x, wu_ref[...])
    dm = dot_nt(dy, wd_ref[...])
    sig = 1.0 / (1.0 + jnp.exp(-gate))
    act = gate * sig
    m_ref[...] = (act * up).astype(jnp.bfloat16)
    du_ref[...] = (dm * act).astype(jnp.bfloat16)
    dg_ref[...] = (dm * up * (sig * (1.0 + gate * (1.0 - sig)))).astype(jnp.bfloat16)


def mlp_call(x, dy, wg, wu, wd):
    t, d = x.shape
    f = wg.shape[1]
    bf = min(256, f)
    col = pl.BlockSpec((d, bf), lambda i: (0, i))
    out = pl.BlockSpec((t, bf), lambda i: (0, i))
    res = pl.BlockSpec((t, d), lambda i: (0, 0))
    return pl.pallas_call(
        mlp_body,
        grid=(f // bf,),
        in_specs=[res, res, col, col, pl.BlockSpec((bf, d), lambda i: (i, 0))],
        out_specs=[out] * 3,
        out_shape=[jax.ShapeDtypeStruct((t, f), jnp.bfloat16)] * 3,
        compiler_params=pltpu.CompilerParams(vmem_limit_bytes=VMEM_LIMIT),
        cost_estimate=pl.CostEstimate(flops=6 * t * d * f, bytes_accessed=2 * (2 * x.size + 3 * wg.size + 3 * t * f), transcendentals=t * f),
        name="mlp",
    )(x, dy, wg, wu, wd)


def grad_body(nl, nr, got, tiles_ref, *refs):
    lefts = refs[:nl]
    rights = [refs[nl + i * nl : nl + (i + 1) * nl] for i in range(nr)]
    refs = refs[nl + nl * nr :]
    recvs, outs = (refs[:nr], refs[nr:]) if got else ([None] * nr, refs)
    turned = [x[...].T for x in lefts]
    for right, recv, out in zip(rights, recvs, outs):
        total = dot_nn(turned[0], right[0][...])
        for a, b in zip(turned[1:], right[1:]):
            total += dot_nn(a, b[...])
        if got:
            total += recv[0].astype(jnp.float32)
        out[0] = total.astype(jnp.bfloat16)


def grad_call(tiles, part, lefts, rights, recvs=()):
    count = tiles.shape[0]
    nl, nr = len(lefts), len(rights)
    outs = [jax.ShapeDtypeStruct((count, part, r[0].shape[1]), jnp.bfloat16) for r in rights]
    out_specs = [pl.BlockSpec((1, part, r[0].shape[1]), lambda j, t: (j, 0, 0)) for r in rights]
    in_specs = [pl.BlockSpec((x.shape[0], part), lambda j, t: (0, t[j])) for x in lefts]
    in_specs += [
        pl.BlockSpec(x.shape, lambda j, t: (0, 0), pipeline_mode=pl.Buffered(1)) for r in rights for x in r
    ]
    if recvs:
        in_specs += out_specs
    rows = sum(x.shape[0] for x in lefts)
    cols = sum(r[0].shape[1] for r in rights)
    return pl.pallas_call(
        functools.partial(grad_body, nl, nr, bool(recvs)),
        grid_spec=pltpu.PrefetchScalarGridSpec(
            num_scalar_prefetch=1, grid=(count,), in_specs=in_specs, out_specs=out_specs
        ),
        out_shape=outs,
        compiler_params=pltpu.CompilerParams(vmem_limit_bytes=VMEM_LIMIT),
        cost_estimate=pl.CostEstimate(
            flops=2 * rows * count * part * cols,
            bytes_accessed=2 * (rows * (count * part + cols) + count * part * cols * (2 if recvs else 1)),
            transcendentals=0,
        ),
        name="weight_grad",
    )(tiles, *lefts, *[x for r in rights for x in r], *recvs)


def doc_layout(lengths, total_rows):
    ends = jnp.cumsum(lengths)
    starts = ends - lengths
    places = jnp.arange(total_rows, dtype=jnp.int32)
    owner = jnp.sum((places[:, None] >= ends[None, :]).astype(jnp.int32), axis=1)
    picked = owner[:, None] == jnp.arange(lengths.shape[0], dtype=jnp.int32)[None, :]
    first = jnp.sum(jnp.where(picked, starts[None, :], 0), axis=1)
    return first, (places - first).astype(jnp.float32)


def angle_tables(positions):
    indices = jnp.arange(HD // 2, dtype=jnp.float32)
    inverse = jnp.exp(indices * (-2.0 * math.log(THETA_BASE) / HD))
    turned = positions[:, None] * inverse[None, :]
    cosine, sine = jnp.cos(turned), jnp.sin(turned)
    return (
        jnp.concatenate([cosine] * 4, axis=1),
        jnp.concatenate([-sine, sine, -sine, sine], axis=1),
    )


def twice(w):
    heads = w.shape[1] // HD
    return jnp.concatenate([w[:, i * HD : (i + 1) * HD] for i in range(heads) for _ in range(2)], axis=1)


def after(value, *others):
    return lax.optimization_barrier((value, *others))[0]


def scatter_direct(parts, index, size):
    def block(at):
        return lax.dynamic_index_in_dim(parts, at, 0, keepdims=False)

    total = block(index).astype(jnp.float32)
    for k in range(1, size):
        got = lax.ppermute(block(index ^ k), "narrow", [(i, i ^ k) for i in range(size)])
        total = total + got.astype(jnp.float32)
    return total


def gather_line(block, index, size):
    rows = block.shape[0]
    up, down = [], []
    a = b = block
    for step in range(1, size):
        a = lax.ppermute(a, "narrow", [(i, i + 1) for i in range(step - 1, size - 1)])
        b = lax.ppermute(b, "narrow", [(i, i - 1) for i in range(1, size - step + 1)])
        up.append(a)
        down.append(b)
    full = jnp.zeros((size * rows, block.shape[1]), block.dtype)
    full = lax.dynamic_update_slice_in_dim(full, block, index * rows, 0)
    for k in range(1, size):
        got = jnp.where(index >= k, up[k - 1], down[size - k - 1])
        full = lax.dynamic_update_slice_in_dim(full, got, lax.rem(index + size - k, size) * rows, 0)
    return full


def scatter_narrow(parts, size):
    return lax.psum_scatter(
        parts.reshape(-1, parts.shape[-1]), "narrow", scatter_dimension=0, tiled=True
    ).astype(jnp.float32)


def wide_grads(lefts, rights, order, index, size):
    bits = size.bit_length() - 1
    part = lefts[0].shape[1] // size
    mine = index & 1
    pairs = 2 * jnp.arange(size // 2, dtype=jnp.int32)
    sent = grad_call(pairs + (1 - mine), part, lefts, rights)
    got = [lax.ppermute(x, "wide", [(i, i ^ 1) for i in range(size)]) for x in sent]
    sums = grad_call(pairs + mine, part, lefts, rights, got)
    results = []
    for value, bit_order in zip(sums, order):
        value = value.reshape((2,) * (bits - 1) + value.shape[1:])
        left = list(range(1, bits))[::-1]
        for bit in bit_order:
            axis = left.index(bit)
            left.pop(axis)
            here = (index >> bit) & 1
            out = lax.dynamic_index_in_dim(value, 1 - here, axis, keepdims=False).astype(jnp.bfloat16)
            kept = lax.dynamic_index_in_dim(value, here, axis, keepdims=False)
            got = lax.ppermute(out, "wide", [(i, i ^ (1 << bit)) for i in range(size)])
            value = kept.astype(jnp.float32) + got.astype(jnp.float32)
        results.append(value)
    return results


def sum_all(array, wide, narrow):
    for axis, size in (("wide", wide), ("narrow", narrow)):
        step = 1
        while step < size:
            array = array + lax.ppermute(array, axis, [(i, i ^ step) for i in range(size)])
            step *= 2
    return array


def on_device(
    hidden_in, attn_gain, mlp_gain, w_query, w_key, w_value, w_out, w_gate, w_up, w_down, upstream, doc_lengths
):
    narrow, wide = lax.axis_size("narrow"), lax.axis_size("wide")
    here, wide_here = lax.axis_index("narrow"), lax.axis_index("wide")
    local_rows, width = hidden_in.shape
    total_rows = local_rows * narrow
    chunks = 2
    r = local_rows // chunks
    query_width, key_width = w_query.shape[1], w_key.shape[1]
    kv = key_width // HD
    group = query_width // key_width
    first, positions = doc_layout(doc_lengths[0], total_rows)
    tables = angle_tables(positions)
    first_rows = first.astype(jnp.int32).reshape(narrow, chunks, r)
    starts = [jnp.tile(first_rows[:, c], (1, 4)) for c in range(chunks)]
    blocks = [[z * local_rows + c * r for z in range(narrow)] for c in range(chunks)]
    w_twice = jnp.concatenate([w_query, twice(w_key), twice(w_value)], axis=1)
    w_joined = jnp.concatenate([w_query, w_key, w_value], axis=1)

    source = hidden_in.astype(jnp.float32)
    inverse_one = lax.rsqrt(jnp.mean(source * source, axis=-1, keepdims=True) + EPSILON)
    unit_one = source * inverse_one
    normed_one = (unit_one * attn_gain).astype(jnp.bfloat16)
    full_one = lax.all_gather(normed_one, "narrow", axis=0, tiled=True)
    q, k, v = qkv_call(full_one, w_twice, *tables, query_width, 2 * key_width)

    def rows_of(array, c):
        return array[c * r : (c + 1) * r]

    def out_parts(o):
        parts = jnp.dot(o, w_out, preferred_element_type=jnp.float32).astype(jnp.bfloat16)
        return parts.reshape(narrow, r, width)

    def second_norm(c, summed):
        resid = rows_of(source, c) + summed
        inverse = lax.rsqrt(jnp.mean(resid * resid, axis=-1, keepdims=True) + EPSILON)
        unit = resid * inverse
        return resid, inverse, unit, (unit * mlp_gain).astype(jnp.bfloat16)

    heads_a, lse_a = attend(q, k, v, starts[0], blocks[0], r, kv, group)
    parts_a = out_parts(heads_a)
    summed_a = scatter_narrow(parts_a, narrow)
    q_late, upstream_late, _ = lax.optimization_barrier((q, upstream, parts_a))
    dy_full = gather_line(upstream_late, here, narrow).reshape(narrow, chunks, r, width)
    heads_b, lse_b = attend(q_late, k, v, starts[1], blocks[1], r, kv, group)
    summed_b = scatter_direct(out_parts(heads_b), here, narrow)
    resid_a, inverse_a, unit_a, normed_a = second_norm(0, summed_a)
    full_a = lax.all_gather(normed_a, "narrow", axis=0, tiled=True)
    resid_b, inverse_b, unit_b, normed_b = second_norm(1, summed_b)
    normed_b = after(normed_b, normed_a)
    full_b = lax.all_gather(normed_b, "narrow", axis=0, tiled=True)
    dy_a, dy_b = (dy_full[:, c].reshape(narrow * r, width) for c in range(chunks))

    def mlp_back(dg, du):
        return (dot_nt(dg, w_gate) + dot_nt(du, w_up)).astype(jnp.bfloat16).reshape(narrow, r, width)

    def second_back(c, grad, unit, inverse):
        scaled = grad * mlp_gain
        back = rows_of(upstream, c).astype(jnp.float32) + inverse * (
            scaled - unit * jnp.mean(scaled * unit, axis=-1, keepdims=True)
        )
        return back, jnp.sum(grad * unit, axis=0)

    m_a, dg_a, du_a = mlp_call(full_a, dy_a, w_gate, w_up, w_down)
    parts_a = mlp_back(dg_a, du_a)
    grad_a = scatter_narrow(parts_a, narrow)
    full_b = after(full_b, parts_a)
    m_b, dg_b, du_b = mlp_call(full_b, dy_b, w_gate, w_up, w_down)
    parts_b = mlp_back(dg_b, du_b)
    grad_b = scatter_direct(parts_b, here, narrow)
    back_a, gain_two_a = second_back(0, grad_a, unit_a, inverse_a)
    back_b, gain_two_b = second_back(1, grad_b, unit_b, inverse_b)
    low_a, low_b = back_a.astype(jnp.bfloat16), back_b.astype(jnp.bfloat16)
    back_full_a = lax.all_gather(low_a, "narrow", axis=0, tiled=True)
    back_full_b = lax.all_gather(after(low_b, low_a), "narrow", axis=0, tiled=True)

    m_a, m_b, dg_a, dg_b, du_a, du_b, _ = lax.optimization_barrier((m_a, m_b, dg_a, dg_b, du_a, du_b, parts_b))
    high = list(range(1, wide.bit_length() - 1))
    swap = high[::-1]
    gate_sum, up_sum = wide_grads(
        [full_a, full_b], [[dg_a, dg_b], [du_a, du_b]], [high, swap], wide_here, wide
    )
    (down_sum,) = wide_grads([dy_a, dy_b], [[m_a, m_b]], [high], wide_here, wide)

    def layer_rows(m, resid):
        parts = jnp.dot(m, w_down, preferred_element_type=jnp.float32).astype(jnp.bfloat16)
        return (resid + scatter_direct(parts.reshape(narrow, r, width), here, narrow)).astype(jnp.bfloat16)

    layer_out = jnp.concatenate([layer_rows(m_a, resid_a), layer_rows(m_b, resid_b)], axis=0)

    heads_grad_a = dot_nt(back_full_a, w_out).astype(jnp.bfloat16)
    carried = attend_back(
        q, k, v, starts[0], heads_grad_a, heads_a, lse_a, None, None, blocks[0], r, kv, group
    )
    back_full_b = after(back_full_b, carried[0])
    heads_grad_b = dot_nt(back_full_b, w_out).astype(jnp.bfloat16)
    joined_grad = attend_back(
        q, k, v, starts[1], heads_grad_b, heads_b, lse_b, carried, tables, blocks[1], r, kv, group
    )
    parts = dot_nt(joined_grad, w_joined).astype(jnp.bfloat16)
    normed_one_grad = scatter_narrow(parts, narrow)
    parts = after(parts, joined_grad)
    gain_one = jnp.sum(parts.astype(jnp.float32) * full_one.astype(jnp.float32), axis=0) / attn_gain
    gains = sum_all(jnp.stack([gain_one, gain_two_a + gain_two_b]), wide, narrow)
    joined_late = after(joined_grad, parts)
    (joined_sum,) = wide_grads([full_one], [[joined_late]], [high], wide_here, wide)
    (out_sum,) = wide_grads([back_full_a, back_full_b], [[heads_a, heads_b]], [swap], wide_here, wide)
    scaled_one = normed_one_grad * attn_gain
    resid_grad = jnp.concatenate([back_a, back_b], axis=0)
    input_grad = resid_grad + inverse_one * (
        scaled_one - unit_one * jnp.mean(scaled_one * unit_one, axis=-1, keepdims=True)
    )
    return (
        layer_out,
        input_grad,
        gains[0],
        gains[1],
        joined_sum[:, :query_width],
        joined_sum[:, query_width : query_width + key_width],
        joined_sum[:, query_width + key_width :],
        out_sum.T,
        gate_sum,
        up_sum,
        down_sum.T,
    )


def solution(mesh):
    in_specs = (
        P(("wide", "narrow"), None),
        P(),
        P(),
        P(None, "narrow"),
        P(None, "narrow"),
        P(None, "narrow"),
        P("narrow", None),
        P(None, "narrow"),
        P(None, "narrow"),
        P("narrow", None),
        P(("wide", "narrow"), None),
        P("wide", None),
    )
    out_specs = (
        P(("wide", "narrow"), None),
        P(("wide", "narrow"), None),
        P(),
        P(),
        P("wide", "narrow"),
        P("wide", "narrow"),
        P("wide", "narrow"),
        P("narrow", "wide"),
        P("wide", "narrow"),
        P("wide", "narrow"),
        P("narrow", "wide"),
    )
    return jax.shard_map(
        on_device, mesh=mesh, in_specs=in_specs, out_specs=out_specs, check_vma=False
    )
```

time: 1310 us -> 786 us (0.60)
  waiting for transfers between devices: 834 us -> 378 us
  matrix products: 252 us -> 66.6 us
  Pallas kernels: 0 us -> 164 us
  blocking collectives: 46.3 us -> 0 us
  starting transfers between devices: 0.61 us -> 41.5 us
  other arithmetic: 80.9 us -> 57.5 us
    reduce_scatter x11 -> x3, waiting for transfers between devices: 583 us -> 0.01 us  [scatter_narrow(): lax.psum_scatter(parts.reshape(-1, parts.shape[-1]), 'narrow', scatter_di...]
    ppermute x0 -> x38, waiting for transfers between devices: none -> 228 us  [the longest x12 115 us: scatter_direct(): lax.ppermute(block(index ^ k), 'narrow', [(i, i ^ k) for i in range(size)])]
    dot_general x29 -> x11, matrix products: 252 us -> 66.6 us  [the longest x7 51 us: dot_nt(): lax.dot_general(a, b, (((1,), (1,)), ((), ())), preferred_element_type=jn...]
    pallas_call x0 -> x15, Pallas kernels: none -> 164 us  [the longest x8 75.2 us: grad_call(): pl.pallas_call(functools.partial(grad_body, nl, nr, bool(recvs)), grid_sp...]
    all_gather x4 -> x5, waiting for transfers between devices: 250 us -> 149 us  [the longest x1 69 us: on_device(): full_one = lax.all_gather(normed_one, 'narrow', axis=0, tiled=True)]
    psum x1 -> x0, blocking collectives: 46.3 us -> none  [on_device(): lax.psum((attn_gain_part, mlp_gain_part), ('wide', 'narrow'))]
    ppermute x0 -> x38, starting transfers between devices: none -> 41 us  [the longest x12 13.9 us: scatter_direct(): lax.ppermute(block(index ^ k), 'narrow', [(i, i ^ k) for i in range(size)])]
    dynamic_update_slice x4 -> x1, local copies, waits for them, and re-layouts: 41.5 us -> 1.34 us  [gather_line(): full = lax.dynamic_update_slice_in_dim(full, block, index * rows, 0)]
  transfers between devices with their start and end apart: 15 -> 46, of which waited for: 13 -> 18; matrix products, arithmetic and copies ran while one was open for 21% -> 20% of each run, Pallas kernels for 0% -> 19%
where the time goes in v1:
time: 786 us; the launch traced here: 776 us
  waiting for transfers between devices  378 us (48%)
  Pallas kernels  164 us (21%)
  matrix products  66.6 us (8%)
  other arithmetic  57.5 us (7%)
  local copies, waits for them, and re-layouts  52.4 us (7%)
  starting transfers between devices  41.5 us (5%)
  between operations  15.2 us (2%)
    ppermute x12, waiting for transfers between devices, scatter_direct(): lax.ppermute(block(index ^ k), 'narrow', [(i, i ^ k) for i in range(size)])  115 us
    pallas_call x8, Pallas kernels, grad_call(): pl.pallas_call(functools.partial(grad_body, nl, nr, bool(recvs)), grid_sp...  75.2 us
    ppermute x3, waiting for transfers between devices, gather_line(): lax.ppermute(b, 'narrow', [(i, i - 1) for i in range(1, size - step + 1)])  74.9 us
    all_gather x1, waiting for transfers between devices, on_device(): full_one = lax.all_gather(normed_one, 'narrow', axis=0, tiled=True)  69 us
    dot_general x7, matrix products, dot_nt(): lax.dot_general(a, b, (((1,), (1,)), ((), ())), preferred_element_type=jn...  51 us
    pallas_call x2, Pallas kernels, mlp_call(): pl.pallas_call(mlp_body, grid=(f // bf,), in_specs=[res, res, col, col, p...  41 us
    all_gather x1, waiting for transfers between devices, on_device(): full_a = lax.all_gather(normed_a, 'narrow', axis=0, tiled=True)  28.1 us
    all_gather x1, waiting for transfers between devices, on_device(): lax.all_gather(after(low_b, low_a), 'narrow', axis=0, tiled=True)  27.2 us
  transfers between devices with their start and end apart: 46, of which 18 were waited for; matrix products, arithmetic and copies ran while one was open for 20% of the time, Pallas kernels for 19%

profile of v1, /device:TPU:0, one launch (start us, length us, event | category | flops | bytes accessed | tf_op | source)
XLA Modules:
  0.0 775.7 jit_solution(7390156528181681679)
XLA Ops:
  14.7 8.2 %concatenate.18.w_ref = bf16[2048,1024]{1,0:T(8,128)(2,1)} concatenate(bf16[2048,512]{1,0:T(8,128)(2,1)} %param.15, bf16[2048,64]{1,0:T(8,128)(2,1)} %get-tuple-element.132, bf16[2048,128]{1,0:T(8,128)(2,1)S(1)} %copy-done.13, bf16[2048,64]{1,0:T(8,128)(2,1)} %get-tuple-element.133, bf16[2048,64]{1,0:T(8,128)(2,1)} %get-tuple-element.117, bf16[2048,128]{1,0:T(8,128)(2,1)S(1)} %copy-done.11, ...), dimensions={1} | concatenate | bytes 8388608 | tf_op jit(solution)/shard_map/concatenate | solution.py:428
  26.6 69.0 %all-gather.6.cloned.1.call-done.x_ref.refs_0_ = bf16[1024,2048]{1,0:T(8,128)(2,1)} async-done(((bf16[256,2048]{1,0:T(8,128)(2,1)}), bf16[1024,2048]{1,0:T(8,128)(2,1)}) %all-gather.6.cloned.1.call-update) | async-done | bytes 4194320 | tf_op jit(solution)/shard_map/all_gather | solution.py:435
  95.6 9.0 %qkv.1 = (bf16[1024,512]{1,0:T(8,128)(2,1)}, bf16[1024,256]{1,0:T(8,128)(2,1)}, bf16[1024,256]{1,0:T(8,128)(2,1)}) custom-call(bf16[1024,2048]{1,0:T(8,128)(2,1)} %all-gather.6.cloned.1.call-done.x_ref.refs_0_, bf16[2048,1024]{1,0:T(8,128)(2,1)} %concatenate.18.w_ref, f32[1024,128]{1,0:T(8,128)} %get-tuple-element.134.cos_ref.refs_10_, ...), custom_call_target="tpu_custom_call" | custom-call | flops 4294967296 | bytes 10485760 | tf_op jit(solution)/shard_map/qkv/pallas_call | solution.py:57
  104.7 7.2 attend.2
  111.8 3.6 convolution_convert_fusion.4
  117.5 6.0 collective-permute-start
  123.5 7.9 %attend.3 = (bf16[512,512]{1,0:T(8,128)(2,1)}, f32[2,4,512]{2,1,0:T(4,128)}) custom-call(bf16[1024,512]{1,0:T(8,128)(2,1)} %get-tuple-element.50.q_ref.refs_0_, bf16[1024,256]{1,0:T(8,128)(2,1)} %get-tuple-element.45.k_ref.refs_1_, bf16[1024,256]{1,0:T(8,128)(2,1)} %get-tuple-element.46.v_ref.refs_2_, s32[4,512]{1,0:T(4,128)} %bitcast.185), custom_call_target="tpu_custom_call" | custom-call | flops 1342177280 | bytes 4194304 | tf_op jit(solution)/shard_map/attend/pallas_call | solution.py:127
  131.4 45.0 %collective-permute-done.1 = bf16[256,2048]{1,0:T(8,128)(2,1)} collective-permute-done((bf16[256,2048]{1,0:T(8,128)(2,1)}, bf16[256,2048]{1,0:T(8,128)(2,1)}, u32[]{:S(2)}, u32[]{:S(2)}) %collective-permute-start.1) | collective-permute-done | bytes 1048608 | tf_op jit(solution)/shard_map/ppermute | solution.py:361
  189.9 26.0 %collective-permute-done.2 = bf16[256,2048]{1,0:T(8,128)(2,1)} collective-permute-done((bf16[256,2048]{1,0:T(8,128)(2,1)}, bf16[256,2048]{1,0:T(8,128)(2,1)}, u32[]{:S(2)}, u32[]{:S(2)}) %collective-permute-start.2) | collective-permute-done | bytes 1048608 | tf_op jit(solution)/shard_map/ppermute | solution.py:361
  217.2 7.8 %collective-permute-done.6 = bf16[128,2048]{1,0:T(8,128)(2,1)} collective-permute-done((bf16[128,2048]{1,0:T(8,128)(2,1)}, bf16[128,2048]{1,0:T(8,128)(2,1)}, u32[]{:S(2)}, u32[]{:S(2)}) %collective-permute-start.6) | collective-permute-done | bytes 524320 | tf_op jit(solution)/shard_map/ppermute | solution.py:350
  225.0 20.2 %collective-permute-done.7 = bf16[128,2048]{1,0:T(8,128)(2,1)} collective-permute-done((bf16[128,2048]{1,0:T(8,128)(2,1)}, bf16[128,2048]{1,0:T(8,128)(2,1)}, u32[]{:S(2)}, u32[]{:S(2)}) %collective-permute-start.7) | collective-permute-done | bytes 524320 | tf_op jit(solution)/shard_map/ppermute | solution.py:350
  253.5 3.9 collective-permute-done.3
  264.9 28.1 %all-gather.8.cloned.1.call-done.x_ref.refs_0_ = bf16[512,2048]{1,0:T(8,128)(2,1)} async-done(((bf16[128,2048]{1,0:T(8,128)(2,1)}), bf16[512,2048]{1,0:T(8,128)(2,1)}) %all-gather.8.cloned.1.call-update) | async-done | bytes 2097168 | tf_op jit(solution)/shard_map/all_gather | solution.py:459
  293.0 20.3 %mlp.2 = (bf16[512,2048]{1,0:T(8,128)(2,1)}, bf16[512,2048]{1,0:T(8,128)(2,1)}, bf16[512,2048]{1,0:T(8,128)(2,1)}) custom-call(bf16[512,2048]{1,0:T(8,128)(2,1)} %all-gather.8.cloned.1.call-done.x_ref.refs_0_, bf16[512,2048]{1,0:T(8,128)(2,1)} %bitcast.156, bf16[2048,2048]{1,0:T(8,128)(2,1)} %wg_ref.3, bf16[2048,2048]{1,0:T(8,128)(2,1)} %wu_ref.3, ...), custom_call_target="tpu_custom_call" | custom-call | flops 12884901888 | bytes 35651584 | tf_op jit(solution)/shard_map/mlp/pallas_call | solution.py:258
  313.3 7.8 %fusion.47 = f32[512,2048]{1,0:T(8,128)S(1)} fusion(bf16[512,2048]{1,0:T(8,128)(2,1)} %get-tuple-element.69.refs_2_, bf16[2048,2048]{1,0:T(8,128)(2,1)} %wg_ref.3), kind=kOutput, calls=%fused_computation.137 | convolution fusion | flops 4294967296 | bytes 14680064 | tf_op jit(solution)/shard_map/dot_general | solution.py:21
  321.2 9.4 %add_convert_fusion = bf16[512,2048]{1,0:T(8,128)(2,1)} fusion(f32[512,2048]{1,0:T(8,128)S(1)} %fusion.47, bf16[512,2048]{1,0:T(8,128)(2,1)S(1)} %copy-done.37, bf16[2048,2048]{1,0:T(8,128)(2,1)} %wu_ref.3), kind=kOutput, calls=%fused_computation.4 | convolution fusion | flops 4297064448 | bytes 16777216 | tf_op jit(solution)/shard_map/dot_general | solution.py:21
  330.9 24.7 %all-gather.10.cloned.1.call-done.x_ref.refs_1_ = bf16[512,2048]{1,0:T(8,128)(2,1)} async-done(((bf16[128,2048]{1,0:T(8,128)(2,1)}), bf16[512,2048]{1,0:T(8,128)(2,1)}) %all-gather.10.cloned.1.call-update) | async-done | bytes 2097168 | tf_op jit(solution)/shard_map/all_gather | solution.py:462
  355.5 20.7 %mlp.3 = (bf16[512,2048]{1,0:T(8,128)(2,1)}, bf16[512,2048]{1,0:T(8,128)(2,1)}, bf16[512,2048]{1,0:T(8,128)(2,1)}) custom-call(bf16[512,2048]{1,0:T(8,128)(2,1)} %all-gather.10.cloned.1.call-done.x_ref.refs_1_, bf16[512,2048]{1,0:T(8,128)(2,1)} %bitcast.153, bf16[2048,2048]{1,0:T(8,128)(2,1)} %wg_ref.3, bf16[2048,2048]{1,0:T(8,128)(2,1)} %wu_ref.3, ...), custom_call_target="tpu_custom_call" | custom-call | flops 12884901888 | bytes 35651584 | tf_op jit(solution)/shard_map/mlp/pallas_call | solution.py:258
  376.2 10.8 %fusion.46 = f32[512,2048]{1,0:T(8,128)} fusion(bf16[512,2048]{1,0:T(8,128)(2,1)} %get-tuple-element.70.refs_3_, bf16[2048,2048]{1,0:T(8,128)(2,1)} %wg_ref.3), kind=kOutput, calls=%fused_computation.136 | convolution fusion | flops 4294967296 | bytes 14680064 | tf_op jit(solution)/shard_map/dot_general | solution.py:21
  387.0 9.2 %add_convert_fusion.1 = bf16[512,2048]{1,0:T(8,128)(2,1)S(1)} fusion(f32[512,2048]{1,0:T(8,128)} %fusion.46, bf16[512,2048]{1,0:T(8,128)(2,1)S(1)} %copy-done.38, bf16[2048,2048]{1,0:T(8,128)(2,1)} %wu_ref.3), kind=kOutput, calls=%fused_computation.5 | convolution fusion | flops 4297064448 | bytes 16777216 | tf_op jit(solution)/shard_map/dot_general | solution.py:21
  400.9 4.8 convolution_convert_fusion.2
  410.3 4.8 convolution_convert_fusion.1
  415.1 15.3 %weight_grad.12 = (bf16[4,256,2048]{2,1,0:T(8,128)(2,1)}, bf16[4,256,2048]{2,1,0:T(8,128)(2,1)}) custom-call(s32[4]{0:T(128)} %fusion.32.tiles_ref, bf16[512,2048]{1,0:T(8,128)(2,1)} %all-gather.8.cloned.1.call-done.x_ref.refs_0_, bf16[512,2048]{1,0:T(8,128)(2,1)} %all-gather.10.cloned.1.call-done.x_ref.refs_1_, ...), custom_call_target="tpu_custom_call" | custom-call | flops 8589934592 | bytes 18874368 | tf_op jit(solution)/shard_map/weight_grad/pallas_call | solution.py:298
  432.0 9.4 %weight_grad.14 = bf16[4,256,2048]{2,1,0:T(8,128)(2,1)} custom-call(s32[4]{0:T(128)} %fusion.32.tiles_ref, bf16[512,2048]{1,0:T(8,128)(2,1)} %bitcast.157, bf16[512,2048]{1,0:T(8,128)(2,1)} %bitcast.154, bf16[512,2048]{1,0:T(8,128)(2,1)} %get-tuple-element.58.refs_2_, bf16[512,2048]{1,0:T(8,128)(2,1)} %get-tuple-element.59.refs_3_), custom_call_target="tpu_custom_call" | custom-call | flops 4294967296 | bytes 10485760 | tf_op jit(solution)/shard_map/weight_grad/pallas_call | solution.py:298
  443.1 27.2 %collective-permute-done.16 = bf16[128,2048]{1,0:T(8,128)(2,1)} collective-permute-done((bf16[128,2048]{1,0:T(8,128)(2,1)}, bf16[128,2048]{1,0:T(8,128)(2,1)}, u32[]{:S(2)}, u32[]{:S(2)}) %collective-permute-start.16) | collective-permute-done | bytes 524320 | tf_op jit(solution)/shard_map/ppermute | solution.py:350
  471.2 44.0 %collective-permute-done.10 = bf16[128,2048]{1,0:T(8,128)(2,1)} collective-permute-done((bf16[128,2048]{1,0:T(8,128)(2,1)S(1)}, bf16[128,2048]{1,0:T(8,128)(2,1)}, u32[]{:S(2)}, u32[]{:S(2)}) %collective-permute-start.10) | collective-permute-done | bytes 524320 | tf_op jit(solution)/shard_map/ppermute | solution.py:350
  515.2 4.8 fusion.11
  520.6 15.4 %collective-permute-done.13 = bf16[128,2048]{1,0:T(8,128)(2,1)} collective-permute-done((bf16[128,2048]{1,0:T(8,128)(2,1)}, bf16[128,2048]{1,0:T(8,128)(2,1)}, u32[]{:S(2)}, u32[]{:S(2)}) %collective-permute-start.13) | collective-permute-done | bytes 524320 | tf_op jit(solution)/shard_map/ppermute | solution.py:350
  535.9 4.1 fusion.36
  541.4 10.2 %weight_grad.15 = bf16[4,256,2048]{2,1,0:T(8,128)(2,1)} custom-call(s32[4]{0:T(128)} %fusion.33.tiles_ref, bf16[512,2048]{1,0:T(8,128)(2,1)} %bitcast.158, bf16[512,2048]{1,0:T(8,128)(2,1)} %bitcast.155, bf16[512,2048]{1,0:T(8,128)(2,1)} %get-tuple-element.58.refs_2_, bf16[512,2048]{1,0:T(8,128)(2,1)} %get-tuple-element.59.refs_3_, ...), custom_call_target="tpu_custom_call" | custom-call | flops 4294967296 | bytes 14680064 | tf_op jit(solution)/shard_map/weight_grad/pallas_call | solution.py:298
  551.7 4.8 constant_dynamic-slice_fusion.1
  556.5 3.9 copy.47
  561.9 15.7 %weight_grad.13 = (bf16[4,256,2048]{2,1,0:T(8,128)(2,1)}, bf16[4,256,2048]{2,1,0:T(8,128)(2,1)}) custom-call(s32[4]{0:T(128)} %fusion.33.tiles_ref, bf16[512,2048]{1,0:T(8,128)(2,1)} %all-gather.8.cloned.1.call-done.x_ref.refs_0_, bf16[512,2048]{1,0:T(8,128)(2,1)} %all-gather.10.cloned.1.call-done.x_ref.refs_1_, ...), custom_call_target="tpu_custom_call" | custom-call | flops 8589934592 | bytes 27262976 | tf_op jit(solution)/shard_map/weight_grad/pallas_call | solution.py:298
  585.5 4.3 copy.51
  589.8 3.7 convolution_convert_fusion.6.refs_4_
  593.5 10.5 %attend_back.2 = (f32[512,512]{1,0:T(8,128)}, f32[1024,256]{1,0:T(8,128)}, f32[1024,256]{1,0:T(8,128)}) custom-call(bf16[1024,512]{1,0:T(8,128)(2,1)} %get-tuple-element.50.q_ref.refs_0_, bf16[1024,256]{1,0:T(8,128)(2,1)} %get-tuple-element.45.k_ref.refs_1_, bf16[1024,256]{1,0:T(8,128)(2,1)} %get-tuple-element.46.v_ref.refs_2_, s32[4,512]{1,0:T(4,128)} %bitcast.184, ...), custom_call_target="tpu_custom_call" | custom-call | flops 2684354560 | bytes 8388608 | tf_op jit(solution)/shard_map/attend_back/pallas_call | solution.py:228
  604.0 27.2 %all-gather.12.cloned.1.call-done.refs_1_ = bf16[512,2048]{1,0:T(8,128)(2,1)} async-done(((bf16[128,2048]{1,0:T(8,128)(2,1)}), bf16[512,2048]{1,0:T(8,128)(2,1)}) %all-gather.12.cloned.1.call-update) | async-done | bytes 2097168 | tf_op jit(solution)/shard_map/all_gather | solution.py:486
  631.2 3.7 convolution_convert_fusion.5.refs_4_
  634.9 13.5 %attend_back.3.refs_1_ = bf16[1024,768]{1,0:T(8,128)(2,1)} custom-call(bf16[1024,512]{1,0:T(8,128)(2,1)} %get-tuple-element.50.q_ref.refs_0_, bf16[1024,256]{1,0:T(8,128)(2,1)} %get-tuple-element.45.k_ref.refs_1_, bf16[1024,256]{1,0:T(8,128)(2,1)} %get-tuple-element.46.v_ref.refs_2_, s32[4,512]{1,0:T(4,128)} %bitcast.186, ...), custom_call_target="tpu_custom_call" | custom-call | flops 3355443200 | bytes 8388608 | tf_op jit(solution)/shard_map/attend_back/pallas_call | solution.py:228
  648.4 6.5 convolution_convert_fusion
  673.6 5.5 weight_grad.10
  680.3 6.3 weight_grad.8
  686.6 8.5 %collective-permute-done.19 = f32[2,2048]{1,0:T(2,128)S(1)} collective-permute-done((f32[2,2048]{1,0:T(2,128)S(1)}, f32[2,2048]{1,0:T(2,128)S(1)}, u32[]{:S(2)}, u32[]{:S(2)}) %collective-permute-start.19) | collective-permute-done | bytes 16416 | tf_op jit(solution)/shard_map/ppermute | solution.py:406
  699.7 7.2 collective-permute-done.20
  712.6 5.8 weight_grad.11
  722.2 6.9 weight_grad.9
  737.8 14.2 %collective-permute-done.24 = bf16[2,256,768]{2,1,0:T(8,128)(2,1)} collective-permute-done((bf16[2,256,768]{2,1,0:T(8,128)(2,1)}, bf16[2,256,768]{2,1,0:T(8,128)(2,1)}, u32[]{:S(2)}, u32[]{:S(2)}) %collective-permute-start.24) | collective-permute-done | bytes 786464 | tf_op jit(solution)/shard_map/ppermute | solution.py:396
  757.0 4.8 collective-permute-done.25
  (240 shorter events, 122.7 us)
Async XLA Ops:
  7.2 104.7 %copy-start = (bf16[512,2048]{1,0:T(8,128)(2,1)S(1)}, bf16[512,2048]{1,0:T(8,128)(2,1)}, u32[]{:S(2)}) copy-start(bf16[512,2048]{1,0:T(8,128)(2,1)} %param.18) | copy-start | bytes 6291460
  7.2 88.4 %all-gather.6.cloned.1.call-start = ((), (), s32[]{:S(2)}) async-start(), calls=%async_computation.3 | async-start | bytes 5242880 | tf_op jit(solution)/shard_map/all_gather | solution.py:435
  12.0 233.2 %reduce-scatter.4.cloned.1.call-start = ((), (), s32[]{:S(2)}) async-start(), calls=%async_computation.4 | async-start | bytes 2621440 | tf_op jit(solution)/shard_map/reduce_scatter | solution.py:373
  115.5 177.5 %all-gather.8.cloned.1.call-start = ((), (), s32[]{:S(2)}) async-start(), calls=%async_computation.5 | async-start | bytes 2621440 | tf_op jit(solution)/shard_map/all_gather | solution.py:459
  115.5 60.8 %collective-permute-start.1 = (bf16[256,2048]{1,0:T(8,128)(2,1)}, bf16[256,2048]{1,0:T(8,128)(2,1)}, u32[]{:S(2)}, u32[]{:S(2)}) collective-permute-start(bf16[256,2048]{1,0:T(8,128)(2,1)} %param.22), channel_id=1, source_target_pairs={{1,0},{2,1},{3,2},{5,4},{6,5},{7,6},{9,8},{10,9},{11,10},{13,12},{... | collective-permute-start | bytes 3145736 | tf_op jit(solution)/shard_map/ppermute | solution.py:361
  117.5 70.7 %collective-permute-start = (bf16[256,2048]{1,0:T(8,128)(2,1)}, bf16[256,2048]{1,0:T(8,128)(2,1)}, u32[]{:S(2)}, u32[]{:S(2)}) collective-permute-start(bf16[256,2048]{1,0:T(8,128)(2,1)} %param.22), channel_id=1, source_target_pairs={{0,1},{1,2},{2,3},{4,5},{5,6},{6,7},{8,9},{9,10},{10,11},{12,13},{... | collective-permute-start | bytes 3145736 | tf_op jit(solution)/shard_map/ppermute | solution.py:360
  176.4 39.5 %collective-permute-start.2 = (bf16[256,2048]{1,0:T(8,128)(2,1)}, bf16[256,2048]{1,0:T(8,128)(2,1)}, u32[]{:S(2)}, u32[]{:S(2)}) collective-permute-start(bf16[256,2048]{1,0:T(8,128)(2,1)} %collective-permute-done.1), channel_id=1, source_target_pairs={{1,0},{2,1},{5,4},{6,5},{9,8},{10,9},{13,12},{14,13},{17,16},{18,1... | collective-permute-start | bytes 3145736 | tf_op jit(solution)/shard_map/ppermute | solution.py:361
  182.4 42.5 %collective-permute-start.6 = (bf16[128,2048]{1,0:T(8,128)(2,1)}, bf16[128,2048]{1,0:T(8,128)(2,1)}, u32[]{:S(2)}, u32[]{:S(2)}) collective-permute-start(bf16[128,2048]{1,0:T(8,128)(2,1)} %get-tuple-element.105), channel_id=1, source_target_pairs={{0,1},{1,0},{2,3},{3,2},{4,5},{5,4},{6,7},{7,6},{8,9},{9,8},{10,11... | collective-permute-start | bytes 1572872 | tf_op jit(solution)/shard_map/ppermute | solution.py:350
  185.1 39.9 %collective-permute-start.8 = (bf16[128,2048]{1,0:T(8,128)(2,1)}, bf16[128,2048]{1,0:T(8,128)(2,1)}, u32[]{:S(2)}, u32[]{:S(2)}) collective-permute-start(bf16[128,2048]{1,0:T(8,128)(2,1)} %get-tuple-element.106), channel_id=1, source_target_pairs={{0,3},{1,2},{2,1},{3,0},{4,7},{5,6},{6,5},{7,4},{8,11},{9,10},{10,... | collective-permute-start | bytes 1572872 | tf_op jit(solution)/shard_map/ppermute | solution.py:350
  186.5 58.7 %collective-permute-start.7 = (bf16[128,2048]{1,0:T(8,128)(2,1)}, bf16[128,2048]{1,0:T(8,128)(2,1)}, u32[]{:S(2)}, u32[]{:S(2)}) collective-permute-start(bf16[128,2048]{1,0:T(8,128)(2,1)} %get-tuple-element.107), channel_id=1, source_target_pairs={{0,2},{1,3},{2,0},{3,1},{4,6},{5,7},{6,4},{7,5},{8,10},{9,11},{10,... | collective-permute-start | bytes 1572872 | tf_op jit(solution)/shard_map/ppermute | solution.py:350
  188.1 60.9 %copy-start.33 = (f32[2048]{0:T(1024)S(1)}, f32[2048]{0:T(1024)}, u32[]{:S(2)}) copy-start(f32[2048]{0:T(1024)} %param.14) | copy-start | bytes 24580
  188.1 64.6 %collective-permute-start.4 = (bf16[256,2048]{1,0:T(8,128)(2,1)}, bf16[256,2048]{1,0:T(8,128)(2,1)}, u32[]{:S(2)}, u32[]{:S(2)}) collective-permute-start(bf16[256,2048]{1,0:T(8,128)(2,1)} %collective-permute-done), channel_id=1, source_target_pairs={{1,2},{2,3},{5,6},{6,7},{9,10},{10,11},{13,14},{14,15},{17,18},{18... | collective-permute-start | bytes 3145736 | tf_op jit(solution)/shard_map/ppermute | solution.py:360
  215.9 41.5 %collective-permute-start.3 = (bf16[256,2048]{1,0:T(8,128)(2,1)}, bf16[256,2048]{1,0:T(8,128)(2,1)}, u32[]{:S(2)}, u32[]{:S(2)}) collective-permute-start(bf16[256,2048]{1,0:T(8,128)(2,1)} %collective-permute-done.2), channel_id=1, source_target_pairs={{1,0},{5,4},{9,8},{13,12},{17,16},{21,20},{25,24},{29,28}} | collective-permute-start | bytes 3145736 | tf_op jit(solution)/shard_map/ppermute | solution.py:361
  250.3 105.2 %all-gather.10.cloned.1.call-start = ((), (), s32[]{:S(2)}) async-start(), calls=%async_computation.6 | async-start | bytes 2621440 | tf_op jit(solution)/shard_map/all_gather | solution.py:462
  252.8 7.9 %collective-permute-start.5 = (bf16[256,2048]{1,0:T(8,128)(2,1)}, bf16[256,2048]{1,0:T(8,128)(2,1)S(1)}, u32[]{:S(2)}, u32[]{:S(2)}) collective-permute-start(bf16[256,2048]{1,0:T(8,128)(2,1)} %collective-permute-done.4), channel_id=1, source_target_pairs={{2,3},{6,7},{10,11},{14,15},{18,19},{22,23},{26,27},{30,31}} | collective-permute-start | bytes 3145736 | tf_op jit(solution)/shard_map/ppermute | solution.py:360
  264.8 250.4 %reduce-scatter.6.cloned.1.call-start = ((), (), s32[]{:S(2)}) async-start(), calls=%async_computation.7 | async-start | bytes 2621440 | tf_op jit(solution)/shard_map/reduce_scatter | solution.py:373
  330.7 259.2 %all-gather.14.cloned.1.call-start = ((), (), s32[]{:S(2)}) async-start(), calls=%async_computation.9 | async-start | bytes 2621440 | tf_op jit(solution)/shard_map/all_gather | solution.py:485
  397.4 33.0 %collective-permute-start.15 = (bf16[128,2048]{1,0:T(8,128)(2,1)}, bf16[128,2048]{1,0:T(8,128)(2,1)S(1)}, u32[]{:S(2)}, u32[]{:S(2)}) collective-permute-start(bf16[128,2048]{1,0:T(8,128)(2,1)} %get-tuple-element.94), channel_id=1, source_target_pairs={{0,1},{1,0},{2,3},{3,2},{4,5},{5,4},{6,7},{7,6},{8,9},{9,8},{10,11... | collective-permute-start | bytes 1572872 | tf_op jit(solution)/shard_map/ppermute | solution.py:350
  397.4 43.9 %collective-permute-start.17 = (bf16[128,2048]{1,0:T(8,128)(2,1)}, bf16[128,2048]{1,0:T(8,128)(2,1)}, u32[]{:S(2)}, u32[]{:S(2)}) collective-permute-start(bf16[128,2048]{1,0:T(8,128)(2,1)} %get-tuple-element.95), channel_id=1, source_target_pairs={{0,3},{1,2},{2,1},{3,0},{4,7},{5,6},{6,5},{7,4},{8,11},{9,10},{10,... | collective-permute-start | bytes 1572872 | tf_op jit(solution)/shard_map/ppermute | solution.py:350
  399.9 70.4 %collective-permute-start.16 = (bf16[128,2048]{1,0:T(8,128)(2,1)}, bf16[128,2048]{1,0:T(8,128)(2,1)}, u32[]{:S(2)}, u32[]{:S(2)}) collective-permute-start(bf16[128,2048]{1,0:T(8,128)(2,1)} %get-tuple-element.96), channel_id=1, source_target_pairs={{0,2},{1,3},{2,0},{3,1},{4,6},{5,7},{6,4},{7,5},{8,10},{9,11},{10,... | collective-permute-start | bytes 1572872 | tf_op jit(solution)/shard_map/ppermute | solution.py:350
  407.0 64.2 %collective-permute-start.9 = (bf16[128,2048]{1,0:T(8,128)(2,1)}, bf16[128,2048]{1,0:T(8,128)(2,1)}, u32[]{:S(2)}, u32[]{:S(2)}) collective-permute-start(bf16[128,2048]{1,0:T(8,128)(2,1)} %get-tuple-element.97), channel_id=1, source_target_pairs={{0,1},{1,0},{2,3},{3,2},{4,5},{5,4},{6,7},{7,6},{8,9},{9,8},{10,11... | collective-permute-start | bytes 1572872 | tf_op jit(solution)/shard_map/ppermute | solution.py:350
  407.9 63.3 %collective-permute-start.11 = (bf16[128,2048]{1,0:T(8,128)(2,1)}, bf16[128,2048]{1,0:T(8,128)(2,1)}, u32[]{:S(2)}, u32[]{:S(2)}) collective-permute-start(bf16[128,2048]{1,0:T(8,128)(2,1)} %get-tuple-element.98), channel_id=1, source_target_pairs={{0,3},{1,2},{2,1},{3,0},{4,7},{5,6},{6,5},{7,4},{8,11},{9,10},{10,... | collective-permute-start | bytes 1572872 | tf_op jit(solution)/shard_map/ppermute | solution.py:350
  430.5 84.7 %collective-permute-start.10 = (bf16[128,2048]{1,0:T(8,128)(2,1)S(1)}, bf16[128,2048]{1,0:T(8,128)(2,1)}, u32[]{:S(2)}, u32[]{:S(2)}) collective-permute-start(bf16[128,2048]{1,0:T(8,128)(2,1)S(1)} %copy-done.31), channel_id=1, source_target_pairs={{0,2},{1,3},{2,0},{3,1},{4,6},{5,7},{6,4},{7,5},{8,10},{9,11},{10,... | collective-permute-start | bytes 1572872 | tf_op jit(solution)/shard_map/ppermute | solution.py:350
  441.4 78.6 %collective-permute-start.12 = (bf16[128,2048]{1,0:T(8,128)(2,1)}, bf16[128,2048]{1,0:T(8,128)(2,1)}, u32[]{:S(2)}, u32[]{:S(2)}) collective-permute-start(bf16[128,2048]{1,0:T(8,128)(2,1)} %get-tuple-element.100), channel_id=1, source_target_pairs={{0,1},{1,0},{2,3},{3,2},{4,5},{5,4},{6,7},{7,6},{8,9},{9,8},{10,11... | collective-permute-start | bytes 1572872 | tf_op jit(solution)/shard_map/ppermute | solution.py:350
  470.2 50.3 %collective-permute-start.14 = (bf16[128,2048]{1,0:T(8,128)(2,1)}, bf16[128,2048]{1,0:T(8,128)(2,1)}, u32[]{:S(2)}, u32[]{:S(2)}) collective-permute-start(bf16[128,2048]{1,0:T(8,128)(2,1)} %get-tuple-element.101), channel_id=1, source_target_pairs={{0,3},{1,2},{2,1},{3,0},{4,7},{5,6},{6,5},{7,4},{8,11},{9,10},{10,... | collective-permute-start | bytes 1572872 | tf_op jit(solution)/shard_map/ppermute | solution.py:350
  471.1 64.8 %collective-permute-start.13 = (bf16[128,2048]{1,0:T(8,128)(2,1)}, bf16[128,2048]{1,0:T(8,128)(2,1)}, u32[]{:S(2)}, u32[]{:S(2)}) collective-permute-start(bf16[128,2048]{1,0:T(8,128)(2,1)} %get-tuple-element.102), channel_id=1, source_target_pairs={{0,2},{1,3},{2,0},{3,1},{4,6},{5,7},{6,4},{7,5},{8,10},{9,11},{10,... | collective-permute-start | bytes 1572872 | tf_op jit(solution)/shard_map/ppermute | solution.py:350
  471.1 70.3 %collective-permute-start.35 = (bf16[4,256,2048]{2,1,0:T(8,128)(2,1)}, bf16[4,256,2048]{2,1,0:T(8,128)(2,1)}, u32[]{:S(2)}, u32[]{:S(2)}) collective-permute-start(bf16[4,256,2048]{2,1,0:T(8,128)(2,1)} %weight_grad.14), channel_id=1, source_target_pairs={{0,4},{4,0},{8,12},{12,8},{16,20},{20,16},{24,28},{28,24},{1,5},{5... | collective-permute-start | bytes 12582920 | tf_op jit(solution)/shard_map/ppermute | solution.py:384
  515.2 46.7 %collective-permute-start.29 = (bf16[4,256,2048]{2,1,0:T(8,128)(2,1)}, bf16[4,256,2048]{2,1,0:T(8,128)(2,1)}, u32[]{:S(2)}, u32[]{:S(2)}) collective-permute-start(bf16[4,256,2048]{2,1,0:T(8,128)(2,1)} %get-tuple-element.73), channel_id=1, source_target_pairs={{0,4},{4,0},{8,12},{12,8},{16,20},{20,16},{24,28},{28,24},{1,5},{5... | collective-permute-start | bytes 12582920 | tf_op jit(solution)/shard_map/ppermute | solution.py:384
  520.0 41.9 %collective-permute-start.30 = (bf16[4,256,2048]{2,1,0:T(8,128)(2,1)}, bf16[4,256,2048]{2,1,0:T(8,128)(2,1)}, u32[]{:S(2)}, u32[]{:S(2)}) collective-permute-start(bf16[4,256,2048]{2,1,0:T(8,128)(2,1)} %get-tuple-element.74), channel_id=1, source_target_pairs={{0,4},{4,0},{8,12},{12,8},{16,20},{20,16},{24,28},{28,24},{1,5},{5... | collective-permute-start | bytes 12582920 | tf_op jit(solution)/shard_map/ppermute | solution.py:384
  540.0 91.2 %all-gather.12.cloned.1.call-start = ((), (), s32[]{:S(2)}) async-start(), calls=%async_computation.8 | async-start | bytes 2621440 | tf_op jit(solution)/shard_map/all_gather | solution.py:486
  540.8 222.7 %reduce-scatter.8.cloned.1.call-start = ((), (), s32[]{:S(2)}) async-start(), calls=%async_computation.10 | async-start | bytes 5242880 | tf_op jit(solution)/shard_map/reduce_scatter | solution.py:373
  560.4 94.5 %collective-permute-start.36 = (bf16[2,256,2048]{1,2,0:T(8,128)(2,1)}, bf16[2,256,2048]{1,2,0:T(8,128)(2,1)}, u32[]{:S(2)}, u32[]{:S(2)}) collective-permute-start(bf16[2,256,2048]{1,2,0:T(8,128)(2,1)} %bitcast.174), channel_id=1, source_target_pairs={{0,8},{4,12},{8,0},{12,4},{16,24},{20,28},{24,16},{28,20},{1,9},{5... | collective-permute-start | bytes 6291464 | tf_op jit(solution)/shard_map/ppermute | solution.py:396
  581.0 79.5 %collective-permute-start.31 = (bf16[2,256,2048]{2,1,0:T(8,128)(2,1)}, bf16[2,256,2048]{2,1,0:T(8,128)(2,1)}, u32[]{:S(2)}, u32[]{:S(2)}) collective-permute-start(bf16[2,256,2048]{2,1,0:T(8,128)(2,1)} %dynamic-slice_bitcast_fusion.1), channel_id=1, source_target_pairs={{0,8},{4,12},{8,0},{12,4},{16,24},{20,28},{24,16},{28,20},{1,9},{5... | collective-permute-start | bytes 6291464 | tf_op jit(solution)/shard_map/ppermute | solution.py:396
  583.0 81.3 %collective-permute-start.33 = (bf16[2,256,2048]{2,1,0:T(8,128)(2,1)}, bf16[2,256,2048]{2,1,0:T(8,128)(2,1)}, u32[]{:S(2)}, u32[]{:S(2)}) collective-permute-start(bf16[2,256,2048]{2,1,0:T(8,128)(2,1)} %dynamic-slice_bitcast_fusion), channel_id=1, source_target_pairs={{0,16},{4,20},{8,24},{12,28},{16,0},{20,4},{24,8},{28,12},{1,17},{... | collective-permute-start | bytes 6291464 | tf_op jit(solution)/shard_map/ppermute | solution.py:396
  659.0 36.1 %collective-permute-start.37 = (bf16[256,2048]{0,1:T(8,128)(2,1)}, bf16[256,2048]{0,1:T(8,128)(2,1)}, u32[]{:S(2)}, u32[]{:S(2)}) collective-permute-start(bf16[256,2048]{0,1:T(8,128)(2,1)} %fusion.14), channel_id=1, source_target_pairs={{0,16},{4,20},{8,24},{12,28},{16,0},{20,4},{24,8},{28,12},{1,17},{... | collective-permute-start | bytes 3145736 | tf_op jit(solution)/shard_map/ppermute | solution.py:396
  663.2 43.8 %collective-permute-start.32 = (bf16[256,2048]{1,0:T(8,128)(2,1)S(1)}, bf16[256,2048]{1,0:T(8,128)(2,1)}, u32[]{:S(2)}, u32[]{:S(2)}) collective-permute-start(bf16[256,2048]{1,0:T(8,128)(2,1)S(1)} %fusion.12), channel_id=1, source_target_pairs={{0,16},{4,20},{8,24},{12,28},{16,0},{20,4},{24,8},{28,12},{1,17},{... | collective-permute-start | bytes 3145736 | tf_op jit(solution)/shard_map/ppermute | solution.py:396
  670.0 62.7 %collective-permute-start.34 = (bf16[256,2048]{1,0:T(8,128)(2,1)}, bf16[256,2048]{1,0:T(8,128)(2,1)}, u32[]{:S(2)}, u32[]{:S(2)}) collective-permute-start(bf16[256,2048]{1,0:T(8,128)(2,1)} %fusion.13), channel_id=1, source_target_pairs={{0,8},{4,12},{8,0},{12,4},{16,24},{20,28},{24,16},{28,20},{1,9},{5... | collective-permute-start | bytes 3145736 | tf_op jit(solution)/shard_map/ppermute | solution.py:396
  673.5 6.1 collective-permute-start.18
  679.1 33.5 %collective-permute-start.26 = (bf16[4,256,512]{2,1,0:T(8,128)(2,1)}, bf16[4,256,512]{2,1,0:T(8,128)(2,1)}, u32[]{:S(2)}, u32[]{:S(2)}) collective-permute-start(bf16[4,256,512]{2,1,0:T(8,128)(2,1)} %weight_grad.10), channel_id=1, source_target_pairs={{0,4},{4,0},{8,12},{12,8},{16,20},{20,16},{24,28},{28,24},{1,5},{5... | collective-permute-start | bytes 3145736 | tf_op jit(solution)/shard_map/ppermute | solution.py:384
  679.6 15.5 %collective-permute-start.19 = (f32[2,2048]{1,0:T(2,128)S(1)}, f32[2,2048]{1,0:T(2,128)S(1)}, u32[]{:S(2)}, u32[]{:S(2)}) collective-permute-start(f32[2,2048]{1,0:T(2,128)S(1)} %fusion.35), channel_id=1, source_target_pairs={{0,8},{4,12},{8,0},{12,4},{16,24},{20,28},{24,16},{28,20},{1,9},{5... | collective-permute-start | bytes 49160 | tf_op jit(solution)/shard_map/ppermute | solution.py:406
  695.1 27.1 %collective-permute-start.23 = (bf16[4,256,768]{2,1,0:T(8,128)(2,1)}, bf16[4,256,768]{2,1,0:T(8,128)(2,1)}, u32[]{:S(2)}, u32[]{:S(2)}) collective-permute-start(bf16[4,256,768]{2,1,0:T(8,128)(2,1)} %weight_grad.8), channel_id=1, source_target_pairs={{0,4},{4,0},{8,12},{12,8},{16,20},{20,16},{24,28},{28,24},{1,5},{5... | collective-permute-start | bytes 4718600 | tf_op jit(solution)/shard_map/ppermute | solution.py:384
  695.2 11.8 %collective-permute-start.20 = (f32[2,2048]{1,0:T(2,128)S(1)}, f32[2,2048]{1,0:T(2,128)S(1)}, u32[]{:S(2)}, u32[]{:S(2)}) collective-permute-start(f32[2,2048]{1,0:T(2,128)S(1)} %fusion.69), channel_id=1, source_target_pairs={{0,16},{4,20},{8,24},{12,28},{16,0},{20,4},{24,8},{28,12},{1,17},{... | collective-permute-start | bytes 49160 | tf_op jit(solution)/shard_map/ppermute | solution.py:406
  706.9 5.6 collective-permute-start.21
  712.6 23.1 %collective-permute-start.22 = (f32[2,2048]{1,0:T(2,128)S(1)}, f32[2,2048]{1,0:T(2,128)S(1)}, u32[]{:S(2)}, u32[]{:S(2)}) collective-permute-start(f32[2,2048]{1,0:T(2,128)S(1)} %add.302), channel_id=1, source_target_pairs={{0,2},{1,3},{2,0},{3,1},{4,6},{5,7},{6,4},{7,5},{8,10},{9,11},{10,... | collective-permute-start | bytes 49160 | tf_op jit(solution)/shard_map/ppermute | solution.py:406
  720.7 15.1 %collective-permute-start.27 = (bf16[2,256,512]{1,2,0:T(8,128)(2,1)}, bf16[2,256,512]{1,2,0:T(8,128)(2,1)}, u32[]{:S(2)}, u32[]{:S(2)}) collective-permute-start(bf16[2,256,512]{1,2,0:T(8,128)(2,1)} %bitcast.175), channel_id=1, source_target_pairs={{0,16},{4,20},{8,24},{12,28},{16,0},{20,4},{24,8},{28,12},{1,17},{... | collective-permute-start | bytes 1572872 | tf_op jit(solution)/shard_map/ppermute | solution.py:396
  731.3 20.8 %collective-permute-start.24 = (bf16[2,256,768]{2,1,0:T(8,128)(2,1)}, bf16[2,256,768]{2,1,0:T(8,128)(2,1)}, u32[]{:S(2)}, u32[]{:S(2)}) collective-permute-start(bf16[2,256,768]{2,1,0:T(8,128)(2,1)} %dynamic-slice_bitcast_fusion.2), channel_id=1, source_target_pairs={{0,8},{4,12},{8,0},{12,4},{16,24},{20,28},{24,16},{28,20},{1,9},{5... | collective-permute-start | bytes 2359304 | tf_op jit(solution)/shard_map/ppermute | solution.py:396
  737.2 19.0 %collective-permute-start.28 = (bf16[256,512]{0,1:T(8,128)(2,1)S(1)}, bf16[256,512]{0,1:T(8,128)(2,1)S(1)}, u32[]{:S(2)}, u32[]{:S(2)}) collective-permute-start(bf16[256,512]{0,1:T(8,128)(2,1)S(1)} %fusion.29), channel_id=1, source_target_pairs={{0,8},{4,12},{8,0},{12,4},{16,24},{20,28},{24,16},{28,20},{1,9},{5... | collective-permute-start | bytes 786440 | tf_op jit(solution)/shard_map/ppermute | solution.py:396
  753.4 8.4 %collective-permute-start.25 = (bf16[256,768]{1,0:T(8,128)(2,1)S(1)}, bf16[256,768]{1,0:T(8,128)(2,1)S(1)}, u32[]{:S(2)}, u32[]{:S(2)}) collective-permute-start(bf16[256,768]{1,0:T(8,128)(2,1)S(1)} %fusion.28), channel_id=1, source_target_pairs={{0,16},{4,20},{8,24},{12,28},{16,0},{20,4},{24,8},{28,12},{1,17},{... | collective-permute-start | bytes 1179656 | tf_op jit(solution)/shard_map/ppermute | solution.py:396
  (39 other events, 305.0 us)
Sparse Core Ops, SparseCore 0:
  12.1 83.4 all-gather.5
  115.6 61.8 reduce-scatter.3
  250.4 42.5 all-gather.7
  294.5 60.9 all-gather.9
  357.8 42.5 reduce-scatter.5
  540.1 44.8 all-gather.13
  586.6 44.6 all-gather.11
  655.0 76.1 reduce-scatter.7

commit v2 on v1

--- a/solution.py
+++ b/solution.py
@@ -11,6 +11,7 @@
 THETA_BASE = 500000.0
 LANES = 128
 VMEM_LIMIT = 56 * 1024 * 1024
+COST = pl.CostEstimate(flops=1, bytes_accessed=1, transcendentals=0)
 
 
 def dot_nn(a, b):
@@ -65,9 +66,7 @@
             jax.ShapeDtypeStruct((rows, kw), jnp.bfloat16),
         ],
         compiler_params=pltpu.CompilerParams(vmem_limit_bytes=VMEM_LIMIT),
-        cost_estimate=pl.CostEstimate(
-            flops=2 * rows * d * w.shape[1], bytes_accessed=2 * (x.size + w.size) + 4 * rows * qw, transcendentals=0
-        ),
+        cost_estimate=COST,
         name="qkv",
     )(x, w, cosine, sine)
 
@@ -123,7 +122,6 @@
 
 def attend(q, k, v, start, blocks, r, kv, group):
     nb = len(blocks)
-    area = sum(block_extent(b, r, q.shape[0]) for b in blocks) * r * kv * group
     return pl.pallas_call(
         functools.partial(fwd_body, blocks, r, kv, group),
         out_shape=[
@@ -131,7 +129,7 @@
             jax.ShapeDtypeStruct((kv, nb, 4 * r), jnp.float32),
         ],
         compiler_params=pltpu.CompilerParams(vmem_limit_bytes=VMEM_LIMIT),
-        cost_estimate=pl.CostEstimate(flops=area * 512, bytes_accessed=4 << 20, transcendentals=area),
+        cost_estimate=COST,
         name="attend",
     )(q, k, v, start)
 
@@ -213,7 +211,6 @@
     first, last = carried is None, tables is not None
     rows = q.shape[0]
     nb = len(blocks)
-    area = sum(block_extent(b, r, rows) for b in blocks) * r * kv * group
     sums = [
         jax.ShapeDtypeStruct((nb * r, kv * group * HD), jnp.float32),
         jax.ShapeDtypeStruct((rows, kv * LANES), jnp.float32),
@@ -230,14 +227,144 @@
         out_shape=out,
         scratch_shapes=scratch,
         compiler_params=pltpu.CompilerParams(vmem_limit_bytes=VMEM_LIMIT),
-        cost_estimate=pl.CostEstimate(flops=area * 1280, bytes_accessed=8 << 20, transcendentals=area),
+        cost_estimate=COST,
         name="attend_back",
     )(*args)
 
 
+def grad_body(nl, nr, got, tiles_ref, *refs):
+    lefts = refs[:nl]
+    rights = [refs[nl + i * nl : nl + (i + 1) * nl] for i in range(nr)]
+    refs = refs[nl + nl * nr :]
+    recv, outs = (refs[0], refs[1:]) if got else (None, refs)
+    half = pl.num_programs(0) // 2
+    step = pl.program_id(0)
+    turned = [x[...].T for x in lefts]
+    at = 0
+    for right in rights:
+        total = dot_nn(turned[0], right[0][...])
+        for a, b in zip(turned[1:], right[1:]):
+            total += dot_nn(a, b[...])
+        here = slice(at, at + total.shape[1])
+        at += total.shape[1]
+        if not got:
+            outs[0][0, :, here] = total.astype(jnp.bfloat16)
+            continue
+        total = (total + recv[0, :, here].astype(jnp.float32)).astype(jnp.bfloat16)
+
+        @pl.when(step < half)
+        def _():
+            outs[0][0, :, here] = total
+
+        @pl.when(step >= half)
+        def _():
+            outs[1][0, :, here] = total
+
+
+def grad_call(tiles, part, lefts, rights, recv=None):
+    count = tiles.shape[0]
+    half = count // 2
+    nl, nr = len(lefts), len(rights)
+    cols = sum(r[0].shape[1] for r in rights)
+    got = recv is not None
+    shift = half if got else 0
+    in_specs = [pl.BlockSpec((x.shape[0], part), lambda j, t: (0, t[lax.rem(j + shift, count)])) for x in lefts]
+    in_specs += [
+        pl.BlockSpec(x.shape, lambda j, t: (0, 0), pipeline_mode=pl.Buffered(1)) for r in rights for x in r
+    ]
+    if got:
+        in_specs.append(pl.BlockSpec((1, part, cols), lambda j, t: (lax.rem(j + shift, count), 0, 0)))
+        out_specs = [
+            pl.BlockSpec((1, part, cols), lambda j, t: (jnp.minimum(j, half - 1), 0, 0)),
+            pl.BlockSpec((1, part, cols), lambda j, t: (jnp.maximum(j - half, 0), 0, 0)),
+        ]
+        out_shape = [jax.ShapeDtypeStruct((half, part, cols), jnp.bfloat16)] * 2
+    else:
+        out_specs = pl.BlockSpec((1, part, cols), lambda j, t: (j, 0, 0))
+        out_shape = jax.ShapeDtypeStruct((count, part, cols), jnp.bfloat16)
+    return pl.pallas_call(
+        functools.partial(grad_body, nl, nr, got),
+        grid_spec=pltpu.PrefetchScalarGridSpec(
+            num_scalar_prefetch=1, grid=(count,), in_specs=in_specs, out_specs=out_specs
+        ),
+        out_shape=out_shape,
+        compiler_params=pltpu.CompilerParams(vmem_limit_bytes=VMEM_LIMIT),
+        cost_estimate=COST,
+        name="weight_grad",
+    )(tiles, *lefts, *[x for r in rights for x in r], *((recv,) if got else ()))
+
+
+def place(index, part):
+    return pl.ds(pl.multiple_of(index * part, part), part)
+
+
+def out_body(at_ref, x_ref, *refs):
+    pieces, out = refs[:-1], refs[-1]
+    x = jnp.concatenate([x_ref[j] for j in range(x_ref.shape[0])], axis=1)
+    for n, piece in enumerate(pieces):
+        out[:, place(at_ref[n], piece.shape[1])] = dot_nn(x, piece[...])
+
+
+def out_project(at, x, pieces):
+    rows, width = x.shape[1], len(pieces) * pieces[0].shape[1]
+    return pl.pallas_call(
+        out_body,
+        in_specs=[pl.BlockSpec(memory_space=pltpu.SMEM)] + [pl.BlockSpec(memory_space=pltpu.VMEM)] * (1 + len(pieces)),
+        out_specs=pl.BlockSpec(memory_space=pltpu.VMEM),
+        out_shape=jax.ShapeDtypeStruct((rows, width), jnp.float32),
+        compiler_params=pltpu.CompilerParams(vmem_limit_bytes=VMEM_LIMIT),
+        cost_estimate=COST,
+        name="out_project",
+    )(at, x, *pieces)
+
+
+def out_back_body(at_ref, x_ref, *refs):
+    pieces, out = refs[:-1], refs[-1]
+    total = None
+    for n, piece in enumerate(pieces):
+        term = dot_nt(x_ref[:, place(at_ref[n], piece.shape[1])], piece[...])
+        total = term if total is None else total + term
+    total = total.astype(jnp.bfloat16)
+    width = out.shape[2]
+    for j in range(out.shape[0]):
+        out[j] = total[:, j * width : (j + 1) * width]
+
+
+def out_project_back(at, x, pieces, parts):
+    rows, depth = x.shape[0], pieces[0].shape[0]
+    return pl.pallas_call(
+        out_back_body,
+        in_specs=[pl.BlockSpec(memory_space=pltpu.SMEM)] + [pl.BlockSpec(memory_space=pltpu.VMEM)] * (1 + len(pieces)),
+        out_specs=pl.BlockSpec(memory_space=pltpu.VMEM),
+        out_shape=jax.ShapeDtypeStruct((parts, rows, depth // parts), jnp.bfloat16),
+        compiler_params=pltpu.CompilerParams(vmem_limit_bytes=VMEM_LIMIT),
+        cost_estimate=COST,
+        name="out_project_back",
+    )(at, x, *pieces)
+
+
+def in_back_body(at_ref, x_ref, *refs):
+    pieces, out = refs[:-1], refs[-1]
+    x = x_ref[...]
+    for n, piece in enumerate(pieces):
+        out[:, place(at_ref[n], piece.shape[0])] = dot_nt(x, piece[...])
+
+
+def in_project_back(at, x, pieces):
+    rows, width = x.shape[0], len(pieces) * pieces[0].shape[0]
+    return pl.pallas_call(
+        in_back_body,
+        in_specs=[pl.BlockSpec(memory_space=pltpu.SMEM)] + [pl.BlockSpec(memory_space=pltpu.VMEM)] * (1 + len(pieces)),
+        out_specs=pl.BlockSpec(memory_space=pltpu.VMEM),
+        out_shape=jax.ShapeDtypeStruct((rows, width), jnp.float32),
+        compiler_params=pltpu.CompilerParams(vmem_limit_bytes=VMEM_LIMIT),
+        cost_estimate=COST,
+        name="in_project_back",
+    )(at, x, *pieces)
+
+
 def mlp_body(x_ref, dy_ref, wg_ref, wu_ref, wd_ref, m_ref, dg_ref, du_ref):
-    x = x_ref[...]
-    dy = dy_ref[...].reshape(x.shape)
+    x, dy = x_ref[...], dy_ref[...]
     gate = dot_nn(x, wg_ref[...])
     up = dot_nn(x, wu_ref[...])
     dm = dot_nt(dy, wd_ref[...])
@@ -253,62 +380,87 @@
     f = wg.shape[1]
     bf = min(256, f)
     col = pl.BlockSpec((d, bf), lambda i: (0, i))
-    out = pl.BlockSpec((t, bf), lambda i: (0, i))
-    res = pl.BlockSpec((t, d), lambda i: (0, 0))
+    hid = pl.BlockSpec((t, bf), lambda i: (0, i))
+    held = pl.BlockSpec((t, d), lambda i: (0, 0), pipeline_mode=pl.Buffered(1))
     return pl.pallas_call(
         mlp_body,
         grid=(f // bf,),
-        in_specs=[res, res, col, col, pl.BlockSpec((bf, d), lambda i: (i, 0))],
-        out_specs=[out] * 3,
+        in_specs=[held, held, col, col, pl.BlockSpec((bf, d), lambda i: (i, 0))],
+        out_specs=[hid] * 3,
         out_shape=[jax.ShapeDtypeStruct((t, f), jnp.bfloat16)] * 3,
         compiler_params=pltpu.CompilerParams(vmem_limit_bytes=VMEM_LIMIT),
-        cost_estimate=pl.CostEstimate(flops=6 * t * d * f, bytes_accessed=2 * (2 * x.size + 3 * wg.size + 3 * t * f), transcendentals=t * f),
+        cost_estimate=COST,
         name="mlp",
     )(x, dy, wg, wu, wd)
 
 
-def grad_body(nl, nr, got, tiles_ref, *refs):
-    lefts = refs[:nl]
-    rights = [refs[nl + i * nl : nl + (i + 1) * nl] for i in range(nr)]
-    refs = refs[nl + nl * nr :]
-    recvs, outs = (refs[:nr], refs[nr:]) if got else ([None] * nr, refs)
-    turned = [x[...].T for x in lefts]
-    for right, recv, out in zip(rights, recvs, outs):
-        total = dot_nn(turned[0], right[0][...])
-        for a, b in zip(turned[1:], right[1:]):
-            total += dot_nn(a, b[...])
-        if got:
-            total += recv[0].astype(jnp.float32)
-        out[0] = total.astype(jnp.bfloat16)
-
-
-def grad_call(tiles, part, lefts, rights, recvs=()):
-    count = tiles.shape[0]
-    nl, nr = len(lefts), len(rights)
-    outs = [jax.ShapeDtypeStruct((count, part, r[0].shape[1]), jnp.bfloat16) for r in rights]
-    out_specs = [pl.BlockSpec((1, part, r[0].shape[1]), lambda j, t: (j, 0, 0)) for r in rights]
-    in_specs = [pl.BlockSpec((x.shape[0], part), lambda j, t: (0, t[j])) for x in lefts]
-    in_specs += [
-        pl.BlockSpec(x.shape, lambda j, t: (0, 0), pipeline_mode=pl.Buffered(1)) for r in rights for x in r
-    ]
-    if recvs:
-        in_specs += out_specs
-    rows = sum(x.shape[0] for x in lefts)
-    cols = sum(r[0].shape[1] for r in rights)
-    return pl.pallas_call(
-        functools.partial(grad_body, nl, nr, bool(recvs)),
-        grid_spec=pltpu.PrefetchScalarGridSpec(
-            num_scalar_prefetch=1, grid=(count,), in_specs=in_specs, out_specs=out_specs
-        ),
-        out_shape=outs,
-        compiler_params=pltpu.CompilerParams(vmem_limit_bytes=VMEM_LIMIT),
-        cost_estimate=pl.CostEstimate(
-            flops=2 * rows * count * part * cols,
-            bytes_accessed=2 * (rows * (count * part + cols) + count * part * cols * (2 if recvs else 1)),
-            transcendentals=0,
-        ),
-        name="weight_grad",
-    )(tiles, *lefts, *[x for r in rights for x in r], *recvs)
+def mlp_back_body(dg_ref, du_ref, wg_ref, wu_ref, o_ref):
+    o_ref[...] = (dot_nt(dg_ref[...], wg_ref[...]) + dot_nt(du_ref[...], wu_ref[...])).astype(jnp.bfloat16)
+
+
+def mlp_back_call(dg, du, wg, wu):
+    t, f = dg.shape
+    d = wg.shape[0]
+    bn = min(256, d)
+    held = pl.BlockSpec((t, f), lambda i: (0, 0), pipeline_mode=pl.Buffered(1))
+    row = pl.BlockSpec((bn, f), lambda i: (i, 0))
+    return pl.pallas_call(
+        mlp_back_body,
+        grid=(d // bn,),
+        in_specs=[held, held, row, row],
+        out_specs=pl.BlockSpec((t, bn), lambda i: (0, i)),
+        out_shape=jax.ShapeDtypeStruct((t, d), jnp.bfloat16),
+        compiler_params=pltpu.CompilerParams(vmem_limit_bytes=VMEM_LIMIT),
+        cost_estimate=COST,
+        name="mlp_back",
+    )(dg, du, wg, wu)
+
+
+def mat_body(transposed, x_ref, w_ref, o_ref):
+    o_ref[...] = (dot_nt if transposed else dot_nn)(x_ref[...], w_ref[...]).astype(jnp.bfloat16)
+
+
+def mat_call(x, w, transposed):
+    rows, depth = x.shape
+    width = w.shape[0] if transposed else w.shape[1]
+    bn = min(512, width)
+    w_spec = pl.BlockSpec((bn, depth), lambda i: (i, 0)) if transposed else pl.BlockSpec((depth, bn), lambda i: (0, i))
+    return pl.pallas_call(
+        functools.partial(mat_body, transposed),
+        grid=(width // bn,),
+        in_specs=[pl.BlockSpec((rows, depth), lambda i: (0, 0), pipeline_mode=pl.Buffered(1)), w_spec],
+        out_specs=pl.BlockSpec((rows, bn), lambda i: (0, i)),
+        out_shape=jax.ShapeDtypeStruct((rows, width), jnp.bfloat16),
+        compiler_params=pltpu.CompilerParams(vmem_limit_bytes=VMEM_LIMIT),
+        cost_estimate=COST,
+        name="product",
+    )(x, w)
+
+
+def down_body(x_ref, w_ref, *refs):
+    out = refs[-1]
+    out[...] = dot_nn(x_ref[...], w_ref[...]).astype(jnp.bfloat16).reshape(out.shape)
+
+
+def down_call(x, w, blocks, chunks, chunk, into=None):
+    rows, depth = x.shape
+    width = w.shape[1]
+    bn = min(512, width)
+    r = rows // blocks
+    return pl.pallas_call(
+        down_body,
+        grid=(width // bn,),
+        in_specs=[
+            pl.BlockSpec((rows, depth), lambda i: (0, 0), pipeline_mode=pl.Buffered(1)),
+            pl.BlockSpec((depth, bn), lambda i: (0, i)),
+        ] + ([] if into is None else [pl.BlockSpec(memory_space=pl.ANY)]),
+        out_specs=pl.BlockSpec((blocks, 1, r, bn), lambda i: (0, chunk, 0, i)),
+        out_shape=jax.ShapeDtypeStruct((blocks, chunks, r, width), jnp.bfloat16),
+        input_output_aliases={} if into is None else {2: 0},
+        compiler_params=pltpu.CompilerParams(vmem_limit_bytes=VMEM_LIMIT),
+        cost_estimate=COST,
+        name="down",
+    )(x, w, *(() if into is None else (into,)))
 
 
 def doc_layout(lengths, total_rows):
@@ -352,59 +504,102 @@
     return total
 
 
-def gather_line(block, index, size):
-    rows = block.shape[0]
-    up, down = [], []
-    a = b = block
-    for step in range(1, size):
-        a = lax.ppermute(a, "narrow", [(i, i + 1) for i in range(step - 1, size - 1)])
-        b = lax.ppermute(b, "narrow", [(i, i - 1) for i in range(1, size - step + 1)])
-        up.append(a)
-        down.append(b)
-    full = jnp.zeros((size * rows, block.shape[1]), block.dtype)
-    full = lax.dynamic_update_slice_in_dim(full, block, index * rows, 0)
-    for k in range(1, size):
-        got = jnp.where(index >= k, up[k - 1], down[size - k - 1])
-        full = lax.dynamic_update_slice_in_dim(full, got, lax.rem(index + size - k, size) * rows, 0)
-    return full
-
-
-def scatter_narrow(parts, size):
-    return lax.psum_scatter(
-        parts.reshape(-1, parts.shape[-1]), "narrow", scatter_dimension=0, tiled=True
-    ).astype(jnp.float32)
-
-
-def wide_grads(lefts, rights, order, index, size):
-    bits = size.bit_length() - 1
+def swap_blocks(block, index, size):
+    return [block(index)] + [
+        lax.ppermute(block(index ^ k), "narrow", [(i, i ^ k) for i in range(size)]) for k in range(1, size)
+    ]
+
+
+def in_order(items, index):
+    step = 1
+    while step < len(items):
+        flip = (index & step) != 0
+        items = [jnp.where(flip, items[k ^ step], items[k]) for k in range(len(items))]
+        step *= 2
+    return items
+
+
+def high_bits(size):
+    first = list(range(1, size.bit_length() - 1))
+    return first, first[::-1]
+
+
+def by_core(size, step):
+    bits = high_bits(size)
+    return [(i, i ^ (1 << bits[i & 1][step])) for i in range(size)]
+
+
+def masks(size):
+    both = []
+    for bits in high_bits(size):
+        out = [0]
+        for bit in bits[::-1]:
+            out = out + [o ^ (1 << bit) for o in out]
+        both.append(jnp.array(out, dtype=jnp.int32))
+    return both
+
+
+def gather_plane(piece, size):
+    pieces = [piece]
+    for step in range(size.bit_length() - 2)[::-1]:
+        pieces = pieces + [lax.ppermute(p, "wide", by_core(size, step)) for p in pieces]
+    return pieces
+
+
+def gather_cores(pieces, index, size):
+    even, odd = masks(size)
+    first = (index & 1) == 0
+    pieces = pieces + [lax.ppermute(p, "wide", [(i, i ^ 1) for i in range(size)]) for p in pieces]
+    owners = jnp.concatenate([index ^ jnp.where(first, even, odd), index ^ 1 ^ jnp.where(first, odd, even)])
+    return pieces, owners.astype(jnp.int32)
+
+
+def scatter_narrow(parts):
+    return lax.psum_scatter(parts, "narrow", scatter_dimension=0, tiled=True)
+
+
+def grads_sent(lefts, rights, index, size):
+    even, odd = masks(size)
     part = lefts[0].shape[1] // size
-    mine = index & 1
-    pairs = 2 * jnp.arange(size // 2, dtype=jnp.int32)
-    sent = grad_call(pairs + (1 - mine), part, lefts, rights)
-    got = [lax.ppermute(x, "wide", [(i, i ^ 1) for i in range(size)]) for x in sent]
-    sums = grad_call(pairs + mine, part, lefts, rights, got)
-    results = []
-    for value, bit_order in zip(sums, order):
-        value = value.reshape((2,) * (bits - 1) + value.shape[1:])
-        left = list(range(1, bits))[::-1]
-        for bit in bit_order:
-            axis = left.index(bit)
-            left.pop(axis)
-            here = (index >> bit) & 1
-            out = lax.dynamic_index_in_dim(value, 1 - here, axis, keepdims=False).astype(jnp.bfloat16)
-            kept = lax.dynamic_index_in_dim(value, here, axis, keepdims=False)
-            got = lax.ppermute(out, "wide", [(i, i ^ (1 << bit)) for i in range(size)])
-            value = kept.astype(jnp.float32) + got.astype(jnp.float32)
-        results.append(value)
-    return results
-
-
-def sum_all(array, wide, narrow):
-    for axis, size in (("wide", wide), ("narrow", narrow)):
-        step = 1
-        while step < size:
-            array = array + lax.ppermute(array, axis, [(i, i ^ step) for i in range(size)])
-            step *= 2
+    tiles = (index ^ 1 ^ jnp.where((index & 1) == 0, odd, even)).astype(jnp.int32)
+    return grad_call(tiles, part, lefts, rights)
+
+
+def swap_cores(sent, size):
+    return lax.ppermute(sent, "wide", [(i, i ^ 1) for i in range(size)])
+
+
+def grads_kept(lefts, rights, got, index, size):
+    even, odd = masks(size)
+    part = lefts[0].shape[1] // size
+    tiles = (index ^ jnp.where((index & 1) == 0, even, odd)).astype(jnp.int32)
+    return grad_call(tiles, part, lefts, rights, got)
+
+
+def swap_plane(sent, step, size):
+    return lax.ppermute(sent, "wide", by_core(size, step))
+
+
+def halve(sent, kept, step, size):
+    return kept.astype(jnp.float32) + swap_plane(sent, step, size).astype(jnp.float32)
+
+
+def halve_again(value, step, size):
+    half = value.shape[0] // 2
+    return halve(value[half:], value[:half], step, size)
+
+
+def sum_plane(array, size):
+    items = [array] + [
+        lax.ppermute(array, "wide", [(i, i ^ (2 * flip)) for i in range(size)]) for flip in range(1, size // 2)
+    ]
+    return sum(in_order(items, lax.axis_index("wide") >> 1))
+
+
+def sum_column(array, narrow, size):
+    array = array + lax.ppermute(array, "wide", [(i, i ^ 1) for i in range(size)])
+    for bit in range(narrow.bit_length() - 1):
+        array = array + lax.ppermute(array, "narrow", [(i, i ^ (1 << bit)) for i in range(narrow)])
     return array
 
 
@@ -422,105 +617,127 @@
     group = query_width // key_width
     first, positions = doc_layout(doc_lengths[0], total_rows)
     tables = angle_tables(positions)
-    first_rows = first.astype(jnp.int32).reshape(narrow, chunks, r)
-    starts = [jnp.tile(first_rows[:, c], (1, 4)) for c in range(chunks)]
-    blocks = [[z * local_rows + c * r for z in range(narrow)] for c in range(chunks)]
+    start = jnp.tile(first.astype(jnp.int32).reshape(narrow, local_rows), (1, 4))
+    blocks = [z * local_rows for z in range(narrow)]
     w_twice = jnp.concatenate([w_query, twice(w_key), twice(w_value)], axis=1)
     w_joined = jnp.concatenate([w_query, w_key, w_value], axis=1)
+    part = width // wide
 
     source = hidden_in.astype(jnp.float32)
     inverse_one = lax.rsqrt(jnp.mean(source * source, axis=-1, keepdims=True) + EPSILON)
     unit_one = source * inverse_one
     normed_one = (unit_one * attn_gain).astype(jnp.bfloat16)
     full_one = lax.all_gather(normed_one, "narrow", axis=0, tiled=True)
+
+    w_out_part = lax.dynamic_slice_in_dim(w_out, wide_here * part, part, 1)
+    w_out_part = jnp.concatenate(
+        in_order(swap_blocks(lambda j: w_out_part, here, narrow), here), axis=0
+    )
+    w_out_plane = gather_plane(w_out_part, wide)
+    full_one, w_twice, tables, w_out_plane = lax.optimization_barrier((full_one, w_twice, tables, w_out_plane))
+    w_out_parts, w_out_at = gather_cores(w_out_plane, wide_here, wide)
+
+    dy_a = lax.all_gather(after(upstream[:r], full_one), "narrow", axis=0, tiled=True)
     q, k, v = qkv_call(full_one, w_twice, *tables, query_width, 2 * key_width)
 
-    def rows_of(array, c):
-        return array[c * r : (c + 1) * r]
-
-    def out_parts(o):
-        parts = jnp.dot(o, w_out, preferred_element_type=jnp.float32).astype(jnp.bfloat16)
-        return parts.reshape(narrow, r, width)
-
-    def second_norm(c, summed):
-        resid = rows_of(source, c) + summed
+    def swap_heads(x):
+        return lax.all_to_all(x.reshape(total_rows, query_width), "narrow", 0, 0, tiled=True)
+
+    def second_norm(summed):
+        resid = source + summed
         inverse = lax.rsqrt(jnp.mean(resid * resid, axis=-1, keepdims=True) + EPSILON)
         unit = resid * inverse
         return resid, inverse, unit, (unit * mlp_gain).astype(jnp.bfloat16)
 
-    heads_a, lse_a = attend(q, k, v, starts[0], blocks[0], r, kv, group)
-    parts_a = out_parts(heads_a)
-    summed_a = scatter_narrow(parts_a, narrow)
-    q_late, upstream_late, _ = lax.optimization_barrier((q, upstream, parts_a))
-    dy_full = gather_line(upstream_late, here, narrow).reshape(narrow, chunks, r, width)
-    heads_b, lse_b = attend(q_late, k, v, starts[1], blocks[1], r, kv, group)
-    summed_b = scatter_direct(out_parts(heads_b), here, narrow)
-    resid_a, inverse_a, unit_a, normed_a = second_norm(0, summed_a)
+    heads, lse = attend(q, k, v, start, blocks, local_rows, kv, group)
+    heads_rows = swap_heads(heads).reshape(narrow, local_rows, query_width)
+    dy_b = lax.all_gather(after(upstream[r:], heads_rows), "narrow", axis=0, tiled=True)
+    resid, inverse_two, unit_two, normed_two = second_norm(
+        out_project(w_out_at, after(heads_rows, dy_a), w_out_parts)
+    )
+    normed_a, normed_b, dy_b = lax.optimization_barrier((normed_two[:r], normed_two[r:], dy_b))
     full_a = lax.all_gather(normed_a, "narrow", axis=0, tiled=True)
-    resid_b, inverse_b, unit_b, normed_b = second_norm(1, summed_b)
-    normed_b = after(normed_b, normed_a)
-    full_b = lax.all_gather(normed_b, "narrow", axis=0, tiled=True)
-    dy_a, dy_b = (dy_full[:, c].reshape(narrow * r, width) for c in range(chunks))
-
-    def mlp_back(dg, du):
-        return (dot_nt(dg, w_gate) + dot_nt(du, w_up)).astype(jnp.bfloat16).reshape(narrow, r, width)
-
-    def second_back(c, grad, unit, inverse):
-        scaled = grad * mlp_gain
-        back = rows_of(upstream, c).astype(jnp.float32) + inverse * (
-            scaled - unit * jnp.mean(scaled * unit, axis=-1, keepdims=True)
+    full_b = lax.all_gather(after(normed_b, full_a), "narrow", axis=0, tiled=True)
+
+    m_a, dg_a, du_a = mlp_call(full_a, dy_a, w_gate, w_up, w_down)
+    parts_a = mlp_back_call(dg_a, du_a, w_gate, w_up)
+    grad_a = scatter_narrow(parts_a)
+    y_a = down_call(after(m_a, parts_a), w_down, narrow, chunks, 0)
+    m_b, dg_b, du_b = mlp_call(full_b, after(dy_b, y_a), w_gate, w_up, w_down)
+    parts_b = mlp_back_call(dg_b, du_b, w_gate, w_up)
+    parts_b, grad_a = lax.optimization_barrier((parts_b, grad_a))
+    grad_b = scatter_narrow(parts_b)
+
+    here_wide = (wide_here, wide)
+    gate_up = [full_a, after(full_b, parts_b)], [[dg_a, dg_b], [du_a, du_b]]
+    sent_gate_up = grads_sent(*gate_up, *here_wide)
+    down = [after(dy_a, sent_gate_up), dy_b], [[m_a, m_b]]
+    sent_down = grads_sent(*down, *here_wide)
+    gate_up = [after(full_a, sent_down), full_b], gate_up[1]
+    gate_up_sent, gate_up_kept = grads_kept(*gate_up, swap_cores(sent_gate_up, wide), *here_wide)
+    y = down_call(after(m_b, gate_up_sent), w_down, narrow, chunks, 1, y_a)
+    layer_sum = lax.psum_scatter(
+        after(y, grad_b).reshape(total_rows, width), "narrow", scatter_dimension=0, tiled=True
+    )
+    unit_late = after(unit_two, y)
+    grad_a, grad_b = grad_a.astype(jnp.float32), grad_b.astype(jnp.float32)
+    scaled_grad = jnp.concatenate([grad_a, grad_b], axis=0)
+    scaled = scaled_grad * mlp_gain
+    back = upstream.astype(jnp.float32) + inverse_two * (
+        scaled - unit_late * jnp.mean(scaled * unit_late, axis=-1, keepdims=True)
+    )
+    gain_two = jnp.sum(scaled_grad * unit_late, axis=0)
+    low = back.astype(jnp.bfloat16)
+    heads_grad = out_project_back(w_out_at, low, w_out_parts, narrow)
+    gate_up_kept = after(gate_up_kept, heads_grad)
+    heads_side = jnp.concatenate([heads_rows[j] for j in range(narrow)], axis=1)
+    out = [after(low, heads_grad)], [[heads_side]]
+    sent_out = grads_sent(*out, *here_wide)
+    out_sent, out_kept = grads_kept(*out, swap_cores(sent_out, wide), *here_wide)
+    gate_up_sum = halve(gate_up_sent, gate_up_kept, 0, wide).astype(jnp.bfloat16)
+    rest = gate_up_sum.shape[0] // 2
+    gate_up_kept, gate_up_sent = gate_up_sum[:rest], gate_up_sum[rest:]
+    heads_grad = swap_heads(heads_grad)
+    joined_grad = attend_back(
+        after(q, gate_up_sent, out_sent), k, v, start, heads_grad, heads, lse, None, tables, blocks, local_rows, kv,
+        group,
+    )
+    parts = mat_call(joined_grad, after(w_joined, layer_sum), True)
+    normed_one_grad = scatter_narrow(parts).astype(jnp.float32)
+    gate_up_got = swap_plane(gate_up_sent, 1, wide)
+    joined = [after(full_one, parts)], [[joined_grad]]
+    sent_joined = grads_sent(*joined, *here_wide)
+    parts_late, _ = lax.optimization_barrier((parts, sent_joined))
+    gain_one = jnp.sum(parts_late.astype(jnp.float32) * full_one.astype(jnp.float32), axis=0) / attn_gain
+    joined = [after(full_one, gain_one)], [[joined_grad]]
+    joined_sent, joined_kept = grads_kept(*joined, swap_cores(sent_joined, wide), *here_wide)
+    down = [after(dy_a, joined_sent), dy_b], [[m_a, m_b]]
+    down_sent, down_kept = grads_kept(*down, swap_cores(sent_down, wide), *here_wide)
+    gains = sum_column(sum_plane(after(jnp.stack([gain_one, gain_two]), down_sent), wide), narrow, wide)
+    out_sum = halve(out_sent, after(out_kept, parts), 0, wide)
+    joined_got = swap_plane(joined_sent, 0, wide)
+    down_got = swap_plane(down_sent, 0, wide)
+    gate_up_sum = after(gate_up_kept, down_sent).astype(jnp.float32) + gate_up_got.astype(jnp.float32)
+    joined_sum = joined_kept.astype(jnp.float32) + joined_got.astype(jnp.float32)
+    down_sum = down_kept.astype(jnp.float32) + down_got.astype(jnp.float32)
+    for step in range(1, wide.bit_length() - 2):
+        out_sum, joined_sum, down_sum = (
+            halve_again(x.astype(jnp.bfloat16), step, wide) for x in (out_sum, joined_sum, down_sum)
         )
-        return back, jnp.sum(grad * unit, axis=0)
-
-    m_a, dg_a, du_a = mlp_call(full_a, dy_a, w_gate, w_up, w_down)
-    parts_a = mlp_back(dg_a, du_a)
-    grad_a = scatter_narrow(parts_a, narrow)
-    full_b = after(full_b, parts_a)
-    m_b, dg_b, du_b = mlp_call(full_b, dy_b, w_gate, w_up, w_down)
-    parts_b = mlp_back(dg_b, du_b)
-    grad_b = scatter_direct(parts_b, here, narrow)
-    back_a, gain_two_a = second_back(0, grad_a, unit_a, inverse_a)
-    back_b, gain_two_b = second_back(1, grad_b, unit_b, inverse_b)
-    low_a, low_b = back_a.astype(jnp.bfloat16), back_b.astype(jnp.bfloat16)
-    back_full_a = lax.all_gather(low_a, "narrow", axis=0, tiled=True)
-    back_full_b = lax.all_gather(after(low_b, low_a), "narrow", axis=0, tiled=True)
-
-    m_a, m_b, dg_a, dg_b, du_a, du_b, _ = lax.optimization_barrier((m_a, m_b, dg_a, dg_b, du_a, du_b, parts_b))
-    high = list(range(1, wide.bit_length() - 1))
-    swap = high[::-1]
-    gate_sum, up_sum = wide_grads(
-        [full_a, full_b], [[dg_a, dg_b], [du_a, du_b]], [high, swap], wide_here, wide
-    )
-    (down_sum,) = wide_grads([dy_a, dy_b], [[m_a, m_b]], [high], wide_here, wide)
-
-    def layer_rows(m, resid):
-        parts = jnp.dot(m, w_down, preferred_element_type=jnp.float32).astype(jnp.bfloat16)
-        return (resid + scatter_direct(parts.reshape(narrow, r, width), here, narrow)).astype(jnp.bfloat16)
-
-    layer_out = jnp.concatenate([layer_rows(m_a, resid_a), layer_rows(m_b, resid_b)], axis=0)
-
-    heads_grad_a = dot_nt(back_full_a, w_out).astype(jnp.bfloat16)
-    carried = attend_back(
-        q, k, v, starts[0], heads_grad_a, heads_a, lse_a, None, None, blocks[0], r, kv, group
-    )
-    back_full_b = after(back_full_b, carried[0])
-    heads_grad_b = dot_nt(back_full_b, w_out).astype(jnp.bfloat16)
-    joined_grad = attend_back(
-        q, k, v, starts[1], heads_grad_b, heads_b, lse_b, carried, tables, blocks[1], r, kv, group
-    )
-    parts = dot_nt(joined_grad, w_joined).astype(jnp.bfloat16)
-    normed_one_grad = scatter_narrow(parts, narrow)
-    parts = after(parts, joined_grad)
-    gain_one = jnp.sum(parts.astype(jnp.float32) * full_one.astype(jnp.float32), axis=0) / attn_gain
-    gains = sum_all(jnp.stack([gain_one, gain_two_a + gain_two_b]), wide, narrow)
-    joined_late = after(joined_grad, parts)
-    (joined_sum,) = wide_grads([full_one], [[joined_late]], [high], wide_here, wide)
-    (out_sum,) = wide_grads([back_full_a, back_full_b], [[heads_a, heads_b]], [swap], wide_here, wide)
+        if step > 1:
+            gate_up_sum = halve_again(gate_up_sum.astype(jnp.bfloat16), step, wide)
+    gate_up_sum, down_sum, out_sum, joined_sum = gate_up_sum[0], down_sum[0], out_sum[0], joined_sum[0]
+    out_sum = after(out_sum.astype(jnp.bfloat16), joined_got, down_got)
+    got = swap_blocks(
+        lambda j: lax.dynamic_slice_in_dim(out_sum, j * query_width, query_width, 1), here, narrow
+    )
+    out_sum = sum(x.astype(jnp.float32) for x in got)
+    layer_out = (resid + layer_sum.astype(jnp.float32)).astype(jnp.bfloat16)
     scaled_one = normed_one_grad * attn_gain
-    resid_grad = jnp.concatenate([back_a, back_b], axis=0)
-    input_grad = resid_grad + inverse_one * (
+    input_grad = back + inverse_one * (
         scaled_one - unit_one * jnp.mean(scaled_one * unit_one, axis=-1, keepdims=True)
     )
+    gate_sum, up_sum = gate_up_sum[:, : w_gate.shape[1]], gate_up_sum[:, w_gate.shape[1] :]
     return (
         layer_out,
         input_grad,

time: 786 us -> 665 us (0.85)
  the two profiles are of different devices: /device:TPU:0 before, /device:TPU:11 now
where the time goes in v2:
time: 665 us; the launch traced here: 658 us
  waiting for transfers between devices  248 us (37%)
  Pallas kernels  233 us (35%)
  blocking collectives  47.7 us (7%)
  other arithmetic  43.6 us (7%)
  starting transfers between devices  39.8 us (6%)
  local copies, waits for them, and re-layouts  32 us (5%)
  between operations  14.6 us (2%)
    pallas_call x8, Pallas kernels, grad_call(): pl.pallas_call(functools.partial(grad_body, nl, nr, got), grid_spec=pltpu...  80.6 us
    ppermute x6, waiting for transfers between devices, swap_blocks(): lax.ppermute(block(index ^ k), 'narrow', [(i, i ^ k) for i in range(size)])  58.1 us
    ppermute x8, waiting for transfers between devices, swap_plane(): return lax.ppermute(sent, 'wide', by_core(size, step))  48.7 us
    all_to_all x1, blocking collectives, swap_heads(): lax.all_to_all(x.reshape(total_rows, query_width), 'narrow', 0, 0, tiled=...  47.7 us
    all_gather x1, waiting for transfers between devices, on_device(): full_a = lax.all_gather(normed_a, 'narrow', axis=0, tiled=True)  46.6 us
    pallas_call x2, Pallas kernels, mlp_call(): pl.pallas_call(mlp_body, grid=(f // bf,), in_specs=[held, held, col, col,...  40.8 us
    pallas_call x2, Pallas kernels, mlp_back_call(): pl.pallas_call(mlp_back_body, grid=(d // bn,), in_specs=[held, held, row,...  30.5 us
    all_gather x1, waiting for transfers between devices, on_device(): lax.all_gather(after(upstream[r:], heads_rows), 'narrow', axis=0, tiled=T...  24.7 us
  transfers between devices with their start and end apart: 41, of which 24 were waited for; matrix products, arithmetic and copies ran while one was open for 9% of the time, Pallas kernels for 33%

profile of v2, /device:TPU:11, one launch (start us, length us, event | category | flops | bytes accessed | tf_op | source)
XLA Modules:
  0.0 658.4 jit_solution(18082429744253562836)
XLA Ops:
  15.9 23.0 %collective-permute-done = bf16[512,256]{1,0:T(8,128)(2,1)S(1)} collective-permute-done((bf16[512,256]{1,0:T(8,128)(2,1)S(1)}, bf16[512,256]{1,0:T(8,128)(2,1)S(1)}, u32[]{:S(2)}, u32[]{:S(2)}) %collective-permute-start) | collective-permute-done | bytes 262176 | tf_op jit(solution)/shard_map/ppermute | solution.py:509
  38.9 15.9 %collective-permute-done.1 = bf16[512,256]{1,0:T(8,128)(2,1)S(1)} collective-permute-done((bf16[512,256]{1,0:T(8,128)(2,1)S(1)}, bf16[512,256]{1,0:T(8,128)(2,1)S(1)}, u32[]{:S(2)}, u32[]{:S(2)}) %collective-permute-start.1) | collective-permute-done | bytes 262176 | tf_op jit(solution)/shard_map/ppermute | solution.py:509
  59.6 11.0 %collective-permute-done.3.refs_1_ = bf16[2048,256]{1,0:T(8,128)(2,1)S(1)} collective-permute-done((bf16[2048,256]{1,0:T(8,128)(2,1)S(1)}, bf16[2048,256]{1,0:T(8,128)(2,1)S(1)}, u32[]{:S(2)}, u32[]{:S(2)}) %collective-permute-start.3) | collective-permute-done | bytes 1048608 | tf_op jit(solution)/shard_map/ppermute | solution.py:545
  72.9 8.1 %concatenate.29.w_ref = bf16[2048,1024]{1,0:T(8,128)(2,1)} concatenate(bf16[2048,512]{1,0:T(8,128)(2,1)} %param.33, bf16[2048,64]{1,0:T(8,128)(2,1)} %get-tuple-element.194, bf16[2048,128]{1,0:T(8,128)(2,1)S(1)} %copy-done.13, bf16[2048,64]{1,0:T(8,128)(2,1)} %get-tuple-element.195, bf16[2048,64]{1,0:T(8,128)(2,1)} %get-tuple-element.184, bf16[2048,128]{1,0:T(8,128)(2,1)S(1)} %copy-done.11, ...), dimensions={1} | concatenate | bytes 8388608 | tf_op jit(solution)/shard_map/concatenate | solution.py:622
  85.8 9.1 %collective-permute-done.5.refs_3_ = bf16[2048,256]{1,0:T(8,128)(2,1)} collective-permute-done((bf16[2048,256]{1,0:T(8,128)(2,1)S(1)}, bf16[2048,256]{1,0:T(8,128)(2,1)}, u32[]{:S(2)}, u32[]{:S(2)}) %collective-permute-start.5) | collective-permute-done | bytes 1048608 | tf_op jit(solution)/shard_map/ppermute | solution.py:545
  94.9 9.6 %all-gather.6.cloned.1.call-done.x_ref.refs_0_ = bf16[1024,2048]{1,0:T(8,128)(2,1)} async-done(((bf16[256,2048]{1,0:T(8,128)(2,1)}), bf16[1024,2048]{1,0:T(8,128)(2,1)}) %all-gather.6.cloned.1.call-update) | async-done | bytes 4194320 | tf_op jit(solution)/shard_map/all_gather | solution.py:630
  105.4 9.0 %qkv.1 = (bf16[1024,512]{1,0:T(8,128)(2,1)}, bf16[1024,256]{1,0:T(8,128)(2,1)}, bf16[1024,256]{1,0:T(8,128)(2,1)}) custom-call(bf16[1024,2048]{1,0:T(8,128)(2,1)} %all-gather.6.cloned.1.call-done.x_ref.refs_0_, bf16[2048,1024]{1,0:T(8,128)(2,1)} %concatenate.29.w_ref, f32[1024,128]{1,0:T(8,128)} %get-tuple-element.69.cos_ref.refs_7_, ...), custom_call_target="tpu_custom_call" | custom-call | flops 1 | bytes 1 | tf_op jit(solution)/shard_map/qkv/pallas_call | solution.py:58
  114.4 12.2 %attend.1 = (bf16[1024,512]{1,0:T(8,128)(2,1)}, f32[2,4,1024]{2,1,0:T(4,128)}) custom-call(bf16[1024,512]{1,0:T(8,128)(2,1)} %get-tuple-element.107.q_ref.refs_0_, bf16[1024,256]{1,0:T(8,128)(2,1)} %get-tuple-element.72.k_ref.refs_1_, bf16[1024,256]{1,0:T(8,128)(2,1)} %get-tuple-element.73.v_ref.refs_2_, s32[4,1024]{1,0:T(4,128)} %bitcast.40), custom_call_target="tpu_custom_call" | custom-call | flops 1 | bytes 1 | tf_op jit(solution)/shard_map/attend/pallas_call | solution.py:125
  126.6 47.7 %all_to_all.17.x_ref = bf16[4,256,512]{2,1,0:T(8,128)(2,1)} all-to-all(bf16[4,256,512]{2,1,0:T(8,128)(2,1)} %bitcast.39), channel_id=1, replica_groups=mesh['wide'=8,'narrow'=4] {'narrow'}, dimensions={0} | all-to-all | bytes 2097152 | tf_op jit(solution)/shard_map/all_to_all | solution.py:644
  178.7 3.0 collective-permute-done.7.refs_5_
  183.4 7.6 %out_project.1 = f32[256,2048]{1,0:T(8,128)} custom-call(s32[8]{0:T(128)} %pad_add_fusion.at_ref, bf16[4,256,512]{2,1,0:T(8,128)(2,1)} %all_to_all.17.x_ref, bf16[2048,256]{1,0:T(8,128)(2,1)} %copy-done.7, bf16[2048,256]{1,0:T(8,128)(2,1)} %copy-done.19, bf16[2048,256]{1,0:T(8,128)(2,1)} %collective-permute-done.4.refs_2_, ...), custom_call_target="tpu_custom_call" | custom-call | flops 1 | bytes 1 | tf_op jit(solution)/shard_map/out_project/pallas_call | solution.py:310
  194.9 24.7 %all-gather.10.cloned.1.call-done.dy_ref.refs_1_ = bf16[512,2048]{1,0:T(8,128)(2,1)} async-done(((bf16[128,2048]{1,0:T(8,128)(2,1)}), bf16[512,2048]{1,0:T(8,128)(2,1)}) %all-gather.10.cloned.1.call-update) | async-done | bytes 2097168 | tf_op jit(solution)/shard_map/all_gather | solution.py:654
  219.7 46.6 %all-gather.12.cloned.1.call-done.x_ref.refs_0_ = bf16[512,2048]{1,0:T(8,128)(2,1)} async-done(((bf16[128,2048]{1,0:T(8,128)(2,1)}), bf16[512,2048]{1,0:T(8,128)(2,1)}) %all-gather.12.cloned.1.call-update) | async-done | bytes 2097168 | tf_op jit(solution)/shard_map/all_gather | solution.py:659
  266.4 20.5 %mlp.2 = (bf16[512,2048]{1,0:T(8,128)(2,1)}, bf16[512,2048]{1,0:T(8,128)(2,1)}, bf16[512,2048]{1,0:T(8,128)(2,1)}) custom-call(bf16[512,2048]{1,0:T(8,128)(2,1)} %all-gather.12.cloned.1.call-done.x_ref.refs_0_, bf16[512,2048]{1,0:T(8,128)(2,1)} %all-gather.8.cloned.1.call-done.dy_ref.refs_0_, bf16[2048,2048]{1,0:T(8,128)(2,1)} %wg_ref.7, ...), custom_call_target="tpu_custom_call" | custom-call | flops 1 | bytes 1 | tf_op jit(solution)/shard_map/mlp/pallas_call | solution.py:385
  286.9 15.3 %mlp_back.2 = bf16[512,2048]{1,0:T(8,128)(2,1)} custom-call(bf16[512,2048]{1,0:T(8,128)(2,1)} %get-tuple-element.87.dg_ref.refs_2_, bf16[512,2048]{1,0:T(8,128)(2,1)} %get-tuple-element.88.du_ref.refs_4_, bf16[2048,2048]{1,0:T(8,128)(2,1)} %wg_ref.7, bf16[2048,2048]{1,0:T(8,128)(2,1)} %wu_ref.7), custom_call_target="tpu_custom_call" | custom-call | flops 1 | bytes 1 | tf_op jit(solution)/shard_map/mlp_back/pallas_call | solution.py:407
  302.3 8.8 %down.2.refs_0_ = bf16[4,2,128,2048]{3,2,1,0:T(8,128)(2,1)} custom-call(bf16[512,2048]{1,0:T(8,128)(2,1)} %get-tuple-element.89.x_ref.refs_2_, bf16[2048,2048]{1,0:T(8,128)(2,1)} %w_ref.3), custom_call_target="tpu_custom_call" | custom-call | flops 1 | bytes 1 | tf_op jit(solution)/shard_map/down/pallas_call | solution.py:450
  313.0 20.3 %mlp.3 = (bf16[512,2048]{1,0:T(8,128)(2,1)}, bf16[512,2048]{1,0:T(8,128)(2,1)}, bf16[512,2048]{1,0:T(8,128)(2,1)}) custom-call(bf16[512,2048]{1,0:T(8,128)(2,1)} %all-gather.14.cloned.1.call-done.x_ref.refs_1_, bf16[512,2048]{1,0:T(8,128)(2,1)} %all-gather.10.cloned.1.call-done.dy_ref.refs_1_, bf16[2048,2048]{1,0:T(8,128)(2,1)} %wg_ref.7, ...), custom_call_target="tpu_custom_call" | custom-call | flops 1 | bytes 1 | tf_op jit(solution)/shard_map/mlp/pallas_call | solution.py:385
  333.3 15.2 %mlp_back.3 = bf16[512,2048]{1,0:T(8,128)(2,1)} custom-call(bf16[512,2048]{1,0:T(8,128)(2,1)} %get-tuple-element.92.dg_ref.refs_3_, bf16[512,2048]{1,0:T(8,128)(2,1)} %get-tuple-element.93.du_ref.refs_5_, bf16[2048,2048]{1,0:T(8,128)(2,1)} %wg_ref.7, bf16[2048,2048]{1,0:T(8,128)(2,1)} %wu_ref.7), custom_call_target="tpu_custom_call" | custom-call | flops 1 | bytes 1 | tf_op jit(solution)/shard_map/mlp_back/pallas_call | solution.py:407
  348.6 8.7 %reduce-scatter.5.cloned.1.call-done = bf16[128,2048]{1,0:T(8,128)(2,1)} async-done(((bf16[512,2048]{1,0:T(8,128)(2,1)}), bf16[128,2048]{1,0:T(8,128)(2,1)}) %reduce-scatter.5.cloned.1.call-update) | async-done | bytes 524304 | tf_op jit(solution)/shard_map/reduce_scatter | solution.py:558
  357.2 15.2 %weight_grad.8 = bf16[4,256,4096]{2,1,0:T(8,128)(2,1)} custom-call(s32[4]{0:T(128)} %copy-done.27, bf16[512,2048]{1,0:T(8,128)(2,1)} %all-gather.12.cloned.1.call-done.x_ref.refs_0_, bf16[512,2048]{1,0:T(8,128)(2,1)} %all-gather.14.cloned.1.call-done.x_ref.refs_1_, bf16[512,2048]{1,0:T(8,128)(2,1)} %get-tuple-element.87.dg_ref.refs_2_, ...), custom_call_target="tpu_custom_call" | custom-call | flops 1 | bytes 1 | tf_op jit(solution)/shard_map/weight_grad/pallas_call | solution.py:285
  373.7 9.4 %weight_grad.9 = bf16[4,256,2048]{2,1,0:T(8,128)(2,1)} custom-call(s32[4]{0:T(128)} %copy-done.27, bf16[512,2048]{1,0:T(8,128)(2,1)} %all-gather.8.cloned.1.call-done.dy_ref.refs_0_, bf16[512,2048]{1,0:T(8,128)(2,1)} %all-gather.10.cloned.1.call-done.dy_ref.refs_1_, bf16[512,2048]{1,0:T(8,128)(2,1)} %get-tuple-element.89.x_ref.refs_2_, ...), custom_call_target="tpu_custom_call" | custom-call | flops 1 | bytes 1 | tf_op jit(solution)/shard_map/weight_grad/pallas_call | solution.py:285
  383.1 3.3 collective-permute-done.10.refs_6_
  386.4 18.2 %weight_grad.10 = (bf16[2,256,4096]{2,1,0:T(8,128)(2,1)}, bf16[2,256,4096]{2,1,0:T(8,128)(2,1)}) custom-call(s32[4]{0:T(128)} %copy-done.26, bf16[512,2048]{1,0:T(8,128)(2,1)} %all-gather.12.cloned.1.call-done.x_ref.refs_0_, bf16[512,2048]{1,0:T(8,128)(2,1)} %all-gather.14.cloned.1.call-done.x_ref.refs_1_, ...), custom_call_target="tpu_custom_call" | custom-call | flops 1 | bytes 1 | tf_op jit(solution)/shard_map/weight_grad/pallas_call | solution.py:285
  404.6 8.8 %down.3 = bf16[4,2,128,2048]{3,2,1,0:T(8,128)(2,1)} custom-call(bf16[512,2048]{1,0:T(8,128)(2,1)} %get-tuple-element.99.refs_3_.x_ref, bf16[2048,2048]{1,0:T(8,128)(2,1)} %w_ref.3, bf16[4,2,128,2048]{3,2,1,0:T(8,128)(2,1)} %down.2.refs_0_), custom_call_target="tpu_custom_call", output_to_operand_aliasing={{}: (2, {})} | custom-call | flops 1 | bytes 1 | tf_op jit(solution)/shard_map/down/pallas_call | solution.py:450
  413.4 2.7 reduce-scatter.7.cloned.1.call-done
  421.4 7.1 %out_project_back.1 = bf16[4,256,512]{2,1,0:T(8,128)(2,1)} custom-call(s32[8]{0:T(128)} %pad_add_fusion.at_ref, bf16[256,2048]{1,0:T(8,128)(2,1)} %fusion.20.x_ref.refs_0_, bf16[2048,256]{1,0:T(8,128)(2,1)} %copy-done.7, bf16[2048,256]{1,0:T(8,128)(2,1)} %copy-done.19, bf16[2048,256]{1,0:T(8,128)(2,1)} %collective-permute-done.4.refs_2_, ...), custom_call_target="tpu_custom_call" | custom-call | flops 1 | bytes 1 | tf_op jit(solution)/shard_map/out_project_back/pallas_call | solution.py:335
  428.5 6.0 weight_grad.11
  438.3 7.5 %all-to-all-start.1 = ((bf16[4,256,512]{2,1,0:T(8,128)(2,1)}), bf16[4,256,512]{2,1,0:T(8,128)(2,1)}, u32[]{:S(2)}, u32[]{:S(2)}) async-start(bf16[4,256,512]{2,1,0:T(8,128)(2,1)} %out_project_back.1), calls=%async_computation.4 | async-start | bytes 2097152 | tf_op jit(solution)/shard_map/all_to_all | solution.py:644
  445.9 7.8 %weight_grad.12 = (bf16[2,256,2048]{2,1,0:T(8,128)(2,1)}, bf16[2,256,2048]{2,1,0:T(8,128)(2,1)}) custom-call(s32[4]{0:T(128)} %copy-done.26, bf16[256,2048]{1,0:T(8,128)(2,1)} %fusion.20.x_ref.refs_0_, bf16[256,2048]{1,0:T(8,128)(2,1)} %pad_maximum_fusion.3.refs_1_, bf16[4,256,2048]{2,1,0:T(8,128)(2,1)} %collective-permute-done.12.refs_2_), custom_call_target="tpu_custom_call" | custom-call | flops 1 | bytes 1 | tf_op jit(solution)/shard_map/weight_grad/pallas_call | solution.py:285
  454.3 29.9 %collective-permute-done.11 = bf16[2,256,4096]{2,1,0:T(8,128)(2,1)} collective-permute-done((bf16[2,256,4096]{2,1,0:T(8,128)(2,1)}, bf16[2,256,4096]{2,1,0:T(8,128)(2,1)}, u32[]{:S(2)}, u32[]{:S(2)}) %collective-permute-start.11) | collective-permute-done | bytes 4194336 | tf_op jit(solution)/shard_map/ppermute | solution.py:580
  484.3 3.8 add_convert_fusion
  490.4 6.4 all-to-all-done.1
  496.8 20.1 %attend_back.1.x_ref.refs_1_ = bf16[1024,768]{1,0:T(8,128)(2,1)} custom-call(bf16[1024,512]{1,0:T(8,128)(2,1)} %get-tuple-element.107.q_ref.refs_0_, bf16[1024,256]{1,0:T(8,128)(2,1)} %get-tuple-element.72.k_ref.refs_1_, bf16[1024,256]{1,0:T(8,128)(2,1)} %get-tuple-element.73.v_ref.refs_2_, s32[4,1024]{1,0:T(4,128)} %bitcast.41, ...), custom_call_target="tpu_custom_call" | custom-call | flops 1 | bytes 1 | tf_op jit(solution)/shard_map/attend_back/pallas_call | solution.py:225
  519.3 7.4 %product.1 = bf16[1024,2048]{1,0:T(8,128)(2,1)} custom-call(bf16[1024,768]{1,0:T(8,128)(2,1)} %attend_back.1.x_ref.refs_1_, bf16[2048,768]{1,0:T(8,128)(2,1)} %pad_maximum_fusion.w_ref), custom_call_target="tpu_custom_call" | custom-call | flops 1 | bytes 1 | tf_op jit(solution)/shard_map/product/pallas_call | solution.py:428
  526.7 6.3 weight_grad.13
  533.9 3.1 add_convert_fusion.2
  543.6 6.7 %weight_grad.14 = (bf16[2,256,768]{2,1,0:T(8,128)(2,1)}, bf16[2,256,768]{2,1,0:T(8,128)(2,1)}) custom-call(s32[4]{0:T(128)} %copy-done.26, bf16[1024,2048]{1,0:T(8,128)(2,1)} %all-gather.6.cloned.1.call-done.x_ref.refs_0_, bf16[1024,768]{1,0:T(8,128)(2,1)} %attend_back.1.x_ref.refs_1_, bf16[4,256,768]{2,1,0:T(8,128)(2,1)} %copy-done.22), custom_call_target="tpu_custom_call" | custom-call | flops 1 | bytes 1 | tf_op jit(solution)/shard_map/weight_grad/pallas_call | solution.py:285
  550.3 11.1 %weight_grad.15 = (bf16[2,256,2048]{2,1,0:T(8,128)(2,1)}, bf16[2,256,2048]{2,1,0:T(8,128)(2,1)}) custom-call(s32[4]{0:T(128)} %copy-done.26, bf16[512,2048]{1,0:T(8,128)(2,1)} %all-gather.8.cloned.1.call-done.dy_ref.refs_0_, bf16[512,2048]{1,0:T(8,128)(2,1)} %all-gather.10.cloned.1.call-done.dy_ref.refs_1_, ...), custom_call_target="tpu_custom_call" | custom-call | flops 1 | bytes 1 | tf_op jit(solution)/shard_map/weight_grad/pallas_call | solution.py:285
  564.1 7.8 %collective-permute-done.15 = f32[2,2048]{1,0:T(2,128)S(1)} collective-permute-done((f32[2,2048]{1,0:T(2,128)S(1)}, f32[2,2048]{1,0:T(2,128)S(1)}, u32[]{:S(2)}, u32[]{:S(2)}) %collective-permute-start.15) | collective-permute-done | bytes 16416 | tf_op jit(solution)/shard_map/ppermute | solution.py:594
  579.7 4.6 collective-permute-start.20
  586.7 18.7 %collective-permute-done.21 = bf16[2,256,768]{2,1,0:T(8,128)(2,1)S(1)} collective-permute-done((bf16[2,256,768]{2,1,0:T(8,128)(2,1)S(1)}, bf16[2,256,768]{2,1,0:T(8,128)(2,1)S(1)}, u32[]{:S(2)}, u32[]{:S(2)}) %collective-permute-start.21) | collective-permute-done | bytes 786464 | tf_op jit(solution)/shard_map/ppermute | solution.py:580
  611.6 2.6 collective-permute-start.27
  616.1 3.5 collective-permute-done.26
  619.6 11.5 %collective-permute-done.27 = bf16[256,512]{1,0:T(8,128)(2,1)S(1)} collective-permute-done((bf16[256,512]{1,0:T(8,128)(2,1)S(1)}, bf16[256,512]{1,0:T(8,128)(2,1)S(1)}, u32[]{:S(2)}, u32[]{:S(2)}) %collective-permute-start.27) | collective-permute-done | bytes 262176 | tf_op jit(solution)/shard_map/ppermute | solution.py:509
  631.1 4.3 collective-permute-done.28
  638.3 3.2 add_bitcast_fusion.1
  641.5 2.9 copy.48
  646.4 5.2 fusion.13
  (188 shorter events, 82.3 us)
Async XLA Ops:
  7.2 97.3 %all-gather.6.cloned.1.call-start = ((), (), s32[]{:S(2)}) async-start(), calls=%async_computation.6 | async-start | bytes 5242880 | tf_op jit(solution)/shard_map/all_gather | solution.py:630
  11.3 166.2 %all-gather.8.cloned.1.call-start = ((), (), s32[]{:S(2)}) async-start(), calls=%async_computation.7 | async-start | bytes 2621440 | tf_op jit(solution)/shard_map/all_gather | solution.py:640
  12.3 26.5 %collective-permute-start = (bf16[512,256]{1,0:T(8,128)(2,1)S(1)}, bf16[512,256]{1,0:T(8,128)(2,1)S(1)}, u32[]{:S(2)}, u32[]{:S(2)}) collective-permute-start(bf16[512,256]{1,0:T(8,128)(2,1)S(1)} %constant_dynamic-slice_fusion.3), channel_id=1, source_target_pairs={{0,3},{1,2},{2,1},{3,0},{4,7},{5,6},{6,5},{7,4},{8,11},{9,10},{10,... | collective-permute-start | bytes 786440 | tf_op jit(solution)/shard_map/ppermute | solution.py:509
  13.7 41.0 %collective-permute-start.1 = (bf16[512,256]{1,0:T(8,128)(2,1)S(1)}, bf16[512,256]{1,0:T(8,128)(2,1)S(1)}, u32[]{:S(2)}, u32[]{:S(2)}) collective-permute-start(bf16[512,256]{1,0:T(8,128)(2,1)S(1)} %constant_dynamic-slice_fusion.3), channel_id=1, source_target_pairs={{0,2},{1,3},{2,0},{3,1},{4,6},{5,7},{6,4},{7,5},{8,10},{9,11},{10,... | collective-permute-start | bytes 786440 | tf_op jit(solution)/shard_map/ppermute | solution.py:509
  14.8 40.0 %collective-permute-start.2 = (bf16[512,256]{1,0:T(8,128)(2,1)S(1)}, bf16[512,256]{1,0:T(8,128)(2,1)S(1)}, u32[]{:S(2)}, u32[]{:S(2)}) collective-permute-start(bf16[512,256]{1,0:T(8,128)(2,1)S(1)} %constant_dynamic-slice_fusion.3), channel_id=1, source_target_pairs={{0,1},{1,0},{2,3},{3,2},{4,5},{5,4},{6,7},{7,6},{8,9},{9,8},{10,11... | collective-permute-start | bytes 786440 | tf_op jit(solution)/shard_map/ppermute | solution.py:509
  15.9 40.5 %copy-start.30 = (s32[1,4]{1,0:T(1,128)S(1)}, s32[1,4]{1,0:T(1,128)}, u32[]{:S(2)}) copy-start(s32[1,4]{1,0:T(1,128)} %param.41) | copy-start | bytes 52
  15.9 40.8 %copy-start.11 = (bf16[2048,128]{1,0:T(8,128)(2,1)S(1)}, bf16[2048,128]{1,0:T(8,128)(2,1)}, u32[]{:S(2)}) copy-start(bf16[2048,128]{1,0:T(8,128)(2,1)} %param.35) | copy-start | bytes 1572868
  15.9 40.9 %copy-start.13 = (bf16[2048,128]{1,0:T(8,128)(2,1)S(1)}, bf16[2048,128]{1,0:T(8,128)(2,1)}, u32[]{:S(2)}) copy-start(bf16[2048,128]{1,0:T(8,128)(2,1)} %param.34) | copy-start | bytes 1572868
  56.0 118.6 %copy-start.7 = (bf16[2048,256]{1,0:T(8,128)(2,1)}, bf16[2048,256]{1,0:T(8,128)(2,1)S(1)}, u32[]{:S(2)}) copy-start(bf16[2048,256]{1,0:T(8,128)(2,1)S(1)} %pad_maximum_fusion.1.refs_0_) | copy-start | bytes 3145732
  56.0 14.6 %collective-permute-start.3 = (bf16[2048,256]{1,0:T(8,128)(2,1)S(1)}, bf16[2048,256]{1,0:T(8,128)(2,1)S(1)}, u32[]{:S(2)}, u32[]{:S(2)}) collective-permute-start(bf16[2048,256]{1,0:T(8,128)(2,1)S(1)} %pad_maximum_fusion.1.refs_0_), channel_id=1, source_target_pairs={{0,16},{4,12},{8,24},{12,4},{16,0},{20,28},{24,8},{28,20},{1,17},{... | collective-permute-start | bytes 3145736 | tf_op jit(solution)/shard_map/ppermute | solution.py:545
  58.4 27.5 %collective-permute-start.4 = (bf16[2048,256]{1,0:T(8,128)(2,1)S(1)}, bf16[2048,256]{1,0:T(8,128)(2,1)}, u32[]{:S(2)}, u32[]{:S(2)}) collective-permute-start(bf16[2048,256]{1,0:T(8,128)(2,1)S(1)} %pad_maximum_fusion.1.refs_0_), channel_id=1, source_target_pairs={{0,8},{4,20},{8,0},{12,28},{16,24},{20,4},{24,16},{28,12},{1,9},{5... | collective-permute-start | bytes 3145736 | tf_op jit(solution)/shard_map/ppermute | solution.py:545
  70.6 105.7 %copy-start.19 = (bf16[2048,256]{1,0:T(8,128)(2,1)}, bf16[2048,256]{1,0:T(8,128)(2,1)S(1)}, u32[]{:S(2)}) copy-start(bf16[2048,256]{1,0:T(8,128)(2,1)S(1)} %collective-permute-done.3.refs_1_) | copy-start | bytes 3145732
  70.6 24.3 %collective-permute-start.5 = (bf16[2048,256]{1,0:T(8,128)(2,1)S(1)}, bf16[2048,256]{1,0:T(8,128)(2,1)}, u32[]{:S(2)}, u32[]{:S(2)}) collective-permute-start(bf16[2048,256]{1,0:T(8,128)(2,1)S(1)} %collective-permute-done.3.refs_1_), channel_id=1, source_target_pairs={{0,8},{4,20},{8,0},{12,28},{16,24},{20,4},{24,16},{28,12},{1,9},{5... | collective-permute-start | bytes 3145736 | tf_op jit(solution)/shard_map/ppermute | solution.py:545
  104.5 115.1 %all-gather.10.cloned.1.call-start = ((), (), s32[]{:S(2)}) async-start(), calls=%async_computation.8 | async-start | bytes 2621440 | tf_op jit(solution)/shard_map/all_gather | solution.py:654
  114.4 62.5 %copy-start.28 = (s32[4]{0:T(128)S(1)}, s32[4]{0:T(128)}, u32[]{:S(2)}) copy-start(s32[4]{0:T(128)} %constant.43.clone) | copy-start | bytes 52
  174.4 92.0 %all-gather.12.cloned.1.call-start = ((), (), s32[]{:S(2)}) async-start(), calls=%async_computation.9 | async-start | bytes 2621440 | tf_op jit(solution)/shard_map/all_gather | solution.py:659
  174.6 4.1 collective-permute-start.6
  176.3 5.4 collective-permute-start.7
  176.4 5.5 collective-permute-start.8
  176.8 6.6 %collective-permute-start.9 = (bf16[2048,256]{1,0:T(8,128)(2,1)}, bf16[2048,256]{1,0:T(8,128)(2,1)}, u32[]{:S(2)}, u32[]{:S(2)}) collective-permute-start(bf16[2048,256]{1,0:T(8,128)(2,1)} %collective-permute-done.5.refs_3_), channel_id=1, source_target_pairs={{0,4},{4,0},{8,12},{12,8},{16,20},{20,16},{24,28},{28,24},{1,5},{5... | collective-permute-start | bytes 3145736 | tf_op jit(solution)/shard_map/ppermute | solution.py:552
  219.7 93.3 %all-gather.14.cloned.1.call-start = ((), (), s32[]{:S(2)}) async-start(), calls=%async_computation.10 | async-start | bytes 2621440 | tf_op jit(solution)/shard_map/all_gather | solution.py:660
  266.3 90.9 %reduce-scatter.5.cloned.1.call-start = ((), (), s32[]{:S(2)}) async-start(), calls=%async_computation.11 | async-start | bytes 2621440 | tf_op jit(solution)/shard_map/reduce_scatter | solution.py:558
  302.2 113.9 %reduce-scatter.7.cloned.1.call-start = ((), (), s32[]{:S(2)}) async-start(), calls=%async_computation.12 | async-start | bytes 2621440 | tf_op jit(solution)/shard_map/reduce_scatter | solution.py:558
  372.5 13.9 %collective-permute-start.10 = (bf16[4,256,4096]{2,1,0:T(8,128)(2,1)}, bf16[4,256,4096]{2,1,0:T(8,128)(2,1)}, u32[]{:S(2)}, u32[]{:S(2)}) collective-permute-start(bf16[4,256,4096]{2,1,0:T(8,128)(2,1)} %weight_grad.8), channel_id=1, source_target_pairs={{0,4},{4,0},{8,12},{12,8},{16,20},{20,16},{24,28},{28,24},{1,5},{5... | collective-permute-start | bytes 25165832 | tf_op jit(solution)/shard_map/ppermute | solution.py:569
  373.3 146.0 %reduce-scatter.9.cloned.1.call-start = ((), (), s32[]{:S(2)}) async-start(), calls=%async_computation.13 | async-start | bytes 5242880 | tf_op jit(solution)/shard_map/reduce_scatter | solution.py:679
  434.5 11.3 %collective-permute-start.12 = (bf16[4,256,2048]{2,1,0:T(8,128)(2,1)}, bf16[4,256,2048]{2,1,0:T(8,128)(2,1)}, u32[]{:S(2)}, u32[]{:S(2)}) collective-permute-start(bf16[4,256,2048]{2,1,0:T(8,128)(2,1)} %weight_grad.11), channel_id=1, source_target_pairs={{0,4},{4,0},{8,12},{12,8},{16,20},{20,16},{24,28},{28,24},{1,5},{5... | collective-permute-start | bytes 12582920 | tf_op jit(solution)/shard_map/ppermute | solution.py:569
  436.3 48.0 %collective-permute-start.11 = (bf16[2,256,4096]{2,1,0:T(8,128)(2,1)}, bf16[2,256,4096]{2,1,0:T(8,128)(2,1)}, u32[]{:S(2)}, u32[]{:S(2)}) collective-permute-start(bf16[2,256,4096]{2,1,0:T(8,128)(2,1)} %get-tuple-element.98), channel_id=1, source_target_pairs={{0,8},{4,20},{8,0},{12,28},{16,24},{20,4},{24,16},{28,12},{1,9},{5... | collective-permute-start | bytes 12582920 | tf_op jit(solution)/shard_map/ppermute | solution.py:580
  438.3 112.0 %collective-permute-start.14 = (bf16[4,256,2048]{2,1,0:T(8,128)(2,1)}, bf16[4,256,2048]{2,1,0:T(8,128)(2,1)}, u32[]{:S(2)}, u32[]{:S(2)}) collective-permute-start(bf16[4,256,2048]{2,1,0:T(8,128)(2,1)} %weight_grad.9), channel_id=1, source_target_pairs={{0,4},{4,0},{8,12},{12,8},{16,20},{20,16},{24,28},{28,24},{1,5},{5... | collective-permute-start | bytes 12582920 | tf_op jit(solution)/shard_map/ppermute | solution.py:569
  438.3 58.5 %all-to-all-start.1 = ((bf16[4,256,512]{2,1,0:T(8,128)(2,1)}), bf16[4,256,512]{2,1,0:T(8,128)(2,1)}, u32[]{:S(2)}, u32[]{:S(2)}) async-start(bf16[4,256,512]{2,1,0:T(8,128)(2,1)} %out_project_back.1), calls=%async_computation.4 | async-start | bytes 2097152 | tf_op jit(solution)/shard_map/all_to_all | solution.py:644
  445.8 198.6 %reduce-scatter.11.cloned.1.call-start = ((), (), s32[]{:S(2)}) async-start(), calls=%async_computation.14 | async-start | bytes 5242880 | tf_op jit(solution)/shard_map/reduce_scatter | solution.py:558
  445.8 38.4 %copy-start.18 = (bf16[2,256,4096]{2,1,0:T(8,128)(2,1)S(1)}, bf16[2,256,4096]{2,1,0:T(8,128)(2,1)}, u32[]{:S(2)}) copy-start(bf16[2,256,4096]{2,1,0:T(8,128)(2,1)} %get-tuple-element.104) | copy-start | bytes 12582916
  453.7 80.2 %collective-permute-start.23 = (bf16[2,256,2048]{2,1,0:T(8,128)(2,1)}, bf16[2,256,2048]{2,1,0:T(8,128)(2,1)}, u32[]{:S(2)}, u32[]{:S(2)}) collective-permute-start(bf16[2,256,2048]{2,1,0:T(8,128)(2,1)} %get-tuple-element.106), channel_id=1, source_target_pairs={{0,8},{4,20},{8,0},{12,28},{16,24},{20,4},{24,16},{28,12},{1,9},{5... | collective-permute-start | bytes 6291464 | tf_op jit(solution)/shard_map/ppermute | solution.py:580
  533.0 9.4 %collective-permute-start.13 = (bf16[4,256,768]{2,1,0:T(8,128)(2,1)}, bf16[4,256,768]{2,1,0:T(8,128)(2,1)S(1)}, u32[]{:S(2)}, u32[]{:S(2)}) collective-permute-start(bf16[4,256,768]{2,1,0:T(8,128)(2,1)} %weight_grad.13), channel_id=1, source_target_pairs={{0,4},{4,0},{8,12},{12,8},{16,20},{20,16},{24,28},{28,24},{1,5},{5... | collective-permute-start | bytes 4718600 | tf_op jit(solution)/shard_map/ppermute | solution.py:569
  533.6 43.1 %collective-permute-start.29 = (bf16[1,256,4096]{2,1,0:T(8,128)(2,1)}, bf16[1,256,4096]{2,1,0:T(8,128)(2,1)}, u32[]{:S(2)}, u32[]{:S(2)}) collective-permute-start(bf16[1,256,4096]{2,1,0:T(8,128)(2,1)} %get-tuple-element.163), channel_id=1, source_target_pairs={{0,16},{4,12},{8,24},{12,4},{16,0},{20,28},{24,8},{28,20},{1,17},{... | collective-permute-start | bytes 6291464 | tf_op jit(solution)/shard_map/ppermute | solution.py:580
  539.3 32.8 %collective-permute-start.24 = (bf16[1,256,2048]{2,1,0:T(8,128)(2,1)}, bf16[1,256,2048]{2,1,0:T(8,128)(2,1)}, u32[]{:S(2)}, u32[]{:S(2)}) collective-permute-start(bf16[1,256,2048]{2,1,0:T(8,128)(2,1)} %slice.149), channel_id=1, source_target_pairs={{0,16},{4,12},{8,24},{12,4},{16,0},{20,28},{24,8},{28,20},{1,17},{... | collective-permute-start | bytes 3145736 | tf_op jit(solution)/shard_map/ppermute | solution.py:580
  561.3 10.5 %collective-permute-start.15 = (f32[2,2048]{1,0:T(2,128)S(1)}, f32[2,2048]{1,0:T(2,128)S(1)}, u32[]{:S(2)}, u32[]{:S(2)}) collective-permute-start(f32[2,2048]{1,0:T(2,128)S(1)} %pad_maximum_fusion.6), channel_id=1, source_target_pairs={{0,24},{4,28},{8,16},{12,20},{16,8},{20,12},{24,0},{28,4},{1,25},{... | collective-permute-start | bytes 49160 | tf_op jit(solution)/shard_map/ppermute | solution.py:594
  562.8 9.2 %collective-permute-start.16 = (f32[2,2048]{1,0:T(2,128)S(1)}, f32[2,2048]{1,0:T(2,128)S(1)}, u32[]{:S(2)}, u32[]{:S(2)}) collective-permute-start(f32[2,2048]{1,0:T(2,128)S(1)} %pad_maximum_fusion.6), channel_id=1, source_target_pairs={{0,16},{4,20},{8,24},{12,28},{16,0},{20,4},{24,8},{28,12},{1,17},{... | collective-permute-start | bytes 49160 | tf_op jit(solution)/shard_map/ppermute | solution.py:594
  563.0 9.0 %collective-permute-start.17 = (f32[2,2048]{1,0:T(2,128)S(1)}, f32[2,2048]{1,0:T(2,128)S(1)}, u32[]{:S(2)}, u32[]{:S(2)}) collective-permute-start(f32[2,2048]{1,0:T(2,128)S(1)} %pad_maximum_fusion.6), channel_id=1, source_target_pairs={{0,8},{4,12},{8,0},{12,4},{16,24},{20,28},{24,16},{28,20},{1,9},{5... | collective-permute-start | bytes 49160 | tf_op jit(solution)/shard_map/ppermute | solution.py:594
  571.9 34.1 %collective-permute-start.25 = (bf16[2,256,2048]{2,1,0:T(8,128)(2,1)}, bf16[2,256,2048]{2,1,0:T(8,128)(2,1)S(1)}, u32[]{:S(2)}, u32[]{:S(2)}) collective-permute-start(bf16[2,256,2048]{2,1,0:T(8,128)(2,1)} %get-tuple-element.115), channel_id=1, source_target_pairs={{0,8},{4,20},{8,0},{12,28},{16,24},{20,4},{24,16},{28,12},{1,9},{5... | collective-permute-start | bytes 6291464 | tf_op jit(solution)/shard_map/ppermute | solution.py:580
  572.0 3.4 collective-permute-start.18
  574.1 31.3 %collective-permute-start.21 = (bf16[2,256,768]{2,1,0:T(8,128)(2,1)S(1)}, bf16[2,256,768]{2,1,0:T(8,128)(2,1)S(1)}, u32[]{:S(2)}, u32[]{:S(2)}) collective-permute-start(bf16[2,256,768]{2,1,0:T(8,128)(2,1)S(1)} %copy-done.29), channel_id=1, source_target_pairs={{0,8},{4,20},{8,0},{12,28},{16,24},{20,4},{24,16},{28,12},{1,9},{5... | collective-permute-start | bytes 2359304 | tf_op jit(solution)/shard_map/ppermute | solution.py:580
  575.5 4.2 collective-permute-start.19
  579.7 6.9 %collective-permute-start.20 = (f32[2,2048]{1,0:T(2,128)S(1)}, f32[2,2048]{1,0:T(2,128)S(1)}, u32[]{:S(2)}, u32[]{:S(2)}) collective-permute-start(f32[2,2048]{1,0:T(2,128)S(1)} %add.114), channel_id=1, source_target_pairs={{0,2},{1,3},{2,0},{3,1},{4,6},{5,7},{6,4},{7,5},{8,10},{9,11},{10,... | collective-permute-start | bytes 49160 | tf_op jit(solution)/shard_map/ppermute | solution.py:602
  605.6 8.8 %collective-permute-start.22 = (bf16[1,256,768]{2,1,0:T(8,128)(2,1)S(1)}, bf16[1,256,768]{2,1,0:T(8,128)(2,1)S(1)}, u32[]{:S(2)}, u32[]{:S(2)}) collective-permute-start(bf16[1,256,768]{2,1,0:T(8,128)(2,1)S(1)} %slice.144), channel_id=1, source_target_pairs={{0,16},{4,12},{8,24},{12,4},{16,0},{20,28},{24,8},{28,20},{1,17},{... | collective-permute-start | bytes 1179656 | tf_op jit(solution)/shard_map/ppermute | solution.py:580
  608.0 30.3 %collective-permute-start.30 = (bf16[1,256,2048]{2,1,0:T(8,128)(2,1)}, bf16[1,256,2048]{2,1,0:T(8,128)(2,1)}, u32[]{:S(2)}, u32[]{:S(2)}) collective-permute-start(bf16[1,256,2048]{2,1,0:T(8,128)(2,1)} %slice.154), channel_id=1, source_target_pairs={{0,16},{4,12},{8,24},{12,4},{16,0},{20,28},{24,8},{28,20},{1,17},{... | collective-permute-start | bytes 3145736 | tf_op jit(solution)/shard_map/ppermute | solution.py:580
  609.9 9.7 %collective-permute-start.26 = (bf16[256,512]{1,0:T(8,128)(2,1)S(1)}, bf16[256,512]{1,0:T(8,128)(2,1)S(1)}, u32[]{:S(2)}, u32[]{:S(2)}) collective-permute-start(bf16[256,512]{1,0:T(8,128)(2,1)S(1)} %get-tuple-element.164), channel_id=1, source_target_pairs={{0,1},{1,0},{2,3},{3,2},{4,5},{5,4},{6,7},{7,6},{8,9},{9,8},{10,11... | collective-permute-start | bytes 786440 | tf_op jit(solution)/shard_map/ppermute | solution.py:509
  611.6 19.5 %collective-permute-start.27 = (bf16[256,512]{1,0:T(8,128)(2,1)S(1)}, bf16[256,512]{1,0:T(8,128)(2,1)S(1)}, u32[]{:S(2)}, u32[]{:S(2)}) collective-permute-start(bf16[256,512]{1,0:T(8,128)(2,1)S(1)} %get-tuple-element.166), channel_id=1, source_target_pairs={{0,2},{1,3},{2,0},{3,1},{4,6},{5,7},{6,4},{7,5},{8,10},{9,11},{10,... | collective-permute-start | bytes 786440 | tf_op jit(solution)/shard_map/ppermute | solution.py:509
  614.2 21.2 %collective-permute-start.28 = (bf16[256,512]{1,0:T(8,128)(2,1)S(1)}, bf16[256,512]{1,0:T(8,128)(2,1)S(1)}, u32[]{:S(2)}, u32[]{:S(2)}) collective-permute-start(bf16[256,512]{1,0:T(8,128)(2,1)S(1)} %get-tuple-element.165), channel_id=1, source_target_pairs={{0,3},{1,2},{2,1},{3,0},{4,7},{5,6},{6,5},{7,4},{8,11},{9,10},{10,... | collective-permute-start | bytes 786440 | tf_op jit(solution)/shard_map/ppermute | solution.py:509
  (24 other events, 180.8 us)
Sparse Core Ops, SparseCore 0:
  11.4 93.0 all-gather.5
  106.6 64.2 all-gather.7
  174.5 45.1 all-gather.9
  221.6 44.6 all-gather.11
  268.3 44.6 all-gather.13
  315.1 42.0 reduce-scatter.4
  373.4 42.6 reduce-scatter.6
  418.4 100.8 reduce-scatter.8
  526.8 79.0 reduce-scatter.10

commit v3 on v2

--- a/solution.py
+++ b/solution.py
@@ -12,6 +12,7 @@
 LANES = 128
 VMEM_LIMIT = 56 * 1024 * 1024
 COST = pl.CostEstimate(flops=1, bytes_accessed=1, transcendentals=0)
+LONG_COST = pl.CostEstimate(flops=40_000_000_000, bytes_accessed=1, transcendentals=0)
 
 
 def dot_nn(a, b):
@@ -227,7 +228,7 @@
         out_shape=out,
         scratch_shapes=scratch,
         compiler_params=pltpu.CompilerParams(vmem_limit_bytes=VMEM_LIMIT),
-        cost_estimate=COST,
+        cost_estimate=LONG_COST,
         name="attend_back",
     )(*args)
 
@@ -401,7 +402,7 @@
 def mlp_back_call(dg, du, wg, wu):
     t, f = dg.shape
     d = wg.shape[0]
-    bn = min(256, d)
+    bn = min(512, d)
     held = pl.BlockSpec((t, f), lambda i: (0, 0), pipeline_mode=pl.Buffered(1))
     row = pl.BlockSpec((bn, f), lambda i: (i, 0))
     return pl.pallas_call(
@@ -673,12 +674,8 @@
     sent_gate_up = grads_sent(*gate_up, *here_wide)
     down = [after(dy_a, sent_gate_up), dy_b], [[m_a, m_b]]
     sent_down = grads_sent(*down, *here_wide)
-    gate_up = [after(full_a, sent_down), full_b], gate_up[1]
-    gate_up_sent, gate_up_kept = grads_kept(*gate_up, swap_cores(sent_gate_up, wide), *here_wide)
-    y = down_call(after(m_b, gate_up_sent), w_down, narrow, chunks, 1, y_a)
-    layer_sum = lax.psum_scatter(
-        after(y, grad_b).reshape(total_rows, width), "narrow", scatter_dimension=0, tiled=True
-    )
+    y = down_call(after(m_b, sent_down), w_down, narrow, chunks, 1, y_a)
+    layer_sum = scatter_narrow(after(y, grad_b).reshape(total_rows, width))
     unit_late = after(unit_two, y)
     grad_a, grad_b = grad_a.astype(jnp.float32), grad_b.astype(jnp.float32)
     scaled_grad = jnp.concatenate([grad_a, grad_b], axis=0)
@@ -689,45 +686,55 @@
     gain_two = jnp.sum(scaled_grad * unit_late, axis=0)
     low = back.astype(jnp.bfloat16)
     heads_grad = out_project_back(w_out_at, low, w_out_parts, narrow)
-    gate_up_kept = after(gate_up_kept, heads_grad)
+    got_gate_up = swap_cores(after(sent_gate_up, low), wide)
+    got_down = swap_cores(after(sent_down, low), wide)
+    gate_up = [after(full_a, heads_grad), full_b], gate_up[1]
+    gate_up_sent, gate_up_kept = grads_kept(*gate_up, got_gate_up, *here_wide)
+    down = [after(dy_a, gate_up_sent), dy_b], [[m_a, m_b]]
+    down_sent, down_kept = grads_kept(*down, got_down, *here_wide)
     heads_side = jnp.concatenate([heads_rows[j] for j in range(narrow)], axis=1)
-    out = [after(low, heads_grad)], [[heads_side]]
-    sent_out = grads_sent(*out, *here_wide)
-    out_sent, out_kept = grads_kept(*out, swap_cores(sent_out, wide), *here_wide)
-    gate_up_sum = halve(gate_up_sent, gate_up_kept, 0, wide).astype(jnp.bfloat16)
-    rest = gate_up_sum.shape[0] // 2
-    gate_up_kept, gate_up_sent = gate_up_sum[:rest], gate_up_sum[rest:]
     heads_grad = swap_heads(heads_grad)
     joined_grad = attend_back(
-        after(q, gate_up_sent, out_sent), k, v, start, heads_grad, heads, lse, None, tables, blocks, local_rows, kv,
-        group,
-    )
+        after(q, down_sent), k, v, start, heads_grad, heads, lse, None, tables, blocks, local_rows, kv, group
+    )
+    gate_up_got = swap_plane(gate_up_sent, 0, wide)
+    down_got = swap_plane(down_sent, 0, wide)
+
+    def halved(kept, got):
+        out = (kept.astype(jnp.float32) + got.astype(jnp.float32)).astype(jnp.bfloat16)
+        return out[: out.shape[0] // 2], out[out.shape[0] // 2 :]
+
     parts = mat_call(joined_grad, after(w_joined, layer_sum), True)
     normed_one_grad = scatter_narrow(parts).astype(jnp.float32)
+    out = [after(low, parts, gate_up_got, down_got)], [[heads_side]]
+    sent_out = grads_sent(*out, *here_wide)
+    gate_up_kept, gate_up_sent = halved(gate_up_kept, gate_up_got)
     gate_up_got = swap_plane(gate_up_sent, 1, wide)
-    joined = [after(full_one, parts)], [[joined_grad]]
+    joined = [after(full_one, sent_out)], [[joined_grad]]
     sent_joined = grads_sent(*joined, *here_wide)
-    parts_late, _ = lax.optimization_barrier((parts, sent_joined))
+    out = [after(low, sent_joined)], [[heads_side]]
+    out_sent, out_kept = grads_kept(*out, swap_cores(sent_out, wide), *here_wide)
+    down_kept, down_sent = halved(down_kept, down_got)
+    down_got = swap_plane(down_sent, 1, wide)
+    joined = [after(full_one, out_sent)], [[joined_grad]]
+    joined_sent, joined_kept = grads_kept(*joined, swap_cores(sent_joined, wide), *here_wide)
+    parts_late, _ = lax.optimization_barrier((parts, joined_sent))
     gain_one = jnp.sum(parts_late.astype(jnp.float32) * full_one.astype(jnp.float32), axis=0) / attn_gain
-    joined = [after(full_one, gain_one)], [[joined_grad]]
-    joined_sent, joined_kept = grads_kept(*joined, swap_cores(sent_joined, wide), *here_wide)
-    down = [after(dy_a, joined_sent), dy_b], [[m_a, m_b]]
-    down_sent, down_kept = grads_kept(*down, swap_cores(sent_down, wide), *here_wide)
-    gains = sum_column(sum_plane(after(jnp.stack([gain_one, gain_two]), down_sent), wide), narrow, wide)
-    out_sum = halve(out_sent, after(out_kept, parts), 0, wide)
+    gains = sum_column(sum_plane(jnp.stack([gain_one, gain_two]), wide), narrow, wide)
+    gate_up_sum = after(gate_up_kept, joined_sent).astype(jnp.float32) + gate_up_got.astype(jnp.float32)
+    down_sum = after(down_kept, joined_sent).astype(jnp.float32) + down_got.astype(jnp.float32)
     joined_got = swap_plane(joined_sent, 0, wide)
-    down_got = swap_plane(down_sent, 0, wide)
-    gate_up_sum = after(gate_up_kept, down_sent).astype(jnp.float32) + gate_up_got.astype(jnp.float32)
+    out_got = swap_plane(out_sent, 0, wide)
     joined_sum = joined_kept.astype(jnp.float32) + joined_got.astype(jnp.float32)
-    down_sum = down_kept.astype(jnp.float32) + down_got.astype(jnp.float32)
+    out_sum = out_kept.astype(jnp.float32) + out_got.astype(jnp.float32)
     for step in range(1, wide.bit_length() - 2):
-        out_sum, joined_sum, down_sum = (
-            halve_again(x.astype(jnp.bfloat16), step, wide) for x in (out_sum, joined_sum, down_sum)
-        )
+        out_sum, joined_sum = (halve_again(x.astype(jnp.bfloat16), step, wide) for x in (out_sum, joined_sum))
         if step > 1:
-            gate_up_sum = halve_again(gate_up_sum.astype(jnp.bfloat16), step, wide)
+            gate_up_sum, down_sum = (
+                halve_again(x.astype(jnp.bfloat16), step, wide) for x in (gate_up_sum, down_sum)
+            )
     gate_up_sum, down_sum, out_sum, joined_sum = gate_up_sum[0], down_sum[0], out_sum[0], joined_sum[0]
-    out_sum = after(out_sum.astype(jnp.bfloat16), joined_got, down_got)
+    out_sum = out_sum.astype(jnp.bfloat16)
     got = swap_blocks(
         lambda j: lax.dynamic_slice_in_dim(out_sum, j * query_width, query_width, 1), here, narrow
     )

time: 665 us -> 658 us (0.989)
  the two profiles are of different devices: /device:TPU:11 before, /device:TPU:0 now
where the time goes in v3:
time: 658 us; the launch traced here: 653 us
  waiting for transfers between devices  245 us (37%)
  Pallas kernels  231 us (35%)
  other arithmetic  46.9 us (7%)
  blocking collectives  45.7 us (7%)
  starting transfers between devices  40.9 us (6%)
  local copies, waits for them, and re-layouts  27.7 us (4%)
  between operations  14.6 us (2%)
    pallas_call x8, Pallas kernels, grad_call(): pl.pallas_call(functools.partial(grad_body, nl, nr, got), grid_spec=pltpu...  81.5 us
    ppermute x6, waiting for transfers between devices, swap_blocks(): lax.ppermute(block(index ^ k), 'narrow', [(i, i ^ k) for i in range(size)])  68.6 us
    all_gather x1, waiting for transfers between devices, on_device(): full_a = lax.all_gather(normed_a, 'narrow', axis=0, tiled=True)  46.6 us
    all_to_all x1, blocking collectives, swap_heads(): lax.all_to_all(x.reshape(total_rows, query_width), 'narrow', 0, 0, tiled=...  45.7 us
    pallas_call x2, Pallas kernels, mlp_call(): pl.pallas_call(mlp_body, grid=(f // bf,), in_specs=[held, held, col, col,...  41.2 us
    reduce_scatter x4, waiting for transfers between devices, scatter_narrow(): return lax.psum_scatter(parts, 'narrow', scatter_dimension=0, tiled=True)  34.1 us
    pallas_call x2, Pallas kernels, mlp_back_call(): pl.pallas_call(mlp_back_body, grid=(d // bn,), in_specs=[held, held, row,...  27.9 us
    all_gather x1, waiting for transfers between devices, on_device(): lax.all_gather(after(upstream[r:], heads_rows), 'narrow', axis=0, tiled=T...  25.3 us
  transfers between devices with their start and end apart: 41, of which 22 were waited for; matrix products, arithmetic and copies ran while one was open for 10% of the time, Pallas kernels for 35%

profile of v3, /device:TPU:0, one launch (start us, length us, event | category | flops | bytes accessed | tf_op | source)
XLA Modules:
  0.0 652.5 jit_solution(17595602908480233096)
XLA Ops:
  12.9 5.1 collective-permute-start
  18.6 7.2 %collective-permute-done = bf16[512,256]{1,0:T(8,128)(2,1)S(1)} collective-permute-done((bf16[512,256]{1,0:T(8,128)(2,1)S(1)}, bf16[512,256]{1,0:T(8,128)(2,1)S(1)}, u32[]{:S(2)}, u32[]{:S(2)}) %collective-permute-start) | collective-permute-done | bytes 262176 | tf_op jit(solution)/shard_map/ppermute | solution.py:510
  25.9 42.7 %collective-permute-done.1 = bf16[512,256]{1,0:T(8,128)(2,1)S(1)} collective-permute-done((bf16[512,256]{1,0:T(8,128)(2,1)S(1)}, bf16[512,256]{1,0:T(8,128)(2,1)S(1)}, u32[]{:S(2)}, u32[]{:S(2)}) %collective-permute-start.1) | collective-permute-done | bytes 262176 | tf_op jit(solution)/shard_map/ppermute | solution.py:510
  75.0 21.1 %collective-permute-done.3.refs_1_ = bf16[2048,256]{1,0:T(8,128)(2,1)S(1)} collective-permute-done((bf16[2048,256]{1,0:T(8,128)(2,1)S(1)}, bf16[2048,256]{1,0:T(8,128)(2,1)S(1)}, u32[]{:S(2)}, u32[]{:S(2)}) %collective-permute-start.3) | collective-permute-done | bytes 1048608 | tf_op jit(solution)/shard_map/ppermute | solution.py:546
  97.6 8.1 %concatenate.29.w_ref = bf16[2048,1024]{1,0:T(8,128)(2,1)} concatenate(bf16[2048,512]{1,0:T(8,128)(2,1)} %param.33, bf16[2048,64]{1,0:T(8,128)(2,1)} %get-tuple-element.196, bf16[2048,128]{1,0:T(8,128)(2,1)S(1)} %copy-done.9, bf16[2048,64]{1,0:T(8,128)(2,1)} %get-tuple-element.197, bf16[2048,64]{1,0:T(8,128)(2,1)} %get-tuple-element.186, bf16[2048,128]{1,0:T(8,128)(2,1)S(1)} %copy-done.8, ...), dimensions={1} | concatenate | bytes 8388608 | tf_op jit(solution)/shard_map/concatenate | solution.py:623
  112.0 9.0 %qkv.1 = (bf16[1024,512]{1,0:T(8,128)(2,1)}, bf16[1024,256]{1,0:T(8,128)(2,1)}, bf16[1024,256]{1,0:T(8,128)(2,1)}) custom-call(bf16[1024,2048]{1,0:T(8,128)(2,1)} %all-gather.6.cloned.1.call-done.x_ref.refs_0_, bf16[2048,1024]{1,0:T(8,128)(2,1)} %concatenate.29.w_ref, f32[1024,128]{1,0:T(8,128)} %get-tuple-element.69.cos_ref.refs_7_, ...), custom_call_target="tpu_custom_call" | custom-call | flops 1 | bytes 1 | tf_op jit(solution)/shard_map/qkv/pallas_call | solution.py:59
  121.0 12.1 %attend.1 = (bf16[1024,512]{1,0:T(8,128)(2,1)}, f32[2,4,1024]{2,1,0:T(4,128)}) custom-call(bf16[1024,512]{1,0:T(8,128)(2,1)} %get-tuple-element.107.q_ref.refs_0_, bf16[1024,256]{1,0:T(8,128)(2,1)} %get-tuple-element.72.k_ref.refs_1_, bf16[1024,256]{1,0:T(8,128)(2,1)} %get-tuple-element.73.v_ref.refs_2_, s32[4,1024]{1,0:T(4,128)} %bitcast.51), custom_call_target="tpu_custom_call" | custom-call | flops 1 | bytes 1 | tf_op jit(solution)/shard_map/attend/pallas_call | solution.py:126
  133.1 45.7 %all_to_all.17.x_ref = bf16[4,256,512]{2,1,0:T(8,128)(2,1)} all-to-all(bf16[4,256,512]{2,1,0:T(8,128)(2,1)} %bitcast.46), channel_id=1, replica_groups=mesh['wide'=8,'narrow'=4] {'narrow'}, dimensions={0} | all-to-all | bytes 2097152 | tf_op jit(solution)/shard_map/all_to_all | solution.py:645
  182.3 3.0 collective-permute-done.7.refs_5_
  187.0 7.4 %out_project.1 = f32[256,2048]{1,0:T(8,128)} custom-call(s32[8]{0:T(128)} %pad_add_fusion.at_ref, bf16[4,256,512]{2,1,0:T(8,128)(2,1)} %all_to_all.17.x_ref, bf16[2048,256]{1,0:T(8,128)(2,1)} %copy-done.7, bf16[2048,256]{1,0:T(8,128)(2,1)} %copy-done.17, bf16[2048,256]{1,0:T(8,128)(2,1)} %collective-permute-done.4.refs_2_, ...), custom_call_target="tpu_custom_call" | custom-call | flops 1 | bytes 1 | tf_op jit(solution)/shard_map/out_project/pallas_call | solution.py:311
  198.3 25.3 %all-gather.10.cloned.1.call-done.dy_ref.refs_1_ = bf16[512,2048]{1,0:T(8,128)(2,1)} async-done(((bf16[128,2048]{1,0:T(8,128)(2,1)}), bf16[512,2048]{1,0:T(8,128)(2,1)}) %all-gather.10.cloned.1.call-update) | async-done | bytes 2097168 | tf_op jit(solution)/shard_map/all_gather | solution.py:655
  223.6 46.6 %all-gather.12.cloned.1.call-done.x_ref.refs_0_ = bf16[512,2048]{1,0:T(8,128)(2,1)} async-done(((bf16[128,2048]{1,0:T(8,128)(2,1)}), bf16[512,2048]{1,0:T(8,128)(2,1)}) %all-gather.12.cloned.1.call-update) | async-done | bytes 2097168 | tf_op jit(solution)/shard_map/all_gather | solution.py:660
  270.3 20.5 %mlp.2 = (bf16[512,2048]{1,0:T(8,128)(2,1)}, bf16[512,2048]{1,0:T(8,128)(2,1)}, bf16[512,2048]{1,0:T(8,128)(2,1)}) custom-call(bf16[512,2048]{1,0:T(8,128)(2,1)} %all-gather.12.cloned.1.call-done.x_ref.refs_0_, bf16[512,2048]{1,0:T(8,128)(2,1)} %all-gather.8.cloned.1.call-done.dy_ref.refs_0_, bf16[2048,2048]{1,0:T(8,128)(2,1)} %wg_ref.7, ...), custom_call_target="tpu_custom_call" | custom-call | flops 1 | bytes 1 | tf_op jit(solution)/shard_map/mlp/pallas_call | solution.py:386
  290.9 13.9 %mlp_back.2 = bf16[512,2048]{1,0:T(8,128)(2,1)} custom-call(bf16[512,2048]{1,0:T(8,128)(2,1)} %get-tuple-element.87.dg_ref.refs_2_, bf16[512,2048]{1,0:T(8,128)(2,1)} %get-tuple-element.88.du_ref.refs_4_, bf16[2048,2048]{1,0:T(8,128)(2,1)} %wg_ref.7, bf16[2048,2048]{1,0:T(8,128)(2,1)} %wu_ref.7), custom_call_target="tpu_custom_call" | custom-call | flops 1 | bytes 1 | tf_op jit(solution)/shard_map/mlp_back/pallas_call | solution.py:408
  304.9 8.8 %down.2.refs_0_ = bf16[4,2,128,2048]{3,2,1,0:T(8,128)(2,1)} custom-call(bf16[512,2048]{1,0:T(8,128)(2,1)} %get-tuple-element.89.x_ref.refs_2_, bf16[2048,2048]{1,0:T(8,128)(2,1)} %w_ref.3), custom_call_target="tpu_custom_call" | custom-call | flops 1 | bytes 1 | tf_op jit(solution)/shard_map/down/pallas_call | solution.py:451
  313.7 3.3 all-gather.14.cloned.1.call-done.x_ref.refs_1_
  316.9 20.6 %mlp.3 = (bf16[512,2048]{1,0:T(8,128)(2,1)}, bf16[512,2048]{1,0:T(8,128)(2,1)}, bf16[512,2048]{1,0:T(8,128)(2,1)}) custom-call(bf16[512,2048]{1,0:T(8,128)(2,1)} %all-gather.14.cloned.1.call-done.x_ref.refs_1_, bf16[512,2048]{1,0:T(8,128)(2,1)} %all-gather.10.cloned.1.call-done.dy_ref.refs_1_, bf16[2048,2048]{1,0:T(8,128)(2,1)} %wg_ref.7, ...), custom_call_target="tpu_custom_call" | custom-call | flops 1 | bytes 1 | tf_op jit(solution)/shard_map/mlp/pallas_call | solution.py:386
  337.6 14.0 %mlp_back.3 = bf16[512,2048]{1,0:T(8,128)(2,1)} custom-call(bf16[512,2048]{1,0:T(8,128)(2,1)} %get-tuple-element.92.dg_ref.refs_3_, bf16[512,2048]{1,0:T(8,128)(2,1)} %get-tuple-element.93.du_ref.refs_5_, bf16[2048,2048]{1,0:T(8,128)(2,1)} %wg_ref.7, bf16[2048,2048]{1,0:T(8,128)(2,1)} %wu_ref.7), custom_call_target="tpu_custom_call" | custom-call | flops 1 | bytes 1 | tf_op jit(solution)/shard_map/mlp_back/pallas_call | solution.py:408
  351.5 10.1 %reduce-scatter.5.cloned.1.call-done = bf16[128,2048]{1,0:T(8,128)(2,1)} async-done(((bf16[512,2048]{1,0:T(8,128)(2,1)}), bf16[128,2048]{1,0:T(8,128)(2,1)}) %reduce-scatter.5.cloned.1.call-update) | async-done | bytes 524304 | tf_op jit(solution)/shard_map/reduce_scatter | solution.py:559
  361.9 15.2 %weight_grad.8 = bf16[4,256,4096]{2,1,0:T(8,128)(2,1)} custom-call(s32[4]{0:T(128)} %copy-done.27, bf16[512,2048]{1,0:T(8,128)(2,1)} %all-gather.12.cloned.1.call-done.x_ref.refs_0_, bf16[512,2048]{1,0:T(8,128)(2,1)} %all-gather.14.cloned.1.call-done.x_ref.refs_1_, bf16[512,2048]{1,0:T(8,128)(2,1)} %get-tuple-element.87.dg_ref.refs_2_, ...), custom_call_target="tpu_custom_call" | custom-call | flops 1 | bytes 1 | tf_op jit(solution)/shard_map/weight_grad/pallas_call | solution.py:286
  377.2 9.5 %weight_grad.9 = bf16[4,256,2048]{2,1,0:T(8,128)(2,1)} custom-call(s32[4]{0:T(128)} %copy-done.27, bf16[512,2048]{1,0:T(8,128)(2,1)} %all-gather.8.cloned.1.call-done.dy_ref.refs_0_, bf16[512,2048]{1,0:T(8,128)(2,1)} %all-gather.10.cloned.1.call-done.dy_ref.refs_1_, bf16[512,2048]{1,0:T(8,128)(2,1)} %get-tuple-element.89.x_ref.refs_2_, ...), custom_call_target="tpu_custom_call" | custom-call | flops 1 | bytes 1 | tf_op jit(solution)/shard_map/weight_grad/pallas_call | solution.py:286
  386.7 8.8 %down.3 = bf16[4,2,128,2048]{3,2,1,0:T(8,128)(2,1)} custom-call(bf16[512,2048]{1,0:T(8,128)(2,1)} %get-tuple-element.97.refs_3_.x_ref, bf16[2048,2048]{1,0:T(8,128)(2,1)} %w_ref.3, bf16[4,2,128,2048]{3,2,1,0:T(8,128)(2,1)} %down.2.refs_0_), custom_call_target="tpu_custom_call", output_to_operand_aliasing={{}: (2, {})} | custom-call | flops 1 | bytes 1 | tf_op jit(solution)/shard_map/down/pallas_call | solution.py:451
  395.5 11.8 %reduce-scatter.7.cloned.1.call-done = bf16[128,2048]{1,0:T(8,128)(2,1)} async-done(((bf16[512,2048]{1,0:T(8,128)(2,1)}), bf16[128,2048]{1,0:T(8,128)(2,1)}) %reduce-scatter.7.cloned.1.call-update) | async-done | bytes 524304 | tf_op jit(solution)/shard_map/reduce_scatter | solution.py:559
  411.5 7.1 %out_project_back.1 = bf16[4,256,512]{2,1,0:T(8,128)(2,1)} custom-call(s32[8]{0:T(128)} %pad_add_fusion.at_ref, bf16[256,2048]{1,0:T(8,128)(2,1)} %fusion.22.x_ref.refs_0_, bf16[2048,256]{1,0:T(8,128)(2,1)} %copy-done.7, bf16[2048,256]{1,0:T(8,128)(2,1)} %copy-done.17, bf16[2048,256]{1,0:T(8,128)(2,1)} %collective-permute-done.4.refs_2_, ...), custom_call_target="tpu_custom_call" | custom-call | flops 1 | bytes 1 | tf_op jit(solution)/shard_map/out_project_back/pallas_call | solution.py:336
  418.6 4.3 all-to-all-start.1
  422.9 3.9 pad_maximum_fusion.w_ref
  426.9 18.3 %weight_grad.10 = (bf16[2,256,4096]{2,1,0:T(8,128)(2,1)}, bf16[2,256,4096]{2,1,0:T(8,128)(2,1)}) custom-call(s32[4]{0:T(128)} %copy-done.26, bf16[512,2048]{1,0:T(8,128)(2,1)} %all-gather.12.cloned.1.call-done.x_ref.refs_0_, bf16[512,2048]{1,0:T(8,128)(2,1)} %all-gather.14.cloned.1.call-done.x_ref.refs_1_, ...), custom_call_target="tpu_custom_call" | custom-call | flops 1 | bytes 1 | tf_op jit(solution)/shard_map/weight_grad/pallas_call | solution.py:286
  446.6 11.0 %weight_grad.11 = (bf16[2,256,2048]{2,1,0:T(8,128)(2,1)}, bf16[2,256,2048]{2,1,0:T(8,128)(2,1)}) custom-call(s32[4]{0:T(128)} %copy-done.26, bf16[512,2048]{1,0:T(8,128)(2,1)} %all-gather.8.cloned.1.call-done.dy_ref.refs_0_, bf16[512,2048]{1,0:T(8,128)(2,1)} %all-gather.10.cloned.1.call-done.dy_ref.refs_1_, ...), custom_call_target="tpu_custom_call" | custom-call | flops 1 | bytes 1 | tf_op jit(solution)/shard_map/weight_grad/pallas_call | solution.py:286
  458.3 18.5 %all-to-all-done.1 = bf16[4,256,512]{2,1,0:T(8,128)(2,1)} async-done(((bf16[4,256,512]{2,1,0:T(8,128)(2,1)}), bf16[4,256,512]{2,1,0:T(8,128)(2,1)}, u32[]{:S(2)}, u32[]{:S(2)}) %all-to-all-start.1) | async-done | bytes 1048608 | tf_op jit(solution)/shard_map/all_to_all | solution.py:645
  476.9 20.4 %attend_back.1.x_ref.refs_1_ = bf16[1024,768]{1,0:T(8,128)(2,1)} custom-call(bf16[1024,512]{1,0:T(8,128)(2,1)} %get-tuple-element.107.q_ref.refs_0_, bf16[1024,256]{1,0:T(8,128)(2,1)} %get-tuple-element.72.k_ref.refs_1_, bf16[1024,256]{1,0:T(8,128)(2,1)} %get-tuple-element.73.v_ref.refs_2_, s32[4,1024]{1,0:T(4,128)} %bitcast.52, ...), custom_call_target="tpu_custom_call" | custom-call | flops 40000000000 | bytes 1 | tf_op jit(solution)/shard_map/attend_back/pallas_call | solution.py:226
  497.2 6.9 %reduce-scatter.9.cloned.1.call-done = bf16[256,2048]{1,0:T(8,128)(2,1)} async-done(((bf16[1024,2048]{1,0:T(8,128)(2,1)}), bf16[256,2048]{1,0:T(8,128)(2,1)}) %reduce-scatter.9.cloned.1.call-update) | async-done | bytes 1048592 | tf_op jit(solution)/shard_map/reduce_scatter | solution.py:559
  504.1 7.3 %product.1 = bf16[1024,2048]{1,0:T(8,128)(2,1)} custom-call(bf16[1024,768]{1,0:T(8,128)(2,1)} %attend_back.1.x_ref.refs_1_, bf16[2048,768]{1,0:T(8,128)(2,1)} %pad_maximum_fusion.w_ref), custom_call_target="tpu_custom_call" | custom-call | flops 1 | bytes 1 | tf_op jit(solution)/shard_map/product/pallas_call | solution.py:429
  516.5 5.9 weight_grad.12
  522.3 6.9 %weight_grad.13 = bf16[4,256,768]{2,1,0:T(8,128)(2,1)} custom-call(s32[4]{0:T(128)} %copy-done.27, bf16[1024,2048]{1,0:T(8,128)(2,1)} %all-gather.6.cloned.1.call-done.x_ref.refs_0_, bf16[1024,768]{1,0:T(8,128)(2,1)} %attend_back.1.x_ref.refs_1_), custom_call_target="tpu_custom_call" | custom-call | flops 1 | bytes 1 | tf_op jit(solution)/shard_map/weight_grad/pallas_call | solution.py:286
  529.3 3.7 add_convert_fusion
  537.0 3.0 add_convert_fusion.1
  541.9 7.2 %weight_grad.14 = (bf16[2,256,2048]{2,1,0:T(8,128)(2,1)}, bf16[2,256,2048]{2,1,0:T(8,128)(2,1)}) custom-call(s32[4]{0:T(128)} %copy-done.26, bf16[256,2048]{1,0:T(8,128)(2,1)} %fusion.22.x_ref.refs_0_, bf16[256,2048]{1,0:T(8,128)(2,1)} %pad_maximum_fusion.3.refs_1_, bf16[4,256,2048]{2,1,0:T(8,128)(2,1)} %collective-permute-done.14.refs_2_), custom_call_target="tpu_custom_call" | custom-call | flops 1 | bytes 1 | tf_op jit(solution)/shard_map/weight_grad/pallas_call | solution.py:286
  549.1 7.4 %weight_grad.15 = (bf16[2,256,768]{2,1,0:T(8,128)(2,1)}, bf16[2,256,768]{2,1,0:T(8,128)(2,1)}) custom-call(s32[4]{0:T(128)} %copy-done.26, bf16[1024,2048]{1,0:T(8,128)(2,1)} %all-gather.6.cloned.1.call-done.x_ref.refs_0_, bf16[1024,768]{1,0:T(8,128)(2,1)} %attend_back.1.x_ref.refs_1_, bf16[4,256,768]{2,1,0:T(8,128)(2,1)} %collective-permute-done.15.refs_2_), custom_call_target="tpu_custom_call" | custom-call | flops 1 | bytes 1 | tf_op jit(solution)/shard_map/weight_grad/pallas_call | solution.py:286
  556.5 4.1 multiply_reduce_fusion
  570.5 9.6 %collective-permute-done.30 = bf16[1,256,2048]{2,1,0:T(8,128)(2,1)} collective-permute-done((bf16[1,256,2048]{2,1,0:T(8,128)(2,1)}, bf16[1,256,2048]{2,1,0:T(8,128)(2,1)}, u32[]{:S(2)}, u32[]{:S(2)}) %collective-permute-start.30) | collective-permute-done | bytes 1048608 | tf_op jit(solution)/shard_map/ppermute | solution.py:581
  581.8 2.9 add_bitcast_fusion.1
  584.7 2.9 copy.48
  587.8 5.3 reduce-scatter.11.cloned.1.call-done
  598.8 3.0 collective-permute-start.21
  606.1 3.1 fusion.13
  612.7 6.7 %collective-permute-done.25 = bf16[1,256,2048]{2,1,0:T(8,128)(2,1)S(1)} collective-permute-done((bf16[1,256,2048]{2,1,0:T(8,128)(2,1)S(1)}, bf16[1,256,2048]{2,1,0:T(8,128)(2,1)S(1)}, u32[]{:S(2)}, u32[]{:S(2)}) %collective-permute-start.25) | collective-permute-done | bytes 1048608 | tf_op jit(solution)/shard_map/ppermute | solution.py:581
  626.0 5.0 collective-permute-done.28
  631.0 13.7 %collective-permute-done.27 = bf16[256,512]{1,0:T(8,128)(2,1)S(1)} collective-permute-done((bf16[256,512]{1,0:T(8,128)(2,1)S(1)}, bf16[256,512]{1,0:T(8,128)(2,1)S(1)}, u32[]{:S(2)}, u32[]{:S(2)}) %collective-permute-start.27) | collective-permute-done | bytes 262176 | tf_op jit(solution)/shard_map/ppermute | solution.py:510
  (186 shorter events, 79.7 us)
Async XLA Ops:
  7.2 103.8 %all-gather.6.cloned.1.call-start = ((), (), s32[]{:S(2)}) async-start(), calls=%async_computation.6 | async-start | bytes 5242880 | tf_op jit(solution)/shard_map/all_gather | solution.py:631
  11.8 169.3 %all-gather.8.cloned.1.call-start = ((), (), s32[]{:S(2)}) async-start(), calls=%async_computation.7 | async-start | bytes 2621440 | tf_op jit(solution)/shard_map/all_gather | solution.py:641
  12.9 13.0 %collective-permute-start = (bf16[512,256]{1,0:T(8,128)(2,1)S(1)}, bf16[512,256]{1,0:T(8,128)(2,1)S(1)}, u32[]{:S(2)}, u32[]{:S(2)}) collective-permute-start(bf16[512,256]{1,0:T(8,128)(2,1)S(1)} %constant_dynamic-slice_fusion), channel_id=1, source_target_pairs={{0,3},{1,2},{2,1},{3,0},{4,7},{5,6},{6,5},{7,4},{8,11},{9,10},{10,... | collective-permute-start | bytes 786440 | tf_op jit(solution)/shard_map/ppermute | solution.py:510
  18.0 50.6 %collective-permute-start.1 = (bf16[512,256]{1,0:T(8,128)(2,1)S(1)}, bf16[512,256]{1,0:T(8,128)(2,1)S(1)}, u32[]{:S(2)}, u32[]{:S(2)}) collective-permute-start(bf16[512,256]{1,0:T(8,128)(2,1)S(1)} %constant_dynamic-slice_fusion), channel_id=1, source_target_pairs={{0,2},{1,3},{2,0},{3,1},{4,6},{5,7},{6,4},{7,5},{8,10},{9,11},{10,... | collective-permute-start | bytes 786440 | tf_op jit(solution)/shard_map/ppermute | solution.py:510
  18.0 50.6 %collective-permute-start.2 = (bf16[512,256]{1,0:T(8,128)(2,1)S(1)}, bf16[512,256]{1,0:T(8,128)(2,1)S(1)}, u32[]{:S(2)}, u32[]{:S(2)}) collective-permute-start(bf16[512,256]{1,0:T(8,128)(2,1)S(1)} %constant_dynamic-slice_fusion), channel_id=1, source_target_pairs={{0,1},{1,0},{2,3},{3,2},{4,5},{5,4},{6,7},{7,6},{8,9},{9,8},{10,11... | collective-permute-start | bytes 786440 | tf_op jit(solution)/shard_map/ppermute | solution.py:510
  18.6 52.9 %copy-start.29 = (s32[1,4]{1,0:T(1,128)S(1)}, s32[1,4]{1,0:T(1,128)}, u32[]{:S(2)}) copy-start(s32[1,4]{1,0:T(1,128)} %param.41) | copy-start | bytes 52
  18.6 53.2 %copy-start.8 = (bf16[2048,128]{1,0:T(8,128)(2,1)S(1)}, bf16[2048,128]{1,0:T(8,128)(2,1)}, u32[]{:S(2)}) copy-start(bf16[2048,128]{1,0:T(8,128)(2,1)} %param.35) | copy-start | bytes 1572868
  18.6 53.2 %copy-start.9 = (bf16[2048,128]{1,0:T(8,128)(2,1)S(1)}, bf16[2048,128]{1,0:T(8,128)(2,1)}, u32[]{:S(2)}) copy-start(bf16[2048,128]{1,0:T(8,128)(2,1)} %param.34) | copy-start | bytes 1572868
  69.9 109.6 %copy-start.7 = (bf16[2048,256]{1,0:T(8,128)(2,1)}, bf16[2048,256]{1,0:T(8,128)(2,1)S(1)}, u32[]{:S(2)}) copy-start(bf16[2048,256]{1,0:T(8,128)(2,1)S(1)} %pad_maximum_fusion.1.refs_0_) | copy-start | bytes 3145732
  69.9 26.2 %collective-permute-start.3 = (bf16[2048,256]{1,0:T(8,128)(2,1)S(1)}, bf16[2048,256]{1,0:T(8,128)(2,1)S(1)}, u32[]{:S(2)}, u32[]{:S(2)}) collective-permute-start(bf16[2048,256]{1,0:T(8,128)(2,1)S(1)} %pad_maximum_fusion.1.refs_0_), channel_id=1, source_target_pairs={{0,16},{4,12},{8,24},{12,4},{16,0},{20,28},{24,8},{28,20},{1,17},{... | collective-permute-start | bytes 3145736 | tf_op jit(solution)/shard_map/ppermute | solution.py:546
  73.5 37.0 %collective-permute-start.4 = (bf16[2048,256]{1,0:T(8,128)(2,1)S(1)}, bf16[2048,256]{1,0:T(8,128)(2,1)}, u32[]{:S(2)}, u32[]{:S(2)}) collective-permute-start(bf16[2048,256]{1,0:T(8,128)(2,1)S(1)} %pad_maximum_fusion.1.refs_0_), channel_id=1, source_target_pairs={{0,8},{4,20},{8,0},{12,28},{16,24},{20,4},{24,16},{28,12},{1,9},{5... | collective-permute-start | bytes 3145736 | tf_op jit(solution)/shard_map/ppermute | solution.py:546
  96.1 83.5 %copy-start.17 = (bf16[2048,256]{1,0:T(8,128)(2,1)}, bf16[2048,256]{1,0:T(8,128)(2,1)S(1)}, u32[]{:S(2)}) copy-start(bf16[2048,256]{1,0:T(8,128)(2,1)S(1)} %collective-permute-done.3.refs_1_) | copy-start | bytes 3145732
  96.1 14.9 %collective-permute-start.5 = (bf16[2048,256]{1,0:T(8,128)(2,1)S(1)}, bf16[2048,256]{1,0:T(8,128)(2,1)}, u32[]{:S(2)}, u32[]{:S(2)}) collective-permute-start(bf16[2048,256]{1,0:T(8,128)(2,1)S(1)} %collective-permute-done.3.refs_1_), channel_id=1, source_target_pairs={{0,8},{4,20},{8,0},{12,28},{16,24},{20,4},{24,16},{28,12},{1,9},{5... | collective-permute-start | bytes 3145736 | tf_op jit(solution)/shard_map/ppermute | solution.py:546
  111.0 112.6 %all-gather.10.cloned.1.call-start = ((), (), s32[]{:S(2)}) async-start(), calls=%async_computation.8 | async-start | bytes 2621440 | tf_op jit(solution)/shard_map/all_gather | solution.py:655
  121.0 59.6 %copy-start.28 = (s32[4]{0:T(128)S(1)}, s32[4]{0:T(128)}, u32[]{:S(2)}) copy-start(s32[4]{0:T(128)} %constant.47.clone) | copy-start | bytes 52
  178.9 91.4 %all-gather.12.cloned.1.call-start = ((), (), s32[]{:S(2)}) async-start(), calls=%async_computation.9 | async-start | bytes 2621440 | tf_op jit(solution)/shard_map/all_gather | solution.py:660
  179.5 2.9 collective-permute-start.6
  179.6 5.8 collective-permute-start.7
  180.1 5.5 collective-permute-start.8
  180.1 6.9 %collective-permute-start.9 = (bf16[2048,256]{1,0:T(8,128)(2,1)}, bf16[2048,256]{1,0:T(8,128)(2,1)}, u32[]{:S(2)}, u32[]{:S(2)}) collective-permute-start(bf16[2048,256]{1,0:T(8,128)(2,1)} %collective-permute-done.5.refs_3_), channel_id=1, source_target_pairs={{0,4},{4,0},{8,12},{12,8},{16,20},{20,16},{24,28},{28,24},{1,5},{5... | collective-permute-start | bytes 3145736 | tf_op jit(solution)/shard_map/ppermute | solution.py:553
  180.6 13.9 %copy-start.26 = (s32[4]{0:T(128)}, s32[4]{0:T(128)S(1)}, u32[]{:S(2)}) copy-start(s32[4]{0:T(128)S(1)} %get-tuple-element.194.tiles_ref) | copy-start | bytes 52
  223.6 93.3 %all-gather.14.cloned.1.call-start = ((), (), s32[]{:S(2)}) async-start(), calls=%async_computation.10 | async-start | bytes 2621440 | tf_op jit(solution)/shard_map/all_gather | solution.py:661
  270.3 91.4 %reduce-scatter.5.cloned.1.call-start = ((), (), s32[]{:S(2)}) async-start(), calls=%async_computation.11 | async-start | bytes 2621440 | tf_op jit(solution)/shard_map/reduce_scatter | solution.py:559
  304.8 102.5 %reduce-scatter.7.cloned.1.call-start = ((), (), s32[]{:S(2)}) async-start(), calls=%async_computation.12 | async-start | bytes 2621440 | tf_op jit(solution)/shard_map/reduce_scatter | solution.py:559
  361.7 142.4 %reduce-scatter.9.cloned.1.call-start = ((), (), s32[]{:S(2)}) async-start(), calls=%async_computation.13 | async-start | bytes 5242880 | tf_op jit(solution)/shard_map/reduce_scatter | solution.py:559
  410.9 16.0 %collective-permute-start.10 = (bf16[4,256,4096]{2,1,0:T(8,128)(2,1)}, bf16[4,256,4096]{2,1,0:T(8,128)(2,1)}, u32[]{:S(2)}, u32[]{:S(2)}) collective-permute-start(bf16[4,256,4096]{2,1,0:T(8,128)(2,1)} %weight_grad.8), channel_id=1, source_target_pairs={{0,4},{4,0},{8,12},{12,8},{16,20},{20,16},{24,28},{28,24},{1,5},{5... | collective-permute-start | bytes 25165832 | tf_op jit(solution)/shard_map/ppermute | solution.py:570
  410.9 35.7 %collective-permute-start.11 = (bf16[4,256,2048]{2,1,0:T(8,128)(2,1)}, bf16[4,256,2048]{2,1,0:T(8,128)(2,1)}, u32[]{:S(2)}, u32[]{:S(2)}) collective-permute-start(bf16[4,256,2048]{2,1,0:T(8,128)(2,1)} %weight_grad.9), channel_id=1, source_target_pairs={{0,4},{4,0},{8,12},{12,8},{16,20},{20,16},{24,28},{28,24},{1,5},{5... | collective-permute-start | bytes 12582920 | tf_op jit(solution)/shard_map/ppermute | solution.py:570
  418.6 58.3 %all-to-all-start.1 = ((bf16[4,256,512]{2,1,0:T(8,128)(2,1)}), bf16[4,256,512]{2,1,0:T(8,128)(2,1)}, u32[]{:S(2)}, u32[]{:S(2)}) async-start(bf16[4,256,512]{2,1,0:T(8,128)(2,1)} %out_project_back.1), calls=%async_computation.4 | async-start | bytes 2097152 | tf_op jit(solution)/shard_map/all_to_all | solution.py:645
  422.9 170.2 %reduce-scatter.11.cloned.1.call-start = ((), (), s32[]{:S(2)}) async-start(), calls=%async_computation.14 | async-start | bytes 5242880 | tf_op jit(solution)/shard_map/reduce_scatter | solution.py:559
  445.2 71.3 %collective-permute-start.12 = (bf16[2,256,4096]{2,1,0:T(8,128)(2,1)}, bf16[2,256,4096]{2,1,0:T(8,128)(2,1)}, u32[]{:S(2)}, u32[]{:S(2)}) collective-permute-start(bf16[2,256,4096]{2,1,0:T(8,128)(2,1)} %get-tuple-element.103), channel_id=1, source_target_pairs={{0,8},{4,20},{8,0},{12,28},{16,24},{20,4},{24,16},{28,12},{1,9},{5... | collective-permute-start | bytes 12582920 | tf_op jit(solution)/shard_map/ppermute | solution.py:581
  457.7 58.8 %collective-permute-start.13 = (bf16[2,256,2048]{2,1,0:T(8,128)(2,1)}, bf16[2,256,2048]{2,1,0:T(8,128)(2,1)}, u32[]{:S(2)}, u32[]{:S(2)}) collective-permute-start(bf16[2,256,2048]{2,1,0:T(8,128)(2,1)} %get-tuple-element.106), channel_id=1, source_target_pairs={{0,8},{4,20},{8,0},{12,28},{16,24},{20,4},{24,16},{28,12},{1,9},{5... | collective-permute-start | bytes 6291464 | tf_op jit(solution)/shard_map/ppermute | solution.py:581
  522.3 19.6 %collective-permute-start.14 = (bf16[4,256,2048]{2,1,0:T(8,128)(2,1)}, bf16[4,256,2048]{2,1,0:T(8,128)(2,1)}, u32[]{:S(2)}, u32[]{:S(2)}) collective-permute-start(bf16[4,256,2048]{2,1,0:T(8,128)(2,1)} %weight_grad.12), channel_id=1, source_target_pairs={{0,4},{4,0},{8,12},{12,8},{16,20},{20,16},{24,28},{28,24},{1,5},{5... | collective-permute-start | bytes 12582920 | tf_op jit(solution)/shard_map/ppermute | solution.py:570
  529.3 19.8 %collective-permute-start.15 = (bf16[4,256,768]{2,1,0:T(8,128)(2,1)}, bf16[4,256,768]{2,1,0:T(8,128)(2,1)}, u32[]{:S(2)}, u32[]{:S(2)}) collective-permute-start(bf16[4,256,768]{2,1,0:T(8,128)(2,1)} %weight_grad.13), channel_id=1, source_target_pairs={{0,4},{4,0},{8,12},{12,8},{16,20},{20,16},{24,28},{28,24},{1,5},{5... | collective-permute-start | bytes 4718600 | tf_op jit(solution)/shard_map/ppermute | solution.py:570
  535.3 28.9 %collective-permute-start.29 = (bf16[1,256,4096]{2,1,0:T(8,128)(2,1)}, bf16[1,256,4096]{2,1,0:T(8,128)(2,1)}, u32[]{:S(2)}, u32[]{:S(2)}) collective-permute-start(bf16[1,256,4096]{2,1,0:T(8,128)(2,1)} %get-tuple-element.163), channel_id=1, source_target_pairs={{0,16},{4,12},{8,24},{12,4},{16,0},{20,28},{24,8},{28,20},{1,17},{... | collective-permute-start | bytes 6291464 | tf_op jit(solution)/shard_map/ppermute | solution.py:581
  541.5 38.7 %collective-permute-start.30 = (bf16[1,256,2048]{2,1,0:T(8,128)(2,1)}, bf16[1,256,2048]{2,1,0:T(8,128)(2,1)}, u32[]{:S(2)}, u32[]{:S(2)}) collective-permute-start(bf16[1,256,2048]{2,1,0:T(8,128)(2,1)} %get-tuple-element.165), channel_id=1, source_target_pairs={{0,16},{4,12},{8,24},{12,4},{16,0},{20,28},{24,8},{28,20},{1,17},{... | collective-permute-start | bytes 3145736 | tf_op jit(solution)/shard_map/ppermute | solution.py:581
  560.7 26.9 %collective-permute-start.18 = (f32[2,2048]{1,0:T(2,128)S(1)}, f32[2,2048]{1,0:T(2,128)S(1)}, u32[]{:S(2)}, u32[]{:S(2)}) collective-permute-start(f32[2,2048]{1,0:T(2,128)S(1)} %pad_maximum_fusion.6), channel_id=1, source_target_pairs={{0,8},{4,12},{8,0},{12,4},{16,24},{20,28},{24,16},{28,20},{1,9},{5... | collective-permute-start | bytes 49160 | tf_op jit(solution)/shard_map/ppermute | solution.py:595
  562.4 25.2 %collective-permute-start.17 = (f32[2,2048]{1,0:T(2,128)S(1)}, f32[2,2048]{1,0:T(2,128)S(1)}, u32[]{:S(2)}, u32[]{:S(2)}) collective-permute-start(f32[2,2048]{1,0:T(2,128)S(1)} %pad_maximum_fusion.6), channel_id=1, source_target_pairs={{0,16},{4,20},{8,24},{12,28},{16,0},{20,4},{24,8},{28,12},{1,17},{... | collective-permute-start | bytes 49160 | tf_op jit(solution)/shard_map/ppermute | solution.py:595
  563.8 23.9 %collective-permute-start.16 = (f32[2,2048]{1,0:T(2,128)S(1)}, f32[2,2048]{1,0:T(2,128)S(1)}, u32[]{:S(2)}, u32[]{:S(2)}) collective-permute-start(f32[2,2048]{1,0:T(2,128)S(1)} %pad_maximum_fusion.6), channel_id=1, source_target_pairs={{0,24},{4,28},{8,16},{12,20},{16,8},{20,12},{24,0},{28,4},{1,25},{... | collective-permute-start | bytes 49160 | tf_op jit(solution)/shard_map/ppermute | solution.py:595
  564.3 37.6 %collective-permute-start.24 = (bf16[2,256,2048]{2,1,0:T(8,128)(2,1)}, bf16[2,256,2048]{2,1,0:T(8,128)(2,1)}, u32[]{:S(2)}, u32[]{:S(2)}) collective-permute-start(bf16[2,256,2048]{2,1,0:T(8,128)(2,1)} %get-tuple-element.113), channel_id=1, source_target_pairs={{0,8},{4,20},{8,0},{12,28},{16,24},{20,4},{24,16},{28,12},{1,9},{5... | collective-permute-start | bytes 6291464 | tf_op jit(solution)/shard_map/ppermute | solution.py:581
  580.1 29.7 %collective-permute-start.22 = (bf16[2,256,768]{2,1,0:T(8,128)(2,1)}, bf16[2,256,768]{2,1,0:T(8,128)(2,1)}, u32[]{:S(2)}, u32[]{:S(2)}) collective-permute-start(bf16[2,256,768]{2,1,0:T(8,128)(2,1)} %get-tuple-element.115), channel_id=1, source_target_pairs={{0,8},{4,20},{8,0},{12,28},{16,24},{20,4},{24,16},{28,12},{1,9},{5... | collective-permute-start | bytes 2359304 | tf_op jit(solution)/shard_map/ppermute | solution.py:581
  587.7 7.3 %collective-permute-start.19 = (f32[2,2048]{1,0:T(2,128)S(1)}, f32[2,2048]{1,0:T(2,128)S(1)}, u32[]{:S(2)}, u32[]{:S(2)}) collective-permute-start(f32[2,2048]{1,0:T(2,128)S(1)} %select_add_fusion), channel_id=1, source_target_pairs={{0,4},{4,0},{8,12},{12,8},{16,20},{20,16},{24,28},{28,24},{1,5},{5... | collective-permute-start | bytes 49160 | tf_op jit(solution)/shard_map/ppermute | solution.py:601
  595.0 3.8 collective-permute-start.20
  598.8 10.4 %collective-permute-start.21 = (f32[2,2048]{1,0:T(2,128)S(1)}, f32[2,2048]{1,0:T(2,128)S(1)}, u32[]{:S(2)}, u32[]{:S(2)}) collective-permute-start(f32[2,2048]{1,0:T(2,128)S(1)} %add.113), channel_id=1, source_target_pairs={{0,2},{1,3},{2,0},{3,1},{4,6},{5,7},{6,4},{7,5},{8,10},{9,11},{10,... | collective-permute-start | bytes 49160 | tf_op jit(solution)/shard_map/ppermute | solution.py:603
  604.5 14.9 %collective-permute-start.25 = (bf16[1,256,2048]{2,1,0:T(8,128)(2,1)S(1)}, bf16[1,256,2048]{2,1,0:T(8,128)(2,1)S(1)}, u32[]{:S(2)}, u32[]{:S(2)}) collective-permute-start(bf16[1,256,2048]{2,1,0:T(8,128)(2,1)S(1)} %slice.148), channel_id=1, source_target_pairs={{0,16},{4,12},{8,24},{12,4},{16,0},{20,28},{24,8},{28,20},{1,17},{... | collective-permute-start | bytes 3145736 | tf_op jit(solution)/shard_map/ppermute | solution.py:581
  611.2 13.1 %collective-permute-start.23 = (bf16[1,256,768]{2,1,0:T(8,128)(2,1)S(1)}, bf16[1,256,768]{2,1,0:T(8,128)(2,1)S(1)}, u32[]{:S(2)}, u32[]{:S(2)}) collective-permute-start(bf16[1,256,768]{2,1,0:T(8,128)(2,1)S(1)} %slice.143), channel_id=1, source_target_pairs={{0,16},{4,12},{8,24},{12,4},{16,0},{20,28},{24,8},{28,20},{1,17},{... | collective-permute-start | bytes 1179656 | tf_op jit(solution)/shard_map/ppermute | solution.py:581
  619.9 11.1 %collective-permute-start.28 = (bf16[256,512]{1,0:T(8,128)(2,1)S(1)}, bf16[256,512]{1,0:T(8,128)(2,1)S(1)}, u32[]{:S(2)}, u32[]{:S(2)}) collective-permute-start(bf16[256,512]{1,0:T(8,128)(2,1)S(1)} %get-tuple-element.167), channel_id=1, source_target_pairs={{0,3},{1,2},{2,1},{3,0},{4,7},{5,6},{6,5},{7,4},{8,11},{9,10},{10,... | collective-permute-start | bytes 786440 | tf_op jit(solution)/shard_map/ppermute | solution.py:510
  620.9 23.8 %collective-permute-start.27 = (bf16[256,512]{1,0:T(8,128)(2,1)S(1)}, bf16[256,512]{1,0:T(8,128)(2,1)S(1)}, u32[]{:S(2)}, u32[]{:S(2)}) collective-permute-start(bf16[256,512]{1,0:T(8,128)(2,1)S(1)} %get-tuple-element.168), channel_id=1, source_target_pairs={{0,2},{1,3},{2,0},{3,1},{4,6},{5,7},{6,4},{7,5},{8,10},{9,11},{10,... | collective-permute-start | bytes 786440 | tf_op jit(solution)/shard_map/ppermute | solution.py:510
  622.1 22.6 %collective-permute-start.26 = (bf16[256,512]{1,0:T(8,128)(2,1)S(1)}, bf16[256,512]{1,0:T(8,128)(2,1)S(1)}, u32[]{:S(2)}, u32[]{:S(2)}) collective-permute-start(bf16[256,512]{1,0:T(8,128)(2,1)S(1)} %get-tuple-element.166), channel_id=1, source_target_pairs={{0,1},{1,0},{2,3},{3,2},{4,5},{5,4},{6,7},{7,6},{8,9},{9,8},{10,11... | collective-permute-start | bytes 786440 | tf_op jit(solution)/shard_map/ppermute | solution.py:510
  (23 other events, 128.8 us)
Sparse Core Ops, SparseCore 0:
  12.0 96.4 all-gather.5
  111.1 65.4 all-gather.7
  179.0 44.5 all-gather.9
  225.6 44.6 all-gather.11
  272.3 44.6 all-gather.13
  319.1 42.5 reduce-scatter.4
  364.1 43.1 reduce-scatter.6
  411.1 92.9 reduce-scatter.8
  511.6 81.4 reduce-scatter.10
